TPU v7x, 128 devices: a whole 4x4x4 slice. The times are simulated.
128 devices in a mesh: ctx: 16 (over x, y_lo, core), depth: 8 (over y_hi, z).
Axes of the slice: x: 4, y: 4 (y_hi: 2, y_lo: 2; y = y_hi * 2 + y_lo), z: 4, core: 2. Of those that a mesh axis runs over, the one named last changes fastest.
Arguments:
- q_heads: bfloat16 [8192, 2048], P('ctx', 'depth'), may hold values from -200 to 200
- k_heads: bfloat16 [8192, 2048], P('ctx', 'depth'), may hold values from -200 to 200
- v_heads: bfloat16 [8192, 2048], P('ctx', 'depth'), may hold values from -6 to 6
- block_of: int32 [32], replicated, may hold values from 0 to 31, each once
- resid: bfloat16 [8192, 4096], P(('ctx', 'depth')), may hold values from -6 to 6
- w_out_t: bfloat16 [2048, 4096], P('depth'), may hold values from -0.125 to 0.125
- norm_gain: float32 [4096], replicated, may hold values from 0.5 to 1.5
- w_in: bfloat16 [4096, 1024], P('depth'), may hold values from -0.09375 to 0.09375
- embed: bfloat16 [2048, 1024], replicated, may hold values from -6 to 6
- w_qkv: bfloat16 [1024, 3072], replicated, may hold values from -0.1875 to 0.1875
- w_o: bfloat16 [1024, 1024], replicated, may hold values from -0.1875 to 0.1875
- w_head: bfloat16 [1024, 2048], replicated, may hold values from -0.5 to 0.5
- codes: int32 [8192, 8], P(('ctx', 'depth')), may hold values from 0 to 2047
Outputs:
- d_attn: bfloat16 [8192, 2048], P('ctx', 'depth')
- d_wqkv: float32 [1024, 3072], P(('ctx', 'depth'))
All inputs are finite; a program needn't handle non-finite values.
Results may differ from a plain program's by a relative error of at most 0.034.
Values may be sent and summed in bfloat16 or wider, within the bound.
A program may use at most 192 MiB of HBM per device.

v0:
```python
import math

import jax
import jax.numpy as jnp
from jax import lax
from jax.sharding import PartitionSpec as P

D = 4096
HS = 128
DHS = 64


eps = 1e-05


def positions_of(index, block_of, half):
    which = index // half
    slots = jnp.arange(block_of.shape[0], dtype=jnp.int32)
    picked = jnp.sum(jnp.where(which[:, None] == slots[None, :], block_of[None, :], 0), axis=1)
    return picked * half + index % half


def rms_rows(values):
    return values * lax.rsqrt(jnp.mean(values * values, axis=-1, keepdims=True) + eps)


def depth_front(units, codes, embed):
    frames, steps = codes.shape
    width = embed.shape[1]
    earlier = jnp.take(embed, codes[:, : steps - 1], axis=0).astype(jnp.float32)
    lead = jnp.zeros((frames, 1, width), jnp.float32)
    stream = units.astype(jnp.float32)[:, None, :] + jnp.concatenate([lead, earlier], axis=1)
    normed = rms_rows(stream).astype(jnp.bfloat16).reshape(frames * steps, width)
    return (normed, stream)


def depth_back(packed, stream, codes, w_o, w_head, head_size):
    frames, steps, width = stream.shape
    heads = width // head_size
    parts = packed.reshape(frames, steps, 3, heads, head_size).astype(jnp.float32)
    scores = jnp.einsum("fqhd,fkhd->fhqk", parts[:, :, 0], parts[:, :, 1]) * (
        1.0 / math.sqrt(head_size)
    )
    causal = jnp.arange(steps)[:, None] >= jnp.arange(steps)[None, :]
    weights = jnp.where(causal, jnp.exp(scores), 0.0)
    weights = weights / jnp.sum(weights, axis=-1, keepdims=True)
    mixed = (
        jnp.einsum("fhqk,fkhd->fqhd", weights, parts[:, :, 2])
        .astype(jnp.bfloat16)
        .reshape(frames * steps, width)
    )
    after = stream.reshape(frames * steps, width) + jnp.dot(
        mixed, w_o, preferred_element_type=jnp.float32
    )
    normed = rms_rows(after).astype(jnp.bfloat16)
    logits = jnp.dot(normed, w_head, preferred_element_type=jnp.float32)
    total = jnp.log(jnp.sum(jnp.exp(logits), axis=-1))
    vocab = jnp.arange(w_head.shape[1], dtype=jnp.int32)
    picked = jnp.sum(jnp.where(codes.reshape(-1)[:, None] == vocab[None, :], logits, 0.0), axis=-1)
    return jnp.sum(total - picked)


def depth_block(units, codes, embed, w_qkv, w_o, w_head, head_size):
    (normed, stream), pull_front = jax.vjp(lambda u: depth_front(u, codes, embed), units)
    packed = jnp.dot(normed, w_qkv, preferred_element_type=jnp.float32).astype(jnp.bfloat16)
    loss, pull = jax.vjp(
        lambda a, b: depth_back(a, b, codes, w_o, w_head, head_size), packed, stream
    )
    d_packed, d_stream = pull(jnp.ones_like(loss))
    d_normed = jnp.einsum("tc,wc->tw", d_packed, w_qkv, preferred_element_type=jnp.float32).astype(
        jnp.bfloat16
    )
    (d_units,) = pull_front((d_normed, d_stream))
    d_weight = jnp.einsum("tw,tc->wc", normed, d_packed, preferred_element_type=jnp.float32)
    return (d_units, d_weight)


def body(
    q_heads,
    k_heads,
    v_heads,
    block_of,
    resid,
    w_out_t,
    norm_gain,
    w_in,
    embed,
    w_qkv,
    w_o,
    w_head,
    codes,
):
    rows, width = q_heads.shape
    heads = width // HS
    half = rows // 2
    owners = lax.axis_size("depth")
    owned = rows // owners
    mine = lax.axis_index("depth")
    index = lax.axis_index("ctx") * rows + jnp.arange(rows, dtype=jnp.int32)
    pos_q = positions_of(index, block_of, half)
    queries = q_heads.reshape(rows, heads, HS)
    scale = 1.0 / math.sqrt(HS)
    start_state = (
        jnp.full((rows, heads), -1e30, jnp.float32),
        jnp.zeros((rows, heads), jnp.float32),
        jnp.zeros((rows, heads, HS), jnp.float32),
    )
    keys = lax.all_gather(k_heads, "ctx", axis=0, tiled=True)
    values = lax.all_gather(v_heads, "ctx", axis=0, tiled=True)
    count = keys.shape[0]
    pos_k = positions_of(jnp.arange(count, dtype=jnp.int32), block_of, half)
    visible = pos_q[:, None] >= pos_k[None, :]

    def compute(state):
        top, total, acc = state
        scores = (
            jnp.einsum(
                "qhd,khd->qhk",
                queries,
                keys.reshape(count, heads, HS),
                preferred_element_type=jnp.float32,
            )
            * scale
        )
        scores = jnp.where(visible[:, None, :], scores, -1e30)
        new_top = jnp.maximum(top, jnp.max(scores, axis=-1))
        weights = jnp.where(visible[:, None, :], jnp.exp(scores - new_top[:, :, None]), 0.0)
        total = jnp.sum(weights, axis=-1)
        acc = jnp.einsum(
            "qhk,khd->qhd",
            weights.astype(jnp.bfloat16),
            values.reshape(count, heads, HS),
            preferred_element_type=jnp.float32,
        )
        return (new_top, total, acc)

    top, total, acc = lax.cond(jnp.any(visible), compute, lambda state: state, start_state)
    attn = (acc / total[:, :, None]).astype(jnp.bfloat16).reshape(rows, width)
    partial_value = jnp.dot(attn, w_out_t, preferred_element_type=jnp.float32)
    offset = mine * owned
    own_rows = lax.dynamic_slice_in_dim(partial_value, offset, owned, 0) + resid.astype(jnp.float32)
    partial_value = lax.dynamic_update_slice_in_dim(partial_value, own_rows, offset, 0)
    hidden = lax.psum_scatter(
        partial_value.astype(jnp.bfloat16), "depth", scatter_dimension=0, tiled=True
    ).astype(jnp.float32)
    full_in = lax.all_gather(w_in, "depth", axis=0, tiled=True)
    rscale = lax.rsqrt(jnp.mean(hidden * hidden, axis=-1, keepdims=True) + eps)
    normed = (hidden * rscale * norm_gain).astype(jnp.bfloat16)
    units = jnp.dot(normed, full_in, preferred_element_type=jnp.float32).astype(jnp.bfloat16)
    d_units, d_weight = depth_block(units, codes, embed, w_qkv, w_o, w_head, DHS)
    d_normed = jnp.einsum("fk,dk->fd", d_units, full_in, preferred_element_type=jnp.float32).astype(
        jnp.bfloat16
    )
    grad_gain = d_normed.astype(jnp.float32) * norm_gain
    dot_rows = jnp.sum(grad_gain * hidden, axis=-1, keepdims=True)
    d_hidden = (rscale * grad_gain - hidden * rscale * rscale * rscale * dot_rows / D).astype(
        jnp.bfloat16
    )
    d_full = lax.all_gather(d_hidden, "depth", axis=0, tiled=True)
    d_attn = jnp.einsum("rd,cd->rc", d_full, w_out_t, preferred_element_type=jnp.float32).astype(
        jnp.bfloat16
    )
    d_wqkv = lax.psum_scatter(d_weight, ("ctx", "depth"), scatter_dimension=0, tiled=True)
    return (d_attn, d_wqkv)


def solution(mesh):
    in_specs = (
        P("ctx", "depth"),
        P("ctx", "depth"),
        P("ctx", "depth"),
        P(),
        P(("ctx", "depth"), None),
        P("depth", None),
        P(),
        P("depth", None),
        P(),
        P(),
        P(),
        P(),
        P(("ctx", "depth"), None),
    )
    out_specs = (P("ctx", "depth"), P(("ctx", "depth"), None))
    return jax.shard_map(body, mesh=mesh, in_specs=in_specs, out_specs=out_specs, check_vma=False)
```

profile of v0, /device:TPU:0, one launch (start us, length us, event | category | flops | bytes accessed | tf_op | source)
XLA Modules:
  0.0 1194.1 jit_solution(7152007948061875274)
XLA Ops:
  8.8 0.7 select_reduce_fusion.1
  9.5 0.9 select_reduce_fusion
  10.4 6.6 broadcast_compare_fusion
  17.7 31.9 %all-gather.5.cloned.1.call-done = bf16[8192,256]{1,0:T(8,128)(2,1)} async-done(((bf16[512,256]{1,0:T(8,128)(2,1)}), bf16[8192,256]{1,0:T(8,128)(2,1)}) %all-gather.5.cloned.1.call-update) | async-done | bytes 4194320 | tf_op jit(solution)/shard_map/all_gather | solution.py:108
  49.5 39.1 %all-gather.7.cloned.1.call-done = bf16[8192,256]{1,0:T(8,128)(2,1)} async-done(((bf16[512,256]{1,0:T(8,128)(2,1)}), bf16[8192,256]{1,0:T(8,128)(2,1)}) %all-gather.7.cloned.1.call-update) | async-done | bytes 4194320 | tf_op jit(solution)/shard_map/all_gather | solution.py:109
  88.7 50.2 %conditional.1 = (f32[512,2]{0,1:T(2,128)S(1)}, f32[512,2,128]{0,2,1:T(8,128)S(1)}) conditional(s32[]{:T(128)} %convert_element_type.81, () %tuple.18, (pred[512,8192]{0,1:T(8,128)(4,1)}, bf16[8192,256]{1,0:T(8,128)(2,1)}, bf16[512,256]{1,0:T(8,128)(2,1)S(1)}, bf16[8192,256]{1,0:T(8,128)(2,1)}) %tuple.48), branch_computations={%region_3.4_spmd, %region_4.7_spmd} | conditional | flops 4404018176 | bytes 140271664 | solution.py:137
  88.7 16.3 %fusion = (f32[512,2]{0,1:T(2,128)S(1)}, f32[2,8192,512]{2,1,0:T(8,128)}) fusion(pred[512,8192]{0,1:T(8,128)(4,1)} %get-tuple-element.9, bf16[8192,256]{1,0:T(8,128)(2,1)} %get-tuple-element.10, bf16[512,256]{1,0:T(8,128)(2,1)S(1)} %get-tuple-element.20), kind=kOutput, calls=%fused_computation.3 | convolution fusion | flops 2172648448 | bytes 42209280 | tf_op jit(solution)/shard_map/cond/branch_1_fun/qhd,khd->qhk/dot_general | solution.py:117
  105.0 15.9 %fusion.2 = f32[512,2]{0,1:T(2,128)S(1)} fusion(f32[2,8192,512]{2,1,0:T(8,128)} %get-tuple-element.23, f32[512,2]{0,1:T(2,128)S(1)} %broadcast_maximum_fusion, pred[512,8192]{0,1:T(8,128)(4,1)} %get-tuple-element.9), kind=kLoop, calls=%fused_computation.5 | loop fusion | flops 41942016 | bytes 37756928 | tf_op jit(solution)/shard_map/cond/branch_1_fun/reduce_sum | solution.py:128
  120.9 17.7 %fusion.11 = f32[512,2,128]{2,0,1:T(8,128)S(1)} fusion(f32[2,8192,512]{2,1,0:T(8,128)} %get-tuple-element.23, f32[512,2]{0,1:T(2,128)S(1)} %broadcast_maximum_fusion, pred[512,8192]{0,1:T(8,128)(4,1)S(1)} %copy-done.1, bf16[8192,256]{1,0:T(8,128)(2,1)} %get-tuple-element.12), kind=kOutput, calls=%fused_computation.13 | convolution fusion | flops 2189426688 | bytes 42471424 | tf_op jit(solution)/shard_map/cond/branch_1_fun/qhk,khd->qhd/dot_general | solution.py:129
  139.0 1.3 fusion.100
  140.5 2.6 convert_element_type.84
  144.1 5.7 gather_fusion
  149.8 1.3 reshape.183
  151.4 1.4 broadcast_select_fusion
  152.8 75.3 %reduce-scatter.3.cloned.1.call-done = bf16[64,4096]{1,0:T(8,128)(2,1)} async-done(((bf16[512,4096]{1,0:T(8,128)(2,1)}), bf16[64,4096]{1,0:T(8,128)(2,1)}) %reduce-scatter.3.cloned.1.call-update) | async-done | bytes 524304 | tf_op jit(solution)/shard_map/reduce_scatter | solution.py:143
  228.1 1.2 fusion.58
  229.3 107.2 %all-gather.9.cloned.1.call-done = bf16[4096,1024]{1,0:T(8,128)(2,1)} async-done(((bf16[512,1024]{1,0:T(8,128)(2,1)}), bf16[4096,1024]{1,0:T(8,128)(2,1)}) %all-gather.9.cloned.1.call-update) | async-done | bytes 8388624 | tf_op jit(solution)/shard_map/all_gather | solution.py:146
  336.5 5.2 fusion.51
  342.4 7.7 convolution_convert_fusion.1
  350.2 8.6 reshape.176
  358.8 5.6 fusion.99
  364.4 2.2 fusion.30
  366.6 1.0 multiply_divide_fusion
  367.6 1.8 convert_bitcast_fusion
  369.4 1.9 copy.109
  371.4 4.3 reshape.177
  375.7 3.5 multiply_reduce_fusion.1
  379.3 2.5 exponential_reduce_fusion
  381.8 2.6 fusion.31
  384.5 1.0 copy-done.12
  385.5 2.4 convolution_convert_fusion.2
  387.9 4.0 reshape.179
  391.9 6.1 multiply_reduce_fusion
  398.0 0.8 copy-done.16
  398.9 3.9 convolution_bitcast_fusion
  402.8 5.5 convolution_bitcast_fusion.1
  408.4 3.4 convolution_bitcast_fusion.2
  411.8 9.1 add_convert_fusion
  420.9 7.3 copy.112
  428.1 8.7 reshape.180
  436.9 8.3 fusion.33
  445.3 3.6 fusion.34
  448.9 6.2 fusion.59
  455.1 1.2 fusion.57
  456.3 10.5 fusion.67
  466.9 58.9 %all-gather.11.cloned.1.call-done = bf16[512,4096]{1,0:T(8,128)(2,1)} async-done(((bf16[64,4096]{1,0:T(8,128)(2,1)}), bf16[512,4096]{1,0:T(8,128)(2,1)}) %all-gather.11.cloned.1.call-update) | async-done | bytes 4194320 | tf_op jit(solution)/shard_map/all_gather | solution.py:159
  525.7 4.2 convolution_convert_fusion.4
  529.9 657.2 %reduce-scatter.5.cloned.1.call-done = f32[8,3072]{1,0:T(8,128)} async-done(((f32[1024,3072]{1,0:T(8,128)}), f32[8,3072]{1,0:T(8,128)}) %reduce-scatter.5.cloned.1.call-update) | async-done | bytes 98320 | tf_op jit(solution)/shard_map/reduce_scatter | solution.py:163
  (85 shorter events, 4.3 us)
Async XLA Ops:
  7.2 131.8 %copy-start = (bf16[256,4096]{1,0:T(8,128)(2,1)S(1)}, bf16[256,4096]{1,0:T(8,128)(2,1)}, u32[]{:S(2)}) copy-start(bf16[256,4096]{1,0:T(8,128)(2,1)} %param.20) | copy-start | bytes 6291460
  7.2 81.5 %copy-start.22 = (bf16[512,256]{1,0:T(8,128)(2,1)S(1)}, bf16[512,256]{1,0:T(8,128)(2,1)}, u32[]{:S(2)}) copy-start(bf16[512,256]{1,0:T(8,128)(2,1)} %param.15) | copy-start | bytes 786436
  7.2 42.4 %all-gather.5.cloned.1.call-start = ((), (), s32[]{:S(2)}) async-start(), calls=%async_computation.2 | async-start | bytes 4456448 | tf_op jit(solution)/shard_map/all_gather | solution.py:108
  7.9 80.8 %all-gather.7.cloned.1.call-start = ((), (), s32[]{:S(2)}) async-start(), calls=%async_computation.3 | async-start | bytes 4456448 | tf_op jit(solution)/shard_map/all_gather | solution.py:109
  8.7 219.4 %reduce-scatter.3.cloned.1.call-start = ((), (), s32[]{:S(2)}) async-start(), calls=%async_computation.4 | async-start | bytes 4718592 | tf_op jit(solution)/shard_map/reduce_scatter | solution.py:143
  105.0 15.9 %copy-start.1 = (pred[512,8192]{0,1:T(8,128)(4,1)S(1)}, pred[512,8192]{0,1:T(8,128)(4,1)}, u32[]{:S(2)}) copy-start(pred[512,8192]{0,1:T(8,128)(4,1)} %get-tuple-element.9) | copy-start | bytes 12582916 | tf_op jit(solution)/shard_map/cond
  139.0 1.3 copy-start.17
  143.1 0.7 copy-start.19
  143.1 193.4 %all-gather.9.cloned.1.call-start = ((), (), s32[]{:S(2)}) async-start(), calls=%async_computation.5 | async-start | bytes 9437184 | tf_op jit(solution)/shard_map/all_gather | solution.py:146
  143.7 382.1 %all-gather.11.cloned.1.call-start = ((), (), s32[]{:S(2)}) async-start(), calls=%async_computation.6 | async-start | bytes 4718592 | tf_op jit(solution)/shard_map/all_gather | solution.py:159
  149.8 186.7 %copy-start.18 = (f32[4096]{0:T(1024)S(1)}, f32[4096]{0:T(1024)}, u32[]{:S(2)}) copy-start(f32[4096]{0:T(1024)} %param.21) | copy-start | bytes 49156
  152.8 284.1 %copy-start.3 = (bf16[64,7,1024]{2,1,0:T(8,128)(2,1)}, bf16[64,7,1024]{2,1,0:T(8,128)(2,1)S(1)}, u32[]{:S(2)}) copy-start(bf16[64,7,1024]{2,1,0:T(8,128)(2,1)S(1)} %broadcast_select_fusion) | copy-start | bytes 2752516
  364.3 2.2 copy-start.9
  364.3 2.2 copy-start.10
  364.3 3.2 copy-start.5
  366.6 2.9 copy-start.6
  366.6 2.9 copy-start.13
  375.7 3.6 copy-start.20
  379.2 5.3 copy-start.8
  381.8 3.6 copy-start.21
  384.5 1.0 copy-start.12
  391.9 7.0 copy-start.7
  391.9 7.0 copy-start.11
  391.9 7.0 copy-start.14
  398.0 0.9 copy-start.16
  398.9 3.9 copy-start.15
  402.8 5.6 copy-start.4
  445.2 3.7 copy-start.2
  456.3 730.8 %reduce-scatter.5.cloned.1.call-start = ((), (), s32[]{:S(2)}) async-start(), calls=%async_computation.7 | async-start | bytes 12681216 | tf_op jit(solution)/shard_map/reduce_scatter | solution.py:163
Sparse Core Ops, SparseCore 0:
  9.7 39.7 all-gather.4
  51.2 37.3 all-gather.6
  143.2 84.8 reduce-scatter.2
  230.6 105.9 all-gather.8
  456.4 69.2 all-gather.10
  528.7 658.3 reduce-scatter.4
where the time goes:
time: 1200 us; the launch traced here: 1190 us
  waiting for transfers between devices  971 us (81%)
  matrix products  111 us (9%)
  local copies, waits for them, and re-layouts  50.4 us (4%)
  other arithmetic  45.2 us (4%)
  between operations  15.4 us (1%)
    reduce_scatter x1, waiting for transfers between devices, body(): lax.psum_scatter(d_weight, ('ctx', 'depth'), scatter_dimension=0, tiled=T...  657 us
    all_gather x1, waiting for transfers between devices, body(): full_in = lax.all_gather(w_in, 'depth', axis=0, tiled=True)  107 us
    reduce_scatter x1, waiting for transfers between devices, body(): lax.psum_scatter(partial_value.astype(jnp.bfloat16), 'depth', scatter_dim...  75.3 us
    all_gather x1, waiting for transfers between devices, body(): d_full = lax.all_gather(d_hidden, 'depth', axis=0, tiled=True)  58.9 us
    all_gather x1, waiting for transfers between devices, body(): values = lax.all_gather(v_heads, 'ctx', axis=0, tiled=True)  39.1 us
    all_gather x1, waiting for transfers between devices, body(): keys = lax.all_gather(k_heads, 'ctx', axis=0, tiled=True)  31.9 us
  transfers between devices with their start and end apart: 6, of which 6 were waited for; matrix products, arithmetic and copies ran while one was open for 3% of the time, Pallas kernels for 0%

commit v1 on v0

--- a/solution.py
+++ b/solution.py
@@ -3,6 +3,8 @@
 import jax
 import jax.numpy as jnp
 from jax import lax
+from jax.experimental import pallas as pl
+from jax.experimental.pallas import tpu as pltpu
 from jax.sharding import PartitionSpec as P
 
 D = 4096
@@ -11,6 +13,7 @@
 
 
 eps = 1e-05
+MESH = pl.DeviceIdType.MESH
 
 
 def positions_of(index, block_of, half):
@@ -61,18 +64,343 @@
 
 
 def depth_block(units, codes, embed, w_qkv, w_o, w_head, head_size):
-    (normed, stream), pull_front = jax.vjp(lambda u: depth_front(u, codes, embed), units)
+    normed, stream = depth_front(units, codes, embed)
     packed = jnp.dot(normed, w_qkv, preferred_element_type=jnp.float32).astype(jnp.bfloat16)
     loss, pull = jax.vjp(
         lambda a, b: depth_back(a, b, codes, w_o, w_head, head_size), packed, stream
     )
     d_packed, d_stream = pull(jnp.ones_like(loss))
-    d_normed = jnp.einsum("tc,wc->tw", d_packed, w_qkv, preferred_element_type=jnp.float32).astype(
+    return normed, d_packed, stream.reshape(normed.shape), d_stream.reshape(normed.shape)
+
+
+def place():
+    ctx = lax.axis_index("ctx")
+    depth = lax.axis_index("depth")
+    x = ctx // 4
+    y = (depth // 4) * 2 + (ctx // 2) % 2
+    return x, y, ctx % 2, depth % 4
+
+
+def device_at(x, y, core, z):
+    return (x * 4 + (y % 2) * 2 + core, (y // 2) * 4 + z)
+
+
+def step_of(p, by):
+    return (p + by + 4) % 4
+
+
+def greet(devices):
+    barrier = pltpu.get_barrier_semaphore()
+    for device in devices:
+        pl.semaphore_signal(barrier, inc=1, device_id=device, device_id_type=MESH)
+    pl.semaphore_wait(barrier, len(devices))
+
+
+def rows_dot(a, b):
+    return lax.dot_general(a, b, (((1,), (1,)), ((), ())), preferred_element_type=jnp.float32)
+
+
+def columns_dot(a, b):
+    return lax.dot_general(a, b, (((0,), (0,)), ((), ())), preferred_element_type=jnp.float32)
+
+
+CB = 768
+ORDER = (0, 2, 1, 3)
+
+
+def tail_kernel(
+    ynorm_in,
+    packed_in,
+    stream_in,
+    dstream_in,
+    hidden_in,
+    gain_in,
+    wqkv_in,
+    win_in,
+    wout_in,
+    d_attn_ref,
+    d_wqkv_ref,
+    ynorm,
+    d_packed,
+    stream,
+    d_stream,
+    hidden,
+    gain,
+    wqkv,
+    win,
+    wout,
+    dy,
+    d_units,
+    d_normed,
+    d_hidden,
+    d_other,
+    g_parts,
+    core_sum,
+    first_in,
+    first_out,
+    second_in,
+    third_out,
+    third_in,
+    load_sem,
+    send_sem,
+    recv_sem,
+):
+    x, y, core, z = place()
+    other_core = device_at(x, y, 1 - core, z)
+
+    def x_at(by):
+        return device_at(step_of(x, by), y, core, z)
+
+    def y_at(by):
+        return device_at(x, step_of(y, by), core, z)
+
+    def z_at(by):
+        return device_at(x, y, core, step_of(z, by))
+
+    loads = []
+    pairs = (
+        (ynorm_in, ynorm),
+        (packed_in, d_packed),
+        (wqkv_in, wqkv),
+        (stream_in, stream),
+        (dstream_in, d_stream),
+        (win_in, win),
+        (hidden_in, hidden),
+        (gain_in, gain),
+        (wout_in, wout),
+    )
+    for i, (source, target) in enumerate(pairs):
+        load = pltpu.make_async_copy(source, target, load_sem.at[i])
+        load.start()
+        loads.append(load)
+    greet([other_core] + [at(by) for at in (x_at, y_at, z_at) for by in (1, 2, 3)])
+
+    count = [0]
+
+    def send(source, target, device):
+        i = count[0]
+        count[0] += 1
+        copy = pltpu.make_async_remote_copy(
+            src_ref=source,
+            dst_ref=target,
+            send_sem=send_sem.at[i],
+            recv_sem=recv_sem.at[i],
+            device_id=device,
+            device_id_type=MESH,
+        )
+        copy.start()
+        return copy
+
+    loads[0].wait()
+    loads[1].wait()
+
+    core_sends = {}
+    far = {}
+    near = {}
+
+    def axis_of(cb):
+        return (x, x_at) if cb < 2 else (y, y_at)
+
+    def sign_of(cb):
+        return 1 if cb % 2 == 0 else -1
+
+    def chunk(cb, q):
+        return core_sum.at[cb, q] if cb < 2 else core_sum.at[cb, :, q]
+
+    def first_phase(cb):
+        core_sends[cb].wait_recv()
+        core_sum[cb] = (
+            core_sum[cb].astype(jnp.float32) + g_parts[core, cb].astype(jnp.float32)
+        ).astype(jnp.bfloat16)
+        p, at = axis_of(cb)
+        s = sign_of(cb)
+        far[cb] = send(chunk(cb, step_of(p, 2)), first_in.at[cb, 0], at(s))
+        near[cb] = send(chunk(cb, step_of(p, -s)), first_in.at[cb, 1], at(-s))
+
+    for i, cb in enumerate(ORDER):
+
+        def block(xi, carry, cb=cb):
+            left = ynorm[:, pl.ds(pl.multiple_of(xi * 256, 256), 256)]
+            product = columns_dot(left, d_packed[:, cb * CB : (cb + 1) * CB])
+            product = product.astype(jnp.bfloat16)
+            for ylo in range(2):
+                for c in range(2):
+                    for yhi in range(2):
+                        at = ylo * 128 + c * 64 + yhi * 32
+                        g_parts[c, cb, xi, yhi * 2 + ylo] = product[at : at + 32]
+            return carry
+
+        lax.fori_loop(0, 4, block, 0)
+        core_sends[cb] = send(g_parts.at[1 - core, cb], core_sum.at[cb], other_core)
+        if i > 0:
+            first_phase(ORDER[i - 1])
+    loads[2].wait()
+
+    def dy_block(n, carry):
+        columns = pl.ds(pl.multiple_of(n * 256, 256), 256)
+        dy[:, columns] = rows_dot(d_packed[...], wqkv[columns, :]).astype(jnp.bfloat16)
+        return carry
+
+    lax.fori_loop(0, 4, dy_block, 0)
+    first_phase(ORDER[3])
+    loads[3].wait()
+    loads[4].wait()
+
+    def units_block(n, carry):
+        rows = pl.ds(pl.multiple_of(n * 64, 64), 64)
+        s = stream[rows, :]
+        d = dy[rows, :].astype(jnp.float32)
+        r = lax.rsqrt(jnp.mean(s * s, axis=-1, keepdims=True) + eps)
+        dot = jnp.sum(d * s, axis=-1, keepdims=True)
+        ds = d_stream[rows, :] + r * d - s * (r * r * r * dot / 1024)
+        d_units[pl.ds(pl.multiple_of(n * 8, 8), 8), :] = jnp.sum(ds.reshape(8, 8, 1024), axis=1)
+        return carry
+
+    lax.fori_loop(0, 8, units_block, 0)
+    loads[5].wait()
+
+    def normed_block(n, carry):
+        columns = pl.ds(pl.multiple_of(n * 512, 512), 512)
+        d_normed[:, columns] = rows_dot(d_units[...].astype(jnp.bfloat16), win[columns, :]).astype(
+            jnp.bfloat16
+        )
+        return carry
+
+    lax.fori_loop(0, 8, normed_block, 0)
+    loads[6].wait()
+    loads[7].wait()
+    for n in range(2):
+        rows = pl.ds(n * 32, 32)
+        h = hidden[rows, :]
+        rscale = lax.rsqrt(jnp.mean(h * h, axis=-1, keepdims=True) + eps)
+        grad_gain = d_normed[rows, :].astype(jnp.float32) * gain[...]
+        dot_rows = jnp.sum(grad_gain * h, axis=-1, keepdims=True)
+        d_hidden[z, rows, :] = (
+            rscale * grad_gain - h * (rscale * rscale * rscale * dot_rows / D)
+        ).astype(jnp.bfloat16)
+
+    to_right = send(d_hidden.at[z], d_hidden.at[z], z_at(1))
+    to_left = send(d_hidden.at[z], d_hidden.at[z], z_at(-1))
+
+    second = {}
+    last = {}
+    for cb in ORDER:
+        p, at = axis_of(cb)
+        s = sign_of(cb)
+        far[cb].wait_recv()
+        mid = chunk(cb, step_of(p, s))
+        mid[...] = (mid[...].astype(jnp.float32) + first_in[cb, 0].astype(jnp.float32)).astype(
+            jnp.bfloat16
+        )
+        last[cb] = send(mid, first_in.at[cb, 2], at(s))
+
+    loads[8].wait()
+
+    for cb in ORDER:
+        p, at = axis_of(cb)
+        near[cb].wait_recv()
+        last[cb].wait_recv()
+        first_out[cb] = (
+            chunk(cb, p)[...].astype(jnp.float32)
+            + first_in[cb, 1].astype(jnp.float32)
+            + first_in[cb, 2].astype(jnp.float32)
+        ).astype(jnp.bfloat16)
+        q, at = (y, y_at) if cb < 2 else (x, x_at)
+        second[cb] = [
+            send(first_out.at[cb, step_of(q, by)], second_in.at[cb, by - 1], at(by))
+            for by in (1, 2, 3)
+        ]
+
+    to_right.wait_recv()
+    on_right = send(
+        d_hidden.at[step_of(z, -1), pl.ds(0, 32)], d_hidden.at[step_of(z, -1), pl.ds(0, 32)], z_at(1)
+    )
+    to_left.wait_recv()
+    on_left = send(
+        d_hidden.at[step_of(z, 1), pl.ds(32, 32)], d_hidden.at[step_of(z, 1), pl.ds(32, 32)], z_at(-1)
+    )
+
+    for pair in range(2):
+        sums = []
+        for cb in (2 * pair, 2 * pair + 1):
+            q = y if cb < 2 else x
+            total = first_out[cb, q].astype(jnp.float32)
+            for by in (1, 2, 3):
+                second[cb][by - 1].wait_recv()
+                total += second_in[cb, by - 1].astype(jnp.float32)
+            sums.append(total)
+        for zq in range(4):
+            third_out[zq, pair] = jnp.concatenate(
+                [one[zq * 8 : zq * 8 + 8] for one in sums], axis=0
+            ).astype(jnp.bfloat16)
+    third = [
+        send(third_out.at[step_of(z, by)], third_in.at[by - 1], z_at(by)) for by in (1, 2, 3)
+    ]
+
+    on_right.wait_recv()
+    on_left.wait_recv()
+    yhi = y // 2
+    full = d_hidden[...].reshape(256, D)
+    d_other[0] = rows_dot(full, wout[1 - yhi]).astype(jnp.bfloat16)
+    to_other = send(d_other.at[0], d_other.at[1], y_at(2))
+    d_attn_ref[pl.ds(pl.multiple_of(yhi * 256, 256), 256), :] = rows_dot(full, wout[yhi]).astype(
         jnp.bfloat16
     )
-    (d_units,) = pull_front((d_normed, d_stream))
-    d_weight = jnp.einsum("tw,tc->wc", normed, d_packed, preferred_element_type=jnp.float32)
-    return (d_units, d_weight)
+
+    for pair in range(2):
+        total = third_out[z, pair].astype(jnp.float32)
+        for by in (1, 2, 3):
+            if pair == 0:
+                third[by - 1].wait_recv()
+            total += third_in[by - 1, pair].astype(jnp.float32)
+        d_wqkv_ref[:, pair * 2 * CB : (pair * 2 + 1) * CB] = total[:8]
+        d_wqkv_ref[:, (pair * 2 + 1) * CB : (pair * 2 + 2) * CB] = total[8:]
+
+    to_other.wait_recv()
+    d_attn_ref[pl.ds(pl.multiple_of((1 - yhi) * 256, 256), 256), :] = d_other[1]
+    copies = list(core_sends.values()) + list(far.values()) + list(near.values())
+    copies += list(last.values()) + [one for group in second.values() for one in group]
+    copies += third + [to_right, to_left, on_right, on_left, to_other]
+    for copy in copies:
+        copy.wait_send()
+
+
+def tail(ynorm, d_packed, stream, d_stream, hidden, gain, w_qkv, full_in, out_pair):
+    bf16, f32 = jnp.bfloat16, jnp.float32
+    operands = (ynorm, d_packed, stream, d_stream, hidden, gain, w_qkv, full_in, out_pair)
+    return pl.pallas_call(
+        tail_kernel,
+        out_shape=(
+            jax.ShapeDtypeStruct((512, 256), bf16),
+            jax.ShapeDtypeStruct((8, 3072), f32),
+        ),
+        in_specs=[pl.BlockSpec(memory_space=pl.ANY)] * 9,
+        out_specs=(pl.BlockSpec(memory_space=pltpu.VMEM),) * 2,
+        scratch_shapes=[pltpu.VMEM(one.shape, one.dtype) for one in operands]
+        + [
+            pltpu.VMEM((512, 1024), bf16),
+            pltpu.VMEM((64, 1024), f32),
+            pltpu.VMEM((64, D), bf16),
+            pltpu.VMEM((4, 64, D), bf16),
+            pltpu.VMEM((2, 256, 256), bf16),
+            pltpu.VMEM((2, 4, 4, 4, 32, CB), bf16),
+            pltpu.VMEM((4, 4, 4, 32, CB), bf16),
+            pltpu.VMEM((4, 3, 4, 32, CB), bf16),
+            pltpu.VMEM((4, 4, 32, CB), bf16),
+            pltpu.VMEM((4, 3, 32, CB), bf16),
+            pltpu.VMEM((4, 2, 16, CB), bf16),
+            pltpu.VMEM((3, 2, 16, CB), bf16),
+            pltpu.SemaphoreType.DMA((9,)),
+            pltpu.SemaphoreType.DMA((40,)),
+            pltpu.SemaphoreType.DMA((40,)),
+        ],
+        compiler_params=pltpu.CompilerParams(
+            collective_id=1, has_side_effects=True, vmem_limit_bytes=60 * 1024 * 1024
+        ),
+        cost_estimate=pl.CostEstimate(
+            flops=9_000_000_000, bytes_accessed=30_000_000, transcendentals=0
+        ),
+    )(*operands)
 
 
 def body(
@@ -147,20 +475,15 @@
     rscale = lax.rsqrt(jnp.mean(hidden * hidden, axis=-1, keepdims=True) + eps)
     normed = (hidden * rscale * norm_gain).astype(jnp.bfloat16)
     units = jnp.dot(normed, full_in, preferred_element_type=jnp.float32).astype(jnp.bfloat16)
-    d_units, d_weight = depth_block(units, codes, embed, w_qkv, w_o, w_head, DHS)
-    d_normed = jnp.einsum("fk,dk->fd", d_units, full_in, preferred_element_type=jnp.float32).astype(
-        jnp.bfloat16
-    )
-    grad_gain = d_normed.astype(jnp.float32) * norm_gain
-    dot_rows = jnp.sum(grad_gain * hidden, axis=-1, keepdims=True)
-    d_hidden = (rscale * grad_gain - hidden * rscale * rscale * rscale * dot_rows / D).astype(
-        jnp.bfloat16
-    )
-    d_full = lax.all_gather(d_hidden, "depth", axis=0, tiled=True)
-    d_attn = jnp.einsum("rd,cd->rc", d_full, w_out_t, preferred_element_type=jnp.float32).astype(
-        jnp.bfloat16
-    )
-    d_wqkv = lax.psum_scatter(d_weight, ("ctx", "depth"), scatter_dimension=0, tiled=True)
+    ynorm, d_packed, stream, d_stream = depth_block(units, codes, embed, w_qkv, w_o, w_head, DHS)
+    w_other = lax.ppermute(w_out_t, "depth", [(d, (d + 4) % 8) for d in range(8)])
+    upper = mine // 4
+    out_pair = jnp.where(
+        upper == 0, jnp.stack([w_out_t, w_other]), jnp.stack([w_other, w_out_t])
+    )
+    d_attn, d_wqkv = tail(
+        ynorm, d_packed, stream, d_stream, hidden, norm_gain.reshape(1, D), w_qkv, full_in, out_pair
+    )
     return (d_attn, d_wqkv)
 
 

time: 1200 us -> 525 us (0.44)
  waiting for transfers between devices: 971 us -> 266 us
  Pallas kernels: 0 us -> 48.9 us
  matrix products: 111 us -> 81.5 us
    reduce_scatter x1 -> x0, waiting for transfers between devices: 657 us -> none  [body(): lax.psum_scatter(d_weight, ('ctx', 'depth'), scatter_dimension=0, tiled=T...]
    all_gather x1 -> x0, waiting for transfers between devices: 58.9 us -> none  [body(): d_full = lax.all_gather(d_hidden, 'depth', axis=0, tiled=True)]
    ppermute x0 -> x1, waiting for transfers between devices: none -> 55 us  [body(): lax.ppermute(w_out_t, 'depth', [(d, (d + 4) % 8) for d in range(8)])]
    pallas_call x0 -> x1, Pallas kernels: none -> 48.9 us  [tail(): pl.pallas_call(tail_kernel, out_shape=(jax.ShapeDtypeStruct((512, 256), b...]
    reduce_scatter x1, waiting for transfers between devices: 75.3 us -> 30.6 us  [body(): lax.psum_scatter(partial_value.astype(jnp.bfloat16), 'depth', scatter_dim...]
    dot_general x4 -> x0, matrix products: 29.1 us -> none  [the longest x1 10.5 us: depth_block(): jnp.einsum('tw,tc->wc', normed, d_packed, preferred_element_type=jnp.floa...]
  transfers between devices with their start and end apart: 6 -> 5, of which waited for: 6 -> 5; matrix products, arithmetic and copies ran while one was open for 3% -> 5% of each run, Pallas kernels for 0% -> 0%
where the time goes in v1:
time: 525 us; the launch traced here: 516 us
  waiting for transfers between devices  266 us (51%)
  matrix products  81.5 us (16%)
  local copies, waits for them, and re-layouts  52.6 us (10%)
  other arithmetic  49.4 us (9%)
  Pallas kernels  48.9 us (9%)
  between operations  15 us (3%)
    all_gather x1, waiting for transfers between devices, body(): full_in = lax.all_gather(w_in, 'depth', axis=0, tiled=True)  107 us
    ppermute x1, waiting for transfers between devices, body(): lax.ppermute(w_out_t, 'depth', [(d, (d + 4) % 8) for d in range(8)])  55 us
    pallas_call x1, Pallas kernels, tail(): pl.pallas_call(tail_kernel, out_shape=(jax.ShapeDtypeStruct((512, 256), b...  48.9 us
    all_gather x1, waiting for transfers between devices, body(): values = lax.all_gather(v_heads, 'ctx', axis=0, tiled=True)  39.1 us
    all_gather x1, waiting for transfers between devices, body(): keys = lax.all_gather(k_heads, 'ctx', axis=0, tiled=True)  31.9 us
    reduce_scatter x1, waiting for transfers between devices, body(): lax.psum_scatter(partial_value.astype(jnp.bfloat16), 'depth', scatter_dim...  30.6 us
    dot_general x1, matrix products, compute(): jnp.einsum('qhk,khd->qhd', weights.astype(jnp.bfloat16), values.reshape(c...  18.2 us
    reshape x2, local copies, waits for them, and re-layouts, depth_back(): packed.reshape(frames, steps, 3, heads, head_size).astype(jnp.float32)  17.4 us
  transfers between devices with their start and end apart: 5, of which 5 were waited for; matrix products, arithmetic and copies ran while one was open for 5% of the time, Pallas kernels for 0%

profile of v1, /device:TPU:0, one launch (start us, length us, event | category | flops | bytes accessed | tf_op | source)
XLA Modules:
  0.0 516.2 jit_solution(15648226722450439551)
XLA Ops:
  8.8 0.7 select_reduce_fusion.1
  9.5 0.9 select_reduce_fusion
  10.4 6.6 %broadcast_compare_fusion = (pred[512,8192]{0,1:T(8,128)(4,1)}, pred[]{:T(512)}) fusion(s32[512]{0:T(512)S(1)} %fusion.61, s32[8192]{0:T(1024)S(1)} %fusion.59), kind=kLoop, calls=%fused_computation.21 | loop fusion | flops 8388607 | bytes 4229121 | tf_op jit(solution)/shard_map/ge | solution.py:440
  17.7 31.9 %all-gather.4.cloned.1.call-done = bf16[8192,256]{1,0:T(8,128)(2,1)} async-done(((bf16[512,256]{1,0:T(8,128)(2,1)}), bf16[8192,256]{1,0:T(8,128)(2,1)}) %all-gather.4.cloned.1.call-update) | async-done | bytes 4194320 | tf_op jit(solution)/shard_map/all_gather | solution.py:436
  49.5 39.1 %all-gather.6.cloned.1.call-done = bf16[8192,256]{1,0:T(8,128)(2,1)} async-done(((bf16[512,256]{1,0:T(8,128)(2,1)}), bf16[8192,256]{1,0:T(8,128)(2,1)}) %all-gather.6.cloned.1.call-update) | async-done | bytes 4194320 | tf_op jit(solution)/shard_map/all_gather | solution.py:437
  88.7 50.4 %conditional.1 = (f32[512,2]{0,1:T(2,128)S(1)}, f32[512,2,128]{0,2,1:T(8,128)S(1)}) conditional(s32[]{:T(128)} %convert_element_type.57, () %tuple.17, (pred[512,8192]{0,1:T(8,128)(4,1)}, bf16[8192,256]{1,0:T(8,128)(2,1)}, bf16[512,256]{1,0:T(8,128)(2,1)S(1)}, bf16[8192,256]{1,0:T(8,128)(2,1)}) %tuple.43), branch_computations={%region_3.4_spmd, %region_4.7_spmd} | conditional | flops 4404018176 | bytes 123494416 | solution.py:465
  88.7 16.3 %fusion = (f32[512,2]{0,1:T(2,128)S(1)}, f32[2,8192,512]{2,1,0:T(8,128)}) fusion(pred[512,8192]{0,1:T(8,128)(4,1)} %get-tuple-element.9, bf16[8192,256]{1,0:T(8,128)(2,1)} %get-tuple-element.10, bf16[512,256]{1,0:T(8,128)(2,1)S(1)} %get-tuple-element.20), kind=kOutput, calls=%fused_computation.3 | convolution fusion | flops 2172648448 | bytes 42209280 | tf_op jit(solution)/shard_map/cond/branch_1_fun/qhd,khd->qhk/dot_general | solution.py:445
  105.0 18.2 %fusion.11 = f32[512,2,128]{2,0,1:T(8,128)S(1)} fusion(f32[2,8192,512]{2,1,0:T(8,128)} %get-tuple-element.23, f32[512,2]{0,1:T(2,128)S(1)} %broadcast_maximum_fusion, pred[512,8192]{0,1:T(8,128)(4,1)} %get-tuple-element.9, bf16[8192,256]{1,0:T(8,128)(2,1)} %get-tuple-element.12), kind=kOutput, calls=%fused_computation.13 | convolution fusion | flops 2189426688 | bytes 42471424 | tf_op jit(solution)/shard_map/cond/branch_1_fun/qhk,khd->qhd/dot_general | solution.py:457
  123.5 15.6 %fusion.2 = f32[512,2]{0,1:T(2,128)S(1)} fusion(f32[2,8192,512]{2,1,0:T(8,128)} %get-tuple-element.23, f32[512,2]{0,1:T(2,128)S(1)} %broadcast_maximum_fusion, pred[512,8192]{0,1:T(8,128)(4,1)} %get-tuple-element.9), kind=kLoop, calls=%fused_computation.5 | loop fusion | flops 41942016 | bytes 37756928 | tf_op jit(solution)/shard_map/cond/branch_1_fun/reduce_sum | solution.py:456
  139.1 2.9 fusion.74
  142.3 2.6 convert_element_type.60
  145.5 2.8 collective-permute-start
  148.6 6.1 %gather_fusion = bf16[448,1024]{1,0:T(8,128)(2,1)S(1)} fusion(bf16[2048,1024]{1,0:T(8,128)(2,1)} %param.23, s32[1024]{0:T(1024)S(1)} %pad_clamp_fusion), kind=kCustom, calls=%fused_computation | custom fusion | bytes 1836800 | tf_op jit(solution)/shard_map/jit(_take)/gather | solution.py:33
  154.7 1.3 reshape.165
  156.2 1.4 broadcast_select_fusion
  157.6 55.0 %collective-permute-done = bf16[256,4096]{1,0:T(8,128)(2,1)} collective-permute-done((bf16[256,4096]{1,0:T(8,128)(2,1)}, bf16[256,4096]{1,0:T(8,128)(2,1)}, u32[]{:S(2)}, u32[]{:S(2)}) %collective-permute-start) | collective-permute-done | bytes 2097184 | tf_op jit(solution)/shard_map/ppermute | solution.py:479
  212.7 5.9 %maximum_select_fusion.wout_in = bf16[2,256,4096]{2,1,0:T(8,128)(2,1)} fusion(bf16[1,256,4096]{2,1,0:T(8,128)(2,1)} %bitcast.18, bf16[1,256,4096]{2,1,0:T(8,128)(2,1)} %bitcast.106, pred[]{:T(512)S(6)} %eq.58), kind=kLoop, calls=%fused_computation.23 | loop fusion | flops 6291456 | bytes 8388609 | tf_op jit(solution)/shard_map/jit(_where)/select_n | solution.py:481
  218.5 30.6 %reduce-scatter.2.cloned.1.call-done = bf16[64,4096]{1,0:T(8,128)(2,1)} async-done(((bf16[512,4096]{1,0:T(8,128)(2,1)}), bf16[64,4096]{1,0:T(8,128)(2,1)}) %reduce-scatter.2.cloned.1.call-update) | async-done | bytes 524304 | tf_op jit(solution)/shard_map/reduce_scatter | solution.py:471
  249.2 1.2 multiply_reduce_fusion.3
  250.4 107.2 %all-gather.8.cloned.1.call-done.win_in = bf16[4096,1024]{1,0:T(8,128)(2,1)} async-done(((bf16[512,1024]{1,0:T(8,128)(2,1)}), bf16[4096,1024]{1,0:T(8,128)(2,1)}) %all-gather.8.cloned.1.call-update) | async-done | bytes 8388624 | tf_op jit(solution)/shard_map/all_gather | solution.py:474
  357.6 5.2 %fusion.44 = f32[64,1024]{1,0:T(8,128)S(1)} fusion(bf16[4096,1024]{1,0:T(8,128)(2,1)} %all-gather.8.cloned.1.call-done.win_in, f32[4096]{0:T(1024)S(1)} %copy-done.16, f32[64]{0:T(128)S(1)} %add_rsqrt_fusion.1, bf16[64,4096]{1,0:T(8,128)(2,1)} %reduce-scatter.2.cloned.1.call-done), kind=kOutput, calls=%fused_computation.68 | convolution fusion | flops 538050560 | bytes 9191680 | tf_op jit(solution)/shard_map/dot_general | solution.py:477
  363.5 1.8 fusion.37
  365.4 1.0 copy-done.12
  366.3 7.5 %convolution_convert_fusion = bf16[512,3072]{1,0:T(8,128)(2,1)} fusion(bf16[512,1024]{1,0:T(8,128)(2,1)S(1)} %get-tuple-element.28.ynorm_in, bf16[1024,3072]{1,0:T(8,128)(2,1)} %wqkv_in.1), kind=kOutput, calls=%fused_computation.22 | convolution fusion | flops 3222798336 | bytes 10485760 | tf_op jit(solution)/shard_map/dot_general | solution.py:68
  373.9 8.6 %reshape.160 = bf16[64,8,3,16,64]{4,3,2,1,0:T(8,128)(2,1)} reshape(bf16[512,3072]{1,0:T(8,128)(2,1)} %convolution_convert_fusion) | data formatting | bytes 6291456 | tf_op jit(solution)/shard_map/jvp()/reshape | solution.py:43
  382.5 5.6 %fusion.73 = (bf16[64,8,1,16,64]{4,3,2,1,0:T(8,128)(2,1)S(1)}, bf16[64,8,1,16,64]{4,3,2,1,0:T(8,128)(2,1)S(1)}, bf16[64,8,1,16,64]{4,3,2,1,0:T(8,128)(2,1)S(1)}) fusion(bf16[64,8,3,16,64]{4,3,2,1,0:T(8,128)(2,1)} %reshape.160), kind=kLoop, calls=%fused_computation.125 | loop fusion | bytes 6291456 | tf_op jit(solution)/shard_map/jvp()/slice | solution.py:44
  388.1 2.2 fusion.28
  390.3 1.1 multiply_divide_fusion
  391.4 1.8 convert_bitcast_fusion
  393.2 2.0 copy.109
  395.2 4.2 reshape.161
  399.4 2.9 multiply_reduce_fusion.1
  402.3 2.5 exponential_reduce_fusion
  404.8 2.7 fusion.29
  407.9 1.4 copy-done.8
  409.3 1.3 fusion.75
  410.6 2.3 reshape.162
  413.0 6.4 %convolution_bitcast_fusion.2 = f32[64,8,1,16,64]{4,1,3,0,2:T(8,128)} fusion(bf16[64,8,16,64]{3,2,1,0:T(8,128)(2,1)} %reshape.162, f32[64,16,8,8]{2,3,1,0:T(8,128)} %copy-done.5, f32[64,16,8]{2,1,0:T(8,128)} %copy-done.13, pred[8,8]{0,1:T(8,128)(4,1)S(1)} %iota_compare_fusion.4), kind=kOutput, calls=%fused_computation.42 | convolution fusion | flops 8585216 | bytes 3440704 | tf_op jit(solution)/shard_map/transpose(jvp(fhqk,fkhd->fqhd))/dot_general | solution.py:51
  419.4 2.9 multiply_reduce_fusion
  422.4 5.3 %convolution_bitcast_fusion.1 = f32[64,8,1,16,64]{4,1,3,0,2:T(8,128)} fusion(bf16[64,8,1,16,64]{4,3,2,1,0:T(8,128)(2,1)} %copy-done.11, f32[64,16,8,8]{2,3,1,0:T(8,128)S(1)} %get-tuple-element.40, f32[64,16,8,8]{2,3,1,0:T(8,128)S(1)} %copy-done.6, f32[64,16,8]{2,1,0:T(8,128)S(1)} %neg.6, f32[64,16,8]{2,1,0:T(8,128)S(1)} %copy-done.14, ...), kind=kOutput, calls=%fused_computation.41 | convolution fusion | flops 8781824 | bytes 3735616 | tf_op jit(solution)/shard_map/transpose(jvp(fqhd,fkhd->fhqk))/dot_general | solution.py:44
  427.7 3.3 convolution_bitcast_fusion
  431.0 9.1 %add_convert_fusion = bf16[64,8,3,16,64]{4,1,3,0,2:T(8,128)(2,1)} fusion(f32[64,8,1,16,64]{4,1,3,0,2:T(8,128)} %convolution_bitcast_fusion, f32[64,8,1,16,64]{4,1,3,0,2:T(8,128)} %convolution_bitcast_fusion.1, f32[64,8,1,16,64]{4,1,3,0,2:T(8,128)} %convolution_bitcast_fusion.2), kind=kLoop, calls=%fused_computation.20 | loop fusion | flops 4718592 | bytes 9437184 | tf_op jit(solution)/shard_map/transpose(jvp())/convert_element_type | solution.py:43
  440.1 7.3 %copy.112 = bf16[64,8,3,16,64]{4,3,2,1,0:T(8,128)(2,1)} copy(bf16[64,8,3,16,64]{4,1,3,0,2:T(8,128)(2,1)} %add_convert_fusion) | data formatting | bytes 6291456 | tf_op jit(solution)/shard_map/transpose(jvp())/convert_element_type | solution.py:43
  447.4 8.8 %reshape.163.packed_in = bf16[512,3072]{1,0:T(8,128)(2,1)} reshape(bf16[64,8,3,16,64]{4,3,2,1,0:T(8,128)(2,1)} %copy.112) | data formatting | bytes 6291456 | tf_op jit(solution)/shard_map/transpose(jvp())/reshape | solution.py:43
  456.2 1.1 convert_element_type.61.hidden_in
  457.3 48.9 %shard_map.141 = (bf16[512,256]{1,0:T(8,128)(2,1)}, f32[8,3072]{1,0:T(8,128)}) custom-call(bf16[512,1024]{1,0:T(8,128)(2,1)} %copy-done.12, bf16[512,3072]{1,0:T(8,128)(2,1)} %reshape.163.packed_in, f32[512,1024]{1,0:T(8,128)} %get-tuple-element.27.stream_in, f32[512,1024]{1,0:T(8,128)} %copy-done.8, f32[64,4096]{1,0:T(8,128)} %convert_element_type.61.hidden_in, ...), custom_call_target="tpu_custom_call" | custom-call | flops 8999999488 | bytes 30000000 | tf_op jit(solution)/shard_map/pallas_call | solution.py:371
  506.2 1.7 copy.174
  507.9 1.5 copy.175
  (73 shorter events, 4.4 us)
Async XLA Ops:
  7.2 392.2 %copy-start = (bf16[1024,1024]{1,0:T(8,128)(2,1)S(1)}, bf16[1024,1024]{1,0:T(8,128)(2,1)}, u32[]{:S(2)}) copy-start(bf16[1024,1024]{1,0:T(8,128)(2,1)} %param.25) | copy-start | bytes 6291460
  7.2 81.5 %copy-start.19 = (bf16[512,256]{1,0:T(8,128)(2,1)S(1)}, bf16[512,256]{1,0:T(8,128)(2,1)}, u32[]{:S(2)}) copy-start(bf16[512,256]{1,0:T(8,128)(2,1)} %param.15) | copy-start | bytes 786436
  7.2 42.4 %all-gather.4.cloned.1.call-start = ((), (), s32[]{:S(2)}) async-start(), calls=%async_computation.1 | async-start | bytes 4456448 | tf_op jit(solution)/shard_map/all_gather | solution.py:436
  7.9 80.8 %all-gather.6.cloned.1.call-start = ((), (), s32[]{:S(2)}) async-start(), calls=%async_computation.2 | async-start | bytes 4456448 | tf_op jit(solution)/shard_map/all_gather | solution.py:437
  8.7 240.5 %reduce-scatter.2.cloned.1.call-start = ((), (), s32[]{:S(2)}) async-start(), calls=%async_computation.3 | async-start | bytes 4718592 | tf_op jit(solution)/shard_map/reduce_scatter | solution.py:471
  139.1 3.0 copy-start.15
  144.9 3.4 copy-start.17
  144.9 212.7 %all-gather.8.cloned.1.call-start = ((), (), s32[]{:S(2)}) async-start(), calls=%async_computation.4 | async-start | bytes 9437184 | tf_op jit(solution)/shard_map/all_gather | solution.py:474
  145.5 67.2 %collective-permute-start = (bf16[256,4096]{1,0:T(8,128)(2,1)}, bf16[256,4096]{1,0:T(8,128)(2,1)}, u32[]{:S(2)}, u32[]{:S(2)}) collective-permute-start(bf16[256,4096]{1,0:T(8,128)(2,1)} %param.20), channel_id=1, source_target_pairs={{0,4},{1,5},{2,6},{3,7},{4,0},{5,1},{6,2},{7,3},{8,12},{9,13},{10,... | collective-permute-start | bytes 6291464 | tf_op jit(solution)/shard_map/ppermute | solution.py:479
  212.7 145.0 %copy-start.16 = (f32[4096]{0:T(1024)S(1)}, f32[4096]{0:T(1024)}, u32[]{:S(2)}) copy-start(f32[4096]{0:T(1024)} %param.21) | copy-start | bytes 49156
  365.4 1.0 copy-start.12
  388.0 2.2 copy-start.9
  388.0 2.2 copy-start.11
  388.1 3.3 copy-start.2
  390.3 2.9 copy-start.5
  390.3 2.9 copy-start.13
  399.4 2.9 copy-start.18
  407.9 1.4 copy-start.8
  413.0 6.4 %copy-start.1 = (bf16[64,8,16,64]{3,2,1,0:T(8,128)(2,1)S(1)}, bf16[64,8,16,64]{3,2,1,0:T(8,128)(2,1)}, u32[]{:S(2)}) copy-start(bf16[64,8,16,64]{3,2,1,0:T(8,128)(2,1)} %reshape.162) | copy-start | bytes 3145732
  413.0 6.4 %copy-start.3 = (bf16[64,8,1,16,64]{4,3,2,1,0:T(8,128)(2,1)S(1)}, bf16[64,8,1,16,64]{4,3,2,1,0:T(8,128)(2,1)}, u32[]{:S(2)}) copy-start(bf16[64,8,1,16,64]{4,3,2,1,0:T(8,128)(2,1)} %copy-done.2) | copy-start | bytes 3145732
  413.0 6.4 %copy-start.6 = (f32[64,16,8,8]{2,3,1,0:T(8,128)S(1)}, f32[64,16,8,8]{2,3,1,0:T(8,128)}, u32[]{:S(2)}) copy-start(f32[64,16,8,8]{2,3,1,0:T(8,128)} %copy-done.5) | copy-start | bytes 786436
  413.0 6.4 %copy-start.7 = (f32[64,16,8]{2,1,0:T(8,128)S(1)}, f32[64,16,8]{2,1,0:T(8,128)}, u32[]{:S(2)}) copy-start(f32[64,16,8]{2,1,0:T(8,128)} %multiply_divide_fusion) | copy-start | bytes 98308
  419.4 2.9 copy-start.14
  422.3 5.3 %copy-start.10 = (bf16[64,8,1,16,64]{4,3,2,1,0:T(8,128)(2,1)S(1)}, bf16[64,8,1,16,64]{4,3,2,1,0:T(8,128)(2,1)}, u32[]{:S(2)}) copy-start(bf16[64,8,1,16,64]{4,3,2,1,0:T(8,128)(2,1)} %copy-done.9) | copy-start | bytes 3145732
  447.4 8.8 %copy-start.4 = (bf16[64,4096]{1,0:T(8,128)(2,1)S(1)}, bf16[64,4096]{1,0:T(8,128)(2,1)}, u32[]{:S(2)}) copy-start(bf16[64,4096]{1,0:T(8,128)(2,1)} %reduce-scatter.2.cloned.1.call-done) | copy-start | bytes 1572868
Sparse Core Ops, SparseCore 0:
  9.7 39.7 all-gather.3
  51.2 37.3 all-gather.5
  145.0 104.0 reduce-scatter.1
  251.6 105.9 all-gather.7

commit v2 on v1

--- a/solution.py
+++ b/solution.py
@@ -16,63 +16,6 @@
 MESH = pl.DeviceIdType.MESH
 
 
-def positions_of(index, block_of, half):
-    which = index // half
-    slots = jnp.arange(block_of.shape[0], dtype=jnp.int32)
-    picked = jnp.sum(jnp.where(which[:, None] == slots[None, :], block_of[None, :], 0), axis=1)
-    return picked * half + index % half
-
-
-def rms_rows(values):
-    return values * lax.rsqrt(jnp.mean(values * values, axis=-1, keepdims=True) + eps)
-
-
-def depth_front(units, codes, embed):
-    frames, steps = codes.shape
-    width = embed.shape[1]
-    earlier = jnp.take(embed, codes[:, : steps - 1], axis=0).astype(jnp.float32)
-    lead = jnp.zeros((frames, 1, width), jnp.float32)
-    stream = units.astype(jnp.float32)[:, None, :] + jnp.concatenate([lead, earlier], axis=1)
-    normed = rms_rows(stream).astype(jnp.bfloat16).reshape(frames * steps, width)
-    return (normed, stream)
-
-
-def depth_back(packed, stream, codes, w_o, w_head, head_size):
-    frames, steps, width = stream.shape
-    heads = width // head_size
-    parts = packed.reshape(frames, steps, 3, heads, head_size).astype(jnp.float32)
-    scores = jnp.einsum("fqhd,fkhd->fhqk", parts[:, :, 0], parts[:, :, 1]) * (
-        1.0 / math.sqrt(head_size)
-    )
-    causal = jnp.arange(steps)[:, None] >= jnp.arange(steps)[None, :]
-    weights = jnp.where(causal, jnp.exp(scores), 0.0)
-    weights = weights / jnp.sum(weights, axis=-1, keepdims=True)
-    mixed = (
-        jnp.einsum("fhqk,fkhd->fqhd", weights, parts[:, :, 2])
-        .astype(jnp.bfloat16)
-        .reshape(frames * steps, width)
-    )
-    after = stream.reshape(frames * steps, width) + jnp.dot(
-        mixed, w_o, preferred_element_type=jnp.float32
-    )
-    normed = rms_rows(after).astype(jnp.bfloat16)
-    logits = jnp.dot(normed, w_head, preferred_element_type=jnp.float32)
-    total = jnp.log(jnp.sum(jnp.exp(logits), axis=-1))
-    vocab = jnp.arange(w_head.shape[1], dtype=jnp.int32)
-    picked = jnp.sum(jnp.where(codes.reshape(-1)[:, None] == vocab[None, :], logits, 0.0), axis=-1)
-    return jnp.sum(total - picked)
-
-
-def depth_block(units, codes, embed, w_qkv, w_o, w_head, head_size):
-    normed, stream = depth_front(units, codes, embed)
-    packed = jnp.dot(normed, w_qkv, preferred_element_type=jnp.float32).astype(jnp.bfloat16)
-    loss, pull = jax.vjp(
-        lambda a, b: depth_back(a, b, codes, w_o, w_head, head_size), packed, stream
-    )
-    d_packed, d_stream = pull(jnp.ones_like(loss))
-    return normed, d_packed, stream.reshape(normed.shape), d_stream.reshape(normed.shape)
-
-
 def place():
     ctx = lax.axis_index("ctx")
     depth = lax.axis_index("depth")
@@ -102,6 +45,607 @@
 
 def columns_dot(a, b):
     return lax.dot_general(a, b, (((0,), (0,)), ((), ())), preferred_element_type=jnp.float32)
+
+
+def front_kernel(
+    block_of,
+    q_in,
+    k_in,
+    v_in,
+    resid_in,
+    gain_ref,
+    win_in,
+    wout_in,
+    embed_in,
+    earlier_code,
+    units_ref,
+    earlier_ref,
+    hidden_ref,
+    win_out,
+    wout_out,
+    kv,
+    queries,
+    top,
+    total,
+    mixed,
+    attn,
+    heads_in,
+    win,
+    wout,
+    embed,
+    resid,
+    partial,
+    partial_in,
+    normed,
+    load_sem,
+    send_sem,
+    recv_sem,
+):
+    x, y, core, z = place()
+    yhi = y // 2
+    ylo = y % 2
+    side = y + 1 - 2 * ylo
+    cross = 3 - y
+    own = yhi * 4 + z
+    crossed = (1 - yhi) * 4 + z
+    other_core = device_at(x, y, 1 - core, z)
+
+    def x_at(by):
+        return device_at(step_of(x, by), y, core, z)
+
+    def z_at(by):
+        return device_at(x, y, core, step_of(z, by))
+
+    loads = []
+
+    def load(source, target):
+        i = len(loads)
+        copy = pltpu.make_async_copy(source, target, load_sem.at[i])
+        copy.start()
+        loads.append(copy)
+        return copy
+
+    sends = []
+
+    def send(source, target, device):
+        i = len(sends)
+        copy = pltpu.make_async_remote_copy(
+            src_ref=source,
+            dst_ref=target,
+            send_sem=send_sem.at[i],
+            recv_sem=recv_sem.at[i],
+            device_id=device,
+            device_id_type=MESH,
+        )
+        copy.start()
+        sends.append(copy)
+        return copy
+
+    def half(which):
+        return pl.ds(pl.multiple_of(which * 512, 512), 512)
+
+    def lanes(which):
+        return pl.ds(pl.multiple_of(which * 128, 128), 128)
+
+    load_k = load(k_in.at[:, lanes(core)], kv.at[0, x, ylo, half(core)])
+    load_v = load(v_in.at[:, lanes(core)], kv.at[1, x, ylo, half(core)])
+    load_q = load(q_in.at[:, lanes(core)], queries.at[half(core)])
+    greet(
+        [
+            other_core,
+            x_at(1),
+            x_at(-1),
+            z_at(1),
+            z_at(-1),
+            device_at(x, side, core, z),
+            device_at(x, cross, core, z),
+            device_at(x, step_of(y, 2), core, z),
+            device_at(x, step_of(y, 2), 1 - core, z),
+        ]
+    )
+    swap_k = send(k_in.at[:, lanes(1 - core)], kv.at[0, x, ylo, half(core)], other_core)
+    swap_v = send(v_in.at[:, lanes(1 - core)], kv.at[1, x, ylo, half(core)], other_core)
+    swap_q = send(q_in.at[:, lanes(1 - core)], queries.at[half(core)], other_core)
+
+    shard = win_in.at[pl.ds(pl.multiple_of(core * 256, 256), 256)]
+    win_cross = send(shard, win.at[own, core], device_at(x, cross, core, z))
+    win_right = send(shard, win.at[own, core], z_at(1))
+    win_left = send(shard, win.at[own, core], z_at(-1))
+    load_win = [
+        load(win_in.at[pl.ds(i * 256, 256)], win.at[own, i]) for i in range(2)
+    ]
+    load_embed = load(embed_in, embed)
+    load_wout = load(wout_in, wout.at[yhi])
+    load_resid = load(resid_in, resid)
+
+    load_k.wait()
+    load_v.wait()
+    swap_k.wait_recv()
+    swap_v.wait_recv()
+    kv_side = send(kv.at[:, x, ylo], kv.at[:, x, ylo], device_at(x, side, core, z))
+    kv_right = send(kv.at[:, x, ylo], kv.at[:, x, ylo], x_at(1))
+    kv_left = send(kv.at[:, x, ylo], kv.at[:, x, ylo], x_at(-1))
+
+    top[...] = jnp.full_like(top, -1e29)
+    total[...] = jnp.zeros_like(total)
+    mixed[...] = jnp.zeros_like(mixed)
+    factor = math.log2(math.e) / math.sqrt(HS)
+
+    def attend(xi, yi):
+        base = xi * 8 + yi * 4
+        lane = lax.broadcasted_iota(jnp.int32, (1, 1024), 1)
+        block = jnp.where(
+            lane < 512,
+            jnp.where(lane < 256, block_of[base], block_of[base + 1]),
+            jnp.where(lane < 768, block_of[base + 2], block_of[base + 3]),
+        )
+        key_pos = lane % 256 + block * 256
+
+        def rows_of(n, carry):
+            rows = pl.ds(pl.multiple_of(n * 256, 256), 256)
+            pos = lax.broadcasted_iota(jnp.int32, (256, 1), 0) + block_of[x * 8 + ylo * 4 + n] * 256
+            scores = rows_dot(queries[rows, :], kv[0, xi, yi])
+            scores = jnp.where(pos >= key_pos, scores, -1e30)
+            before = top[rows, :]
+            now = jnp.maximum(before, jnp.max(scores, axis=-1, keepdims=True))
+            weights = jnp.exp2((scores - now[:, :1]) * factor)
+            fade = jnp.exp2((before - now) * factor)
+            top[rows, :] = now
+            total[rows, :] = total[rows, :] * fade + jnp.sum(weights, axis=-1, keepdims=True)
+            mixed[rows, :] = mixed[rows, :] * fade + jnp.dot(
+                weights.astype(jnp.bfloat16), kv[1, xi, yi], preferred_element_type=jnp.float32
+            )
+            return carry
+
+        lax.fori_loop(0, 4, rows_of, 0)
+
+    load_q.wait()
+    swap_q.wait_recv()
+    attend(x, ylo)
+
+    load_embed.wait()
+
+    def look_up(n, carry):
+        rows = pl.ds(pl.multiple_of(n * 128, 128), 128)
+        entry = lax.broadcasted_iota(jnp.int32, (128, 2048), 1)
+        hot = (entry == earlier_code[rows, :]).astype(jnp.bfloat16)
+        earlier_ref[rows, :] = jnp.dot(
+            hot, embed[...], preferred_element_type=jnp.float32
+        ).astype(jnp.bfloat16)
+        return carry
+
+    lax.fori_loop(0, 4, look_up, 0)
+
+    def pass_on(ref, left_arrived, right_arrived, at, before, after, first, second):
+        left_arrived.wait_recv()
+        on_right = send(ref(before, first), ref(before, first), at(1))
+        right_arrived.wait_recv()
+        on_left = send(ref(after, second), ref(after, second), at(-1))
+        return on_right, on_left
+
+    def kv_of(yi):
+        return lambda xi, part: kv.at[:, xi, yi, part]
+
+    def win_of(up):
+        return lambda zi, part: win.at[up * 4 + zi, core, part]
+
+    kv_side.wait_recv()
+    side_lo = 1 - ylo
+    side_right = send(kv.at[:, x, side_lo], kv.at[:, x, side_lo], x_at(1))
+    side_left = send(kv.at[:, x, side_lo], kv.at[:, x, side_lo], x_at(-1))
+    win_cross.wait_recv()
+    cross_right = send(win.at[crossed, core], win.at[crossed, core], z_at(1))
+    cross_left = send(win.at[crossed, core], win.at[crossed, core], z_at(-1))
+    wout_half = pl.ds(pl.multiple_of(core * 128, 128), 128)
+    wout_cross = send(
+        wout_in.at[wout_half], wout.at[yhi, wout_half], device_at(x, cross, core, z)
+    )
+    to_core = [send(win.at[crossed, core], win.at[crossed, core], other_core)]
+    attend(x, side_lo)
+
+    before_x, after_x = step_of(x, -1), step_of(x, 1)
+    before_z, after_z = step_of(z, -1), step_of(z, 1)
+    win_on = pass_on(
+        win_of(yhi), win_right, win_left, z_at, before_z, after_z, pl.ds(0, 128), pl.ds(128, 128)
+    )
+    kv_on = pass_on(
+        kv_of(ylo), kv_right, kv_left, x_at, before_x, after_x, pl.ds(0, 512), pl.ds(512, 512)
+    )
+    for zi in (before_z, after_z):
+        to_core.append(send(win.at[yhi * 4 + zi, core], win.at[yhi * 4 + zi, core], other_core))
+    attend(before_x, ylo)
+    attend(after_x, ylo)
+    side_on = pass_on(
+        kv_of(side_lo), side_right, side_left, x_at, before_x, after_x, pl.ds(0, 512), pl.ds(512, 512)
+    )
+    cross_on = pass_on(
+        win_of(1 - yhi), cross_right, cross_left, z_at, before_z, after_z, pl.ds(0, 128), pl.ds(128, 128)
+    )
+    for zi in (before_z, after_z):
+        at = (1 - yhi) * 4 + zi
+        to_core.append(send(win.at[at, core], win.at[at, core], other_core))
+    attend(before_x, side_lo)
+    attend(after_x, side_lo)
+    wout_cross.wait_recv()
+    wout_core = send(wout.at[1 - yhi, wout_half], wout.at[1 - yhi, wout_half], other_core)
+    for one in kv_on:
+        one.wait_recv()
+    attend(step_of(x, 2), ylo)
+    for one in win_on:
+        one.wait_recv()
+    at = yhi * 4 + step_of(z, 2)
+    to_core.append(send(win.at[at, core], win.at[at, core], other_core))
+    for one in side_on:
+        one.wait_recv()
+    attend(step_of(x, 2), side_lo)
+
+    for n in range(4):
+        rows = pl.ds(n * 256, 256)
+        attn[n // 2, n % 2] = (mixed[rows, :] / total[rows, :]).astype(jnp.bfloat16)
+    swaps = [
+        send(attn.at[1 - core, yhi], heads_in.at[yhi, core], other_core),
+        send(
+            attn.at[core, 1 - yhi],
+            heads_in.at[yhi, core],
+            device_at(x, step_of(y, 2), core, z),
+        ),
+        send(
+            attn.at[1 - core, 1 - yhi],
+            heads_in.at[yhi, core],
+            device_at(x, step_of(y, 2), 1 - core, z),
+        ),
+    ]
+    heads_in[yhi, core] = attn[core, yhi]
+    for one in cross_on:
+        one.wait_recv()
+    at = (1 - yhi) * 4 + step_of(z, 2)
+    to_core.append(send(win.at[at, core], win.at[at, core], other_core))
+    load_wout.wait()
+    wout_core.wait_recv()
+    store_wout = load(wout, wout_out)
+    for one in swaps:
+        one.wait_recv()
+
+    far = {}
+    near = {}
+    last = {}
+    for cb in range(4):
+        s = 1 if cb % 2 == 0 else -1
+        columns = pl.ds(cb * 1024, 1024)
+        sums = jnp.zeros((256, 1024), jnp.float32)
+        for up in range(2):
+            left = jnp.concatenate([heads_in[up, 0], heads_in[up, 1]], axis=1)
+            sums += jnp.dot(left, wout[up, :, columns], preferred_element_type=jnp.float32)
+        partial[cb] = sums.astype(jnp.bfloat16).reshape(4, 64, 1024)
+        far[cb] = send(partial.at[cb, step_of(z, 2)], partial_in.at[cb, 0], z_at(s))
+        near[cb] = send(partial.at[cb, step_of(z, -s)], partial_in.at[cb, 1], z_at(-s))
+    for cb in range(4):
+        s = 1 if cb % 2 == 0 else -1
+        far[cb].wait_recv()
+        mid = step_of(z, s)
+        partial[cb, mid] = (
+            partial[cb, mid].astype(jnp.float32) + partial_in[cb, 0].astype(jnp.float32)
+        ).astype(jnp.bfloat16)
+        last[cb] = send(partial.at[cb, mid], partial_in.at[cb, 2], z_at(s))
+    load_resid.wait()
+    squares = jnp.zeros((64, 1), jnp.float32)
+    for cb in range(4):
+        columns = pl.ds(cb * 1024, 1024)
+        near[cb].wait_recv()
+        last[cb].wait_recv()
+        h = partial[cb, z].astype(jnp.float32) + resid[:, columns].astype(jnp.float32)
+        h = h + partial_in[cb, 1].astype(jnp.float32) + partial_in[cb, 2].astype(jnp.float32)
+        hidden_ref[:, columns] = h
+        squares += jnp.sum(h * h, axis=-1, keepdims=True)
+    rscale = lax.rsqrt(squares / D + eps)
+    for cb in range(4):
+        columns = pl.ds(cb * 1024, 1024)
+        normed[:, columns] = (hidden_ref[:, columns] * rscale * gain_ref[:, columns]).astype(
+            jnp.bfloat16
+        )
+    for one in load_win:
+        one.wait()
+    for one in to_core:
+        one.wait_recv()
+    store_win = load(win, win_out)
+
+    def enter(n, carry):
+        columns = pl.ds(pl.multiple_of(n * 256, 256), 256)
+        units_ref[:, columns] = jnp.dot(
+            normed[...],
+            win[:, :, :, columns].reshape(D, 256),
+            preferred_element_type=jnp.float32,
+        ).astype(jnp.bfloat16)
+        return carry
+
+    lax.fori_loop(0, 4, enter, 0)
+    store_wout.wait()
+    store_win.wait()
+    for one in sends:
+        one.wait_send()
+
+
+def front(block_of, q, k, v, resid, gain, w_in, w_out, embed, earlier_code):
+    bf16, f32 = jnp.bfloat16, jnp.float32
+    shapes = (
+        ((64, 1024), bf16),
+        ((512, 1024), bf16),
+        ((64, D), f32),
+        ((8, 2, 256, 1024), bf16),
+        ((2, 256, D), bf16),
+    )
+    vmem = pl.BlockSpec(memory_space=pltpu.VMEM)
+    anywhere = pl.BlockSpec(memory_space=pl.ANY)
+    return pl.pallas_call(
+        front_kernel,
+        out_shape=tuple(jax.ShapeDtypeStruct(*one) for one in shapes),
+        in_specs=[pl.BlockSpec(memory_space=pltpu.SMEM)]
+        + [anywhere] * 4
+        + [vmem]
+        + [anywhere] * 3
+        + [vmem],
+        out_specs=(vmem, vmem, vmem, anywhere, anywhere),
+        scratch_shapes=[
+            pltpu.VMEM((2, 4, 2, 1024, HS), bf16),
+            pltpu.VMEM((1024, HS), bf16),
+            pltpu.VMEM((1024, HS), f32),
+            pltpu.VMEM((1024, HS), f32),
+            pltpu.VMEM((1024, HS), f32),
+            pltpu.VMEM((2, 2, 256, HS), bf16),
+            pltpu.VMEM((2, 2, 256, HS), bf16),
+            pltpu.VMEM((8, 2, 256, 1024), bf16),
+            pltpu.VMEM((2, 256, D), bf16),
+            pltpu.VMEM((2048, 1024), bf16),
+            pltpu.VMEM((64, D), bf16),
+            pltpu.VMEM((4, 4, 64, 1024), bf16),
+            pltpu.VMEM((4, 3, 64, 1024), bf16),
+            pltpu.VMEM((64, D), bf16),
+            pltpu.SemaphoreType.DMA((12,)),
+            pltpu.SemaphoreType.DMA((48,)),
+            pltpu.SemaphoreType.DMA((48,)),
+        ],
+        compiler_params=pltpu.CompilerParams(
+            collective_id=2, has_side_effects=True, vmem_limit_bytes=60 * 1024 * 1024
+        ),
+        cost_estimate=pl.CostEstimate(
+            flops=9_000_000_000, bytes_accessed=40_000_000, transcendentals=8_000_000
+        ),
+    )(block_of, q, k, v, resid, gain, w_in, w_out, embed, earlier_code)
+
+
+STEPS = 8
+GROUP = 128
+
+
+def lower_lanes():
+    return lax.broadcasted_iota(jnp.int32, (1, 128), 1) < DHS
+
+
+def split_heads(value, low):
+    zero = jnp.zeros_like(value)
+    return jnp.concatenate([jnp.where(low, value, zero), jnp.where(low, zero, value)], axis=0)
+
+
+def join_heads(value, low):
+    return jnp.where(low, value[:GROUP], value[GROUP:])
+
+
+def per_head(op, value):
+    return jnp.concatenate(
+        [
+            jnp.broadcast_to(op(half, axis=-1, keepdims=True), half.shape)
+            for half in (value[:, :GROUP], value[:, GROUP:])
+        ],
+        axis=1,
+    )
+
+
+def depth_kernel(
+    units_ref,
+    earlier_ref,
+    code_ref,
+    wqkv_in,
+    wo_in,
+    whead_in,
+    ynorm,
+    d_packed,
+    stream,
+    d_stream,
+    wqkv,
+    wo,
+    whead,
+    packed,
+    weights,
+    mixed,
+    after,
+    ynorm2,
+    grown,
+    d_logits,
+    dy2,
+    load_sem,
+):
+    loads = []
+    for i, (source, target) in enumerate(((wqkv_in, wqkv), (wo_in, wo), (whead_in, whead))):
+        load = pltpu.make_async_copy(source, target, load_sem.at[i])
+        load.start()
+        loads.append(load)
+    frame_of = lax.broadcasted_iota(jnp.int32, (GROUP, 16), 0) // STEPS
+    spread = (frame_of == lax.broadcasted_iota(jnp.int32, (GROUP, 16), 1)).astype(jnp.bfloat16)
+
+    def front(n, carry):
+        rows = pl.ds(pl.multiple_of(n * GROUP, GROUP), GROUP)
+        units = units_ref[pl.ds(pl.multiple_of(n * 16, 16), 16), :]
+        s = jnp.dot(spread, units, preferred_element_type=jnp.float32)
+        s = s + earlier_ref[rows, :].astype(jnp.float32)
+        r = lax.rsqrt(jnp.mean(s * s, axis=-1, keepdims=True) + eps)
+        stream[rows, :] = s
+        ynorm[rows, :] = (s * r).astype(jnp.bfloat16)
+        return carry
+
+    lax.fori_loop(0, 4, front, 0)
+    loads[0].wait()
+
+    def project(n, carry):
+        columns = pl.ds(pl.multiple_of(n * 512, 512), 512)
+        packed[:, columns] = jnp.dot(
+            ynorm[...], wqkv[:, columns], preferred_element_type=jnp.float32
+        ).astype(jnp.bfloat16)
+        return carry
+
+    lax.fori_loop(0, 6, project, 0)
+
+    low = lower_lanes()
+    row = lax.broadcasted_iota(jnp.int32, (GROUP, 2 * GROUP), 0)
+    column = lax.broadcasted_iota(jnp.int32, (GROUP, 2 * GROUP), 1) % GROUP
+    seen = jnp.logical_and(row // STEPS == column // STEPS, column <= row)
+
+    def mix(n, carry):
+        rows = pl.ds(pl.multiple_of(n * GROUP, GROUP), GROUP)
+        for pair in range(8):
+            at = pair * 128
+            q = packed[rows, at : at + 128]
+            k = split_heads(packed[rows, 1024 + at : 1024 + at + 128], low)
+            v = split_heads(packed[rows, 2048 + at : 2048 + at + 128], low)
+            scores = rows_dot(q, k) * (1.0 / math.sqrt(DHS))
+            grown_scores = jnp.exp(jnp.where(seen, scores, -1e30))
+            a = (grown_scores / per_head(jnp.sum, grown_scores)).astype(jnp.bfloat16)
+            weights[pair, rows, :] = a
+            mixed[rows, at : at + 128] = jnp.dot(
+                a, v, preferred_element_type=jnp.float32
+            ).astype(jnp.bfloat16)
+        return carry
+
+    lax.fori_loop(0, 4, mix, 0)
+    loads[1].wait()
+
+    def add_mixed(n, carry):
+        columns = pl.ds(pl.multiple_of(n * 256, 256), 256)
+        after[:, columns] = stream[:, columns] + jnp.dot(
+            mixed[...], wo[:, columns], preferred_element_type=jnp.float32
+        )
+        return carry
+
+    lax.fori_loop(0, 4, add_mixed, 0)
+
+    def norm2(n, carry):
+        rows = pl.ds(pl.multiple_of(n * 64, 64), 64)
+        s = after[rows, :]
+        r = lax.rsqrt(jnp.mean(s * s, axis=-1, keepdims=True) + eps)
+        ynorm2[rows, :] = (s * r).astype(jnp.bfloat16)
+        return carry
+
+    lax.fori_loop(0, 8, norm2, 0)
+    loads[2].wait()
+
+    def grow(n, total):
+        columns = pl.ds(pl.multiple_of(n * 256, 256), 256)
+        e = jnp.exp(
+            jnp.dot(ynorm2[...], whead[:, columns], preferred_element_type=jnp.float32)
+        )
+        grown[:, columns] = e
+        return total + jnp.sum(e, axis=-1, keepdims=True)
+
+    total = lax.fori_loop(0, 8, grow, jnp.zeros((512, 1), jnp.float32))
+    inverse = 1.0 / total
+    code = code_ref[...]
+
+    def from_loss(n, carry):
+        columns = pl.ds(pl.multiple_of(n * 256, 256), 256)
+        entry = lax.broadcasted_iota(jnp.int32, (512, 256), 1) + n * 256
+        d_logits[:, columns] = (
+            grown[:, columns] * inverse - (entry == code).astype(jnp.float32)
+        ).astype(jnp.bfloat16)
+        return carry
+
+    lax.fori_loop(0, 8, from_loss, 0)
+
+    def to_ynorm2(n, carry):
+        columns = pl.ds(pl.multiple_of(n * 256, 256), 256)
+        dy2[:, columns] = rows_dot(d_logits[...], whead[columns, :]).astype(jnp.bfloat16)
+        return carry
+
+    lax.fori_loop(0, 4, to_ynorm2, 0)
+
+    def to_after(n, carry):
+        rows = pl.ds(pl.multiple_of(n * 64, 64), 64)
+        s = after[rows, :]
+        d = dy2[rows, :].astype(jnp.float32)
+        r = lax.rsqrt(jnp.mean(s * s, axis=-1, keepdims=True) + eps)
+        dot = jnp.sum(d * s, axis=-1, keepdims=True)
+        da = r * d - s * (r * r * r * dot / 1024)
+        d_stream[rows, :] = da
+        dy2[rows, :] = da.astype(jnp.bfloat16)
+        return carry
+
+    lax.fori_loop(0, 8, to_after, 0)
+
+    def to_mixed(n, carry):
+        columns = pl.ds(pl.multiple_of(n * 256, 256), 256)
+        mixed[:, columns] = rows_dot(dy2[...], wo[columns, :]).astype(jnp.bfloat16)
+        return carry
+
+    lax.fori_loop(0, 4, to_mixed, 0)
+
+    def unmix(n, carry):
+        rows = pl.ds(pl.multiple_of(n * GROUP, GROUP), GROUP)
+        for pair in range(8):
+            at = pair * 128
+            q = packed[rows, at : at + 128]
+            k = split_heads(packed[rows, 1024 + at : 1024 + at + 128], low)
+            v = split_heads(packed[rows, 2048 + at : 2048 + at + 128], low)
+            d_mixed = mixed[rows, at : at + 128]
+            a = weights[pair, rows, :]
+            wide = a.astype(jnp.float32)
+            part = wide * rows_dot(d_mixed, v)
+            ds = (part - wide * per_head(jnp.sum, part)) * (1.0 / math.sqrt(DHS))
+            ds = ds.astype(jnp.bfloat16)
+            d_packed[rows, at : at + 128] = jnp.dot(
+                ds, k, preferred_element_type=jnp.float32
+            ).astype(jnp.bfloat16)
+            d_packed[rows, 1024 + at : 1024 + at + 128] = join_heads(
+                columns_dot(ds, q), low
+            ).astype(jnp.bfloat16)
+            d_packed[rows, 2048 + at : 2048 + at + 128] = join_heads(
+                columns_dot(a, d_mixed), low
+            ).astype(jnp.bfloat16)
+        return carry
+
+    lax.fori_loop(0, 4, unmix, 0)
+
+
+def depth_step(units, earlier, code, w_qkv, w_o, w_head):
+    bf16, f32 = jnp.bfloat16, jnp.float32
+    shapes = (
+        ((512, 1024), bf16),
+        ((512, 3072), bf16),
+        ((512, 1024), f32),
+        ((512, 1024), f32),
+    )
+    return pl.pallas_call(
+        depth_kernel,
+        out_shape=tuple(jax.ShapeDtypeStruct(*one) for one in shapes),
+        in_specs=[pl.BlockSpec(memory_space=pltpu.VMEM)] * 3
+        + [pl.BlockSpec(memory_space=pl.ANY)] * 3,
+        out_specs=(pl.BlockSpec(memory_space=pltpu.VMEM),) * 4,
+        scratch_shapes=[
+            pltpu.VMEM((1024, 3072), bf16),
+            pltpu.VMEM((1024, 1024), bf16),
+            pltpu.VMEM((1024, 2048), bf16),
+            pltpu.VMEM((512, 3072), bf16),
+            pltpu.VMEM((8, 512, 256), bf16),
+            pltpu.VMEM((512, 1024), bf16),
+            pltpu.VMEM((512, 1024), f32),
+            pltpu.VMEM((512, 1024), bf16),
+            pltpu.VMEM((512, 2048), f32),
+            pltpu.VMEM((512, 2048), bf16),
+            pltpu.VMEM((512, 1024), bf16),
+            pltpu.SemaphoreType.DMA((3,)),
+        ],
+        compiler_params=pltpu.CompilerParams(vmem_limit_bytes=60 * 1024 * 1024),
+        cost_estimate=pl.CostEstimate(
+            flops=13_000_000_000, bytes_accessed=30_000_000, transcendentals=2_000_000
+        ),
+    )(units, earlier, code, w_qkv, w_o, w_head)
 
 
 CB = 768
@@ -418,73 +962,18 @@
     w_head,
     codes,
 ):
-    rows, width = q_heads.shape
-    heads = width // HS
-    half = rows // 2
-    owners = lax.axis_size("depth")
-    owned = rows // owners
-    mine = lax.axis_index("depth")
-    index = lax.axis_index("ctx") * rows + jnp.arange(rows, dtype=jnp.int32)
-    pos_q = positions_of(index, block_of, half)
-    queries = q_heads.reshape(rows, heads, HS)
-    scale = 1.0 / math.sqrt(HS)
-    start_state = (
-        jnp.full((rows, heads), -1e30, jnp.float32),
-        jnp.zeros((rows, heads), jnp.float32),
-        jnp.zeros((rows, heads, HS), jnp.float32),
-    )
-    keys = lax.all_gather(k_heads, "ctx", axis=0, tiled=True)
-    values = lax.all_gather(v_heads, "ctx", axis=0, tiled=True)
-    count = keys.shape[0]
-    pos_k = positions_of(jnp.arange(count, dtype=jnp.int32), block_of, half)
-    visible = pos_q[:, None] >= pos_k[None, :]
-
-    def compute(state):
-        top, total, acc = state
-        scores = (
-            jnp.einsum(
-                "qhd,khd->qhk",
-                queries,
-                keys.reshape(count, heads, HS),
-                preferred_element_type=jnp.float32,
-            )
-            * scale
-        )
-        scores = jnp.where(visible[:, None, :], scores, -1e30)
-        new_top = jnp.maximum(top, jnp.max(scores, axis=-1))
-        weights = jnp.where(visible[:, None, :], jnp.exp(scores - new_top[:, :, None]), 0.0)
-        total = jnp.sum(weights, axis=-1)
-        acc = jnp.einsum(
-            "qhk,khd->qhd",
-            weights.astype(jnp.bfloat16),
-            values.reshape(count, heads, HS),
-            preferred_element_type=jnp.float32,
-        )
-        return (new_top, total, acc)
-
-    top, total, acc = lax.cond(jnp.any(visible), compute, lambda state: state, start_state)
-    attn = (acc / total[:, :, None]).astype(jnp.bfloat16).reshape(rows, width)
-    partial_value = jnp.dot(attn, w_out_t, preferred_element_type=jnp.float32)
-    offset = mine * owned
-    own_rows = lax.dynamic_slice_in_dim(partial_value, offset, owned, 0) + resid.astype(jnp.float32)
-    partial_value = lax.dynamic_update_slice_in_dim(partial_value, own_rows, offset, 0)
-    hidden = lax.psum_scatter(
-        partial_value.astype(jnp.bfloat16), "depth", scatter_dimension=0, tiled=True
-    ).astype(jnp.float32)
-    full_in = lax.all_gather(w_in, "depth", axis=0, tiled=True)
-    rscale = lax.rsqrt(jnp.mean(hidden * hidden, axis=-1, keepdims=True) + eps)
-    normed = (hidden * rscale * norm_gain).astype(jnp.bfloat16)
-    units = jnp.dot(normed, full_in, preferred_element_type=jnp.float32).astype(jnp.bfloat16)
-    ynorm, d_packed, stream, d_stream = depth_block(units, codes, embed, w_qkv, w_o, w_head, DHS)
-    w_other = lax.ppermute(w_out_t, "depth", [(d, (d + 4) % 8) for d in range(8)])
-    upper = mine // 4
-    out_pair = jnp.where(
-        upper == 0, jnp.stack([w_out_t, w_other]), jnp.stack([w_other, w_out_t])
-    )
-    d_attn, d_wqkv = tail(
-        ynorm, d_packed, stream, d_stream, hidden, norm_gain.reshape(1, D), w_qkv, full_in, out_pair
-    )
-    return (d_attn, d_wqkv)
+    gain = norm_gain.reshape(1, D)
+    first = jnp.full((codes.shape[0], 1), -1, codes.dtype)
+    earlier_code = jnp.concatenate([first, codes[:, :-1]], axis=1).reshape(-1, 1)
+    units, earlier, hidden, win, wout = front(
+        block_of, q_heads, k_heads, v_heads, resid, gain, w_in, w_out_t, embed, earlier_code
+    )
+    ynorm, d_packed, stream, d_stream = depth_step(
+        units, earlier, codes.reshape(-1, 1), w_qkv, w_o, w_head
+    )
+    return tail(
+        ynorm, d_packed, stream, d_stream, hidden, gain, w_qkv, win.reshape(D, -1), wout
+    )
 
 
 def solution(mesh):

time: 525 us -> 181 us (0.34); the launches traced: 516 us -> 181 us
  waiting for transfers between devices: 266 us -> 0 us
  Pallas kernels: 48.9 us -> 174 us
  matrix products: 81.5 us -> 0 us
  other arithmetic: 49.4 us -> 0 us
  local copies, waits for them, and re-layouts: 52.6 us -> 6.51 us
  between operations: 15 us -> 0.66 us
    all_gather x3 -> x0, waiting for transfers between devices: 178 us -> none  [the longest x1 107 us: body(): full_in = lax.all_gather(w_in, 'depth', axis=0, tiled=True)]
    pallas_call x0 -> x2, Pallas kernels: none -> 123 us  [the longest x1 83.2 us: front(): pl.pallas_call(front_kernel, out_shape=tuple((jax.ShapeDtypeStruct(*one)...]
    dot_general x15 -> x0, matrix products: 81.5 us -> none  [the longest x1 18.2 us: compute(): jnp.einsum('qhk,khd->qhd', weights.astype(jnp.bfloat16), values.reshape(c...]
    ppermute x1 -> x0, waiting for transfers between devices: 55 us -> none  [body(): lax.ppermute(w_out_t, 'depth', [(d, (d + 4) % 8) for d in range(8)])]
    reduce_scatter x1 -> x0, waiting for transfers between devices: 30.6 us -> none  [body(): lax.psum_scatter(partial_value.astype(jnp.bfloat16), 'depth', scatter_dim...]
    reshape x4 -> x2, local copies, waits for them, and re-layouts: 24 us -> 1.67 us  [the longest x1 0.84 us: body(): codes.reshape(-1, 1)]
    reduce_sum x5 -> x0, other arithmetic: 19 us -> none  [the longest x1 15.6 us: compute(): total = jnp.sum(weights, axis=-1)]
    convert_element_type x4 -> x0, other arithmetic: 12.9 us -> none  [the longest x1 9.11 us: depth_back(): packed.reshape(frames, steps, 3, heads, head_size).astype(jnp.float32)]
  transfers between devices with their start and end apart: 5 -> 0, of which waited for: 5 -> 0; matrix products, arithmetic and copies ran while one was open for 5% -> 0% of each run, Pallas kernels for 0% -> 0%
where the time goes in v2:
time: 181 us
  Pallas kernels  174 us (96%)
  local copies, waits for them, and re-layouts  6.51 us (4%)
    pallas_call x1, Pallas kernels, front(): pl.pallas_call(front_kernel, out_shape=tuple((jax.ShapeDtypeStruct(*one)...  83.2 us
    pallas_call x1, Pallas kernels, tail(): pl.pallas_call(tail_kernel, out_shape=(jax.ShapeDtypeStruct((512, 256), b...  50.7 us
    pallas_call x1, Pallas kernels, depth_step(): pl.pallas_call(depth_kernel, out_shape=tuple((jax.ShapeDtypeStruct(*one)...  39.7 us
    unnamed x4, local copies, waits for them, and re-layouts  4.76 us

profile of v2, /device:TPU:0, one launch (start us, length us, event | category | flops | bytes accessed | tf_op | source)
XLA Modules:
  0.0 180.7 jit_solution(11959436485491089986)
XLA Ops:
  0.6 0.8 copy.21
  1.4 0.1 concatenate.3.clone
  1.5 0.8 copy.19
  2.3 0.8 reshape.21.code_ref
  3.1 0.8 reshape.20.earlier_code
  3.9 83.2 %shard_map.140 = (bf16[64,1024]{1,0:T(8,128)(2,1)}, bf16[512,1024]{1,0:T(8,128)(2,1)}, f32[64,4096]{1,0:T(8,128)}, bf16[8,2,256,1024]{3,2,1,0:T(8,128)(2,1)}, bf16[2,256,4096]{2,1,0:T(8,128)(2,1)}) custom-call(s32[32]{0:T(128)} %block_of.1, bf16[512,256]{1,0:T(8,128)(2,1)} %q_in.1, bf16[512,256]{1,0:T(8,128)(2,1)} %k_in.1, bf16[512,256]{1,0:T(8,128)(2,1)} %v_in.1, ...), custom_call_target="tpu_custom_call" | custom-call | flops 8999999488 | bytes 40000000 | tf_op jit(solution)/shard_map/pallas_call | solution.py:379
  87.1 39.7 %shard_map.141 = (bf16[512,1024]{1,0:T(8,128)(2,1)}, bf16[512,3072]{1,0:T(8,128)(2,1)}, f32[512,1024]{1,0:T(8,128)}, f32[512,1024]{1,0:T(8,128)}) custom-call(bf16[64,1024]{1,0:T(8,128)(2,1)} %get-tuple-element.11.units_ref, bf16[512,1024]{1,0:T(8,128)(2,1)} %get-tuple-element.12.earlier_ref, s32[512,1]{1,0:T(8,128)} %reshape.21.code_ref, ...), custom_call_target="tpu_custom_call" | custom-call | flops 12999999488 | bytes 30000000 | tf_op jit(solution)/shard_map/pallas_call | solution.py:624
  126.8 50.7 %shard_map.142 = (bf16[512,256]{1,0:T(8,128)(2,1)}, f32[8,3072]{1,0:T(8,128)}) custom-call(bf16[512,1024]{1,0:T(8,128)(2,1)} %get-tuple-element.13.ynorm_in, bf16[512,3072]{1,0:T(8,128)(2,1)} %get-tuple-element.14.packed_in, f32[512,1024]{1,0:T(8,128)} %get-tuple-element.15.stream_in, f32[512,1024]{1,0:T(8,128)} %get-tuple-element.16.dstream_in, ...), custom_call_target="tpu_custom_call" | custom-call | flops 8999999488 | bytes 30000000 | tf_op jit(solution)/shard_map/pallas_call | solution.py:915
  177.5 1.7 copy.24
  179.2 1.5 copy.25

commit v3 on v2

--- a/solution.py
+++ b/solution.py
@@ -41,10 +41,6 @@
 
 def rows_dot(a, b):
     return lax.dot_general(a, b, (((1,), (1,)), ((), ())), preferred_element_type=jnp.float32)
-
-
-def columns_dot(a, b):
-    return lax.dot_general(a, b, (((0,), (0,)), ((), ())), preferred_element_type=jnp.float32)
 
 
 def front_kernel(
@@ -76,6 +72,7 @@
     resid,
     partial,
     partial_in,
+    hidden,
     normed,
     load_sem,
     send_sem,
@@ -335,12 +332,13 @@
         last[cb].wait_recv()
         h = partial[cb, z].astype(jnp.float32) + resid[:, columns].astype(jnp.float32)
         h = h + partial_in[cb, 1].astype(jnp.float32) + partial_in[cb, 2].astype(jnp.float32)
-        hidden_ref[:, columns] = h
+        hidden[:, columns] = h
+        hidden_ref[:, columns] = h.astype(jnp.bfloat16)
         squares += jnp.sum(h * h, axis=-1, keepdims=True)
     rscale = lax.rsqrt(squares / D + eps)
     for cb in range(4):
         columns = pl.ds(cb * 1024, 1024)
-        normed[:, columns] = (hidden_ref[:, columns] * rscale * gain_ref[:, columns]).astype(
+        normed[:, columns] = (hidden[:, columns] * rscale * gain_ref[:, columns]).astype(
             jnp.bfloat16
         )
     for one in load_win:
@@ -370,7 +368,7 @@
     shapes = (
         ((64, 1024), bf16),
         ((512, 1024), bf16),
-        ((64, D), f32),
+        ((64, D), bf16),
         ((8, 2, 256, 1024), bf16),
         ((2, 256, D), bf16),
     )
@@ -399,6 +397,7 @@
             pltpu.VMEM((64, D), bf16),
             pltpu.VMEM((4, 4, 64, 1024), bf16),
             pltpu.VMEM((4, 3, 64, 1024), bf16),
+            pltpu.VMEM((64, D), f32),
             pltpu.VMEM((64, D), bf16),
             pltpu.SemaphoreType.DMA((12,)),
             pltpu.SemaphoreType.DMA((48,)),
@@ -413,6 +412,8 @@
     )(block_of, q, k, v, resid, gain, w_in, w_out, embed, earlier_code)
 
 
+CB = 768
+ORDER = (0, 2, 1, 3)
 STEPS = 8
 GROUP = 128
 
@@ -430,253 +431,46 @@
     return jnp.where(low, value[:GROUP], value[GROUP:])
 
 
-def per_head(op, value):
+def head_sums(value, axis):
+    halves = jnp.split(value, 2, axis=axis)
     return jnp.concatenate(
-        [
-            jnp.broadcast_to(op(half, axis=-1, keepdims=True), half.shape)
-            for half in (value[:, :GROUP], value[:, GROUP:])
-        ],
-        axis=1,
-    )
-
-
-def depth_kernel(
+        [jnp.broadcast_to(jnp.sum(h, axis=axis, keepdims=True), h.shape) for h in halves], axis=axis
+    )
+
+
+def product(a, b):
+    return jnp.dot(a, b, preferred_element_type=jnp.float32)
+
+
+def back_kernel(
     units_ref,
     earlier_ref,
     code_ref,
+    gain,
+    hidden_in,
     wqkv_in,
     wo_in,
     whead_in,
-    ynorm,
-    d_packed,
-    stream,
-    d_stream,
+    win_in,
+    wout_in,
+    d_attn_ref,
+    d_wqkv_ref,
     wqkv,
     wo,
     whead,
+    win,
+    wide,
+    ynorm,
+    ynorm_t,
+    stream,
     packed,
     weights,
     mixed,
     after,
     ynorm2,
     grown,
-    d_logits,
-    dy2,
-    load_sem,
-):
-    loads = []
-    for i, (source, target) in enumerate(((wqkv_in, wqkv), (wo_in, wo), (whead_in, whead))):
-        load = pltpu.make_async_copy(source, target, load_sem.at[i])
-        load.start()
-        loads.append(load)
-    frame_of = lax.broadcasted_iota(jnp.int32, (GROUP, 16), 0) // STEPS
-    spread = (frame_of == lax.broadcasted_iota(jnp.int32, (GROUP, 16), 1)).astype(jnp.bfloat16)
-
-    def front(n, carry):
-        rows = pl.ds(pl.multiple_of(n * GROUP, GROUP), GROUP)
-        units = units_ref[pl.ds(pl.multiple_of(n * 16, 16), 16), :]
-        s = jnp.dot(spread, units, preferred_element_type=jnp.float32)
-        s = s + earlier_ref[rows, :].astype(jnp.float32)
-        r = lax.rsqrt(jnp.mean(s * s, axis=-1, keepdims=True) + eps)
-        stream[rows, :] = s
-        ynorm[rows, :] = (s * r).astype(jnp.bfloat16)
-        return carry
-
-    lax.fori_loop(0, 4, front, 0)
-    loads[0].wait()
-
-    def project(n, carry):
-        columns = pl.ds(pl.multiple_of(n * 512, 512), 512)
-        packed[:, columns] = jnp.dot(
-            ynorm[...], wqkv[:, columns], preferred_element_type=jnp.float32
-        ).astype(jnp.bfloat16)
-        return carry
-
-    lax.fori_loop(0, 6, project, 0)
-
-    low = lower_lanes()
-    row = lax.broadcasted_iota(jnp.int32, (GROUP, 2 * GROUP), 0)
-    column = lax.broadcasted_iota(jnp.int32, (GROUP, 2 * GROUP), 1) % GROUP
-    seen = jnp.logical_and(row // STEPS == column // STEPS, column <= row)
-
-    def mix(n, carry):
-        rows = pl.ds(pl.multiple_of(n * GROUP, GROUP), GROUP)
-        for pair in range(8):
-            at = pair * 128
-            q = packed[rows, at : at + 128]
-            k = split_heads(packed[rows, 1024 + at : 1024 + at + 128], low)
-            v = split_heads(packed[rows, 2048 + at : 2048 + at + 128], low)
-            scores = rows_dot(q, k) * (1.0 / math.sqrt(DHS))
-            grown_scores = jnp.exp(jnp.where(seen, scores, -1e30))
-            a = (grown_scores / per_head(jnp.sum, grown_scores)).astype(jnp.bfloat16)
-            weights[pair, rows, :] = a
-            mixed[rows, at : at + 128] = jnp.dot(
-                a, v, preferred_element_type=jnp.float32
-            ).astype(jnp.bfloat16)
-        return carry
-
-    lax.fori_loop(0, 4, mix, 0)
-    loads[1].wait()
-
-    def add_mixed(n, carry):
-        columns = pl.ds(pl.multiple_of(n * 256, 256), 256)
-        after[:, columns] = stream[:, columns] + jnp.dot(
-            mixed[...], wo[:, columns], preferred_element_type=jnp.float32
-        )
-        return carry
-
-    lax.fori_loop(0, 4, add_mixed, 0)
-
-    def norm2(n, carry):
-        rows = pl.ds(pl.multiple_of(n * 64, 64), 64)
-        s = after[rows, :]
-        r = lax.rsqrt(jnp.mean(s * s, axis=-1, keepdims=True) + eps)
-        ynorm2[rows, :] = (s * r).astype(jnp.bfloat16)
-        return carry
-
-    lax.fori_loop(0, 8, norm2, 0)
-    loads[2].wait()
-
-    def grow(n, total):
-        columns = pl.ds(pl.multiple_of(n * 256, 256), 256)
-        e = jnp.exp(
-            jnp.dot(ynorm2[...], whead[:, columns], preferred_element_type=jnp.float32)
-        )
-        grown[:, columns] = e
-        return total + jnp.sum(e, axis=-1, keepdims=True)
-
-    total = lax.fori_loop(0, 8, grow, jnp.zeros((512, 1), jnp.float32))
-    inverse = 1.0 / total
-    code = code_ref[...]
-
-    def from_loss(n, carry):
-        columns = pl.ds(pl.multiple_of(n * 256, 256), 256)
-        entry = lax.broadcasted_iota(jnp.int32, (512, 256), 1) + n * 256
-        d_logits[:, columns] = (
-            grown[:, columns] * inverse - (entry == code).astype(jnp.float32)
-        ).astype(jnp.bfloat16)
-        return carry
-
-    lax.fori_loop(0, 8, from_loss, 0)
-
-    def to_ynorm2(n, carry):
-        columns = pl.ds(pl.multiple_of(n * 256, 256), 256)
-        dy2[:, columns] = rows_dot(d_logits[...], whead[columns, :]).astype(jnp.bfloat16)
-        return carry
-
-    lax.fori_loop(0, 4, to_ynorm2, 0)
-
-    def to_after(n, carry):
-        rows = pl.ds(pl.multiple_of(n * 64, 64), 64)
-        s = after[rows, :]
-        d = dy2[rows, :].astype(jnp.float32)
-        r = lax.rsqrt(jnp.mean(s * s, axis=-1, keepdims=True) + eps)
-        dot = jnp.sum(d * s, axis=-1, keepdims=True)
-        da = r * d - s * (r * r * r * dot / 1024)
-        d_stream[rows, :] = da
-        dy2[rows, :] = da.astype(jnp.bfloat16)
-        return carry
-
-    lax.fori_loop(0, 8, to_after, 0)
-
-    def to_mixed(n, carry):
-        columns = pl.ds(pl.multiple_of(n * 256, 256), 256)
-        mixed[:, columns] = rows_dot(dy2[...], wo[columns, :]).astype(jnp.bfloat16)
-        return carry
-
-    lax.fori_loop(0, 4, to_mixed, 0)
-
-    def unmix(n, carry):
-        rows = pl.ds(pl.multiple_of(n * GROUP, GROUP), GROUP)
-        for pair in range(8):
-            at = pair * 128
-            q = packed[rows, at : at + 128]
-            k = split_heads(packed[rows, 1024 + at : 1024 + at + 128], low)
-            v = split_heads(packed[rows, 2048 + at : 2048 + at + 128], low)
-            d_mixed = mixed[rows, at : at + 128]
-            a = weights[pair, rows, :]
-            wide = a.astype(jnp.float32)
-            part = wide * rows_dot(d_mixed, v)
-            ds = (part - wide * per_head(jnp.sum, part)) * (1.0 / math.sqrt(DHS))
-            ds = ds.astype(jnp.bfloat16)
-            d_packed[rows, at : at + 128] = jnp.dot(
-                ds, k, preferred_element_type=jnp.float32
-            ).astype(jnp.bfloat16)
-            d_packed[rows, 1024 + at : 1024 + at + 128] = join_heads(
-                columns_dot(ds, q), low
-            ).astype(jnp.bfloat16)
-            d_packed[rows, 2048 + at : 2048 + at + 128] = join_heads(
-                columns_dot(a, d_mixed), low
-            ).astype(jnp.bfloat16)
-        return carry
-
-    lax.fori_loop(0, 4, unmix, 0)
-
-
-def depth_step(units, earlier, code, w_qkv, w_o, w_head):
-    bf16, f32 = jnp.bfloat16, jnp.float32
-    shapes = (
-        ((512, 1024), bf16),
-        ((512, 3072), bf16),
-        ((512, 1024), f32),
-        ((512, 1024), f32),
-    )
-    return pl.pallas_call(
-        depth_kernel,
-        out_shape=tuple(jax.ShapeDtypeStruct(*one) for one in shapes),
-        in_specs=[pl.BlockSpec(memory_space=pltpu.VMEM)] * 3
-        + [pl.BlockSpec(memory_space=pl.ANY)] * 3,
-        out_specs=(pl.BlockSpec(memory_space=pltpu.VMEM),) * 4,
-        scratch_shapes=[
-            pltpu.VMEM((1024, 3072), bf16),
-            pltpu.VMEM((1024, 1024), bf16),
-            pltpu.VMEM((1024, 2048), bf16),
-            pltpu.VMEM((512, 3072), bf16),
-            pltpu.VMEM((8, 512, 256), bf16),
-            pltpu.VMEM((512, 1024), bf16),
-            pltpu.VMEM((512, 1024), f32),
-            pltpu.VMEM((512, 1024), bf16),
-            pltpu.VMEM((512, 2048), f32),
-            pltpu.VMEM((512, 2048), bf16),
-            pltpu.VMEM((512, 1024), bf16),
-            pltpu.SemaphoreType.DMA((3,)),
-        ],
-        compiler_params=pltpu.CompilerParams(vmem_limit_bytes=60 * 1024 * 1024),
-        cost_estimate=pl.CostEstimate(
-            flops=13_000_000_000, bytes_accessed=30_000_000, transcendentals=2_000_000
-        ),
-    )(units, earlier, code, w_qkv, w_o, w_head)
-
-
-CB = 768
-ORDER = (0, 2, 1, 3)
-
-
-def tail_kernel(
-    ynorm_in,
-    packed_in,
-    stream_in,
-    dstream_in,
-    hidden_in,
-    gain_in,
-    wqkv_in,
-    win_in,
-    wout_in,
-    d_attn_ref,
-    d_wqkv_ref,
-    ynorm,
-    d_packed,
-    stream,
-    d_stream,
-    hidden,
-    gain,
-    wqkv,
-    win,
-    wout,
-    dy,
     d_units,
     d_normed,
-    d_hidden,
     d_other,
     g_parts,
     core_sum,
@@ -702,28 +496,17 @@
         return device_at(x, y, core, step_of(z, by))
 
     loads = []
-    pairs = (
-        (ynorm_in, ynorm),
-        (packed_in, d_packed),
-        (wqkv_in, wqkv),
-        (stream_in, stream),
-        (dstream_in, d_stream),
-        (win_in, win),
-        (hidden_in, hidden),
-        (gain_in, gain),
-        (wout_in, wout),
-    )
-    for i, (source, target) in enumerate(pairs):
-        load = pltpu.make_async_copy(source, target, load_sem.at[i])
-        load.start()
-        loads.append(load)
-    greet([other_core] + [at(by) for at in (x_at, y_at, z_at) for by in (1, 2, 3)])
-
-    count = [0]
+
+    def load(source, target):
+        copy = pltpu.make_async_copy(source, target, load_sem.at[len(loads)])
+        copy.start()
+        loads.append(copy)
+        return copy
+
+    sends = []
 
     def send(source, target, device):
-        i = count[0]
-        count[0] += 1
+        i = len(sends)
         copy = pltpu.make_async_remote_copy(
             src_ref=source,
             dst_ref=target,
@@ -733,10 +516,189 @@
             device_id_type=MESH,
         )
         copy.start()
+        sends.append(copy)
         return copy
 
-    loads[0].wait()
-    loads[1].wait()
+    load_wqkv = load(wqkv_in, wqkv)
+    load_hidden = load(hidden_in, wide.at[z])
+    load_wo = load(wo_in, wo)
+    load_whead = load(whead_in, whead)
+    load_win = load(win_in, win)
+
+    frame_of = lax.broadcasted_iota(jnp.int32, (GROUP, 16), 0) // STEPS
+    spread = (frame_of == lax.broadcasted_iota(jnp.int32, (GROUP, 16), 1)).astype(jnp.bfloat16)
+
+    def enter(n, carry):
+        rows = pl.ds(pl.multiple_of(n * GROUP, GROUP), GROUP)
+        s = product(spread, units_ref[pl.ds(pl.multiple_of(n * 16, 16), 16), :])
+        s = s + earlier_ref[rows, :].astype(jnp.float32)
+        r = lax.rsqrt(jnp.mean(s * s, axis=-1, keepdims=True) + eps)
+        stream[rows, :] = s
+        ynorm[rows, :] = (s * r).astype(jnp.bfloat16)
+        return carry
+
+    lax.fori_loop(0, 4, enter, 0)
+    greet([other_core] + [at(by) for at in (x_at, y_at, z_at) for by in (1, 2, 3)])
+    load_hidden.wait()
+    wide_right = send(wide.at[z], wide.at[z], z_at(1))
+    wide_left = send(wide.at[z], wide.at[z], z_at(-1))
+    load_wqkv.wait()
+
+    def project(n, carry):
+        columns = pl.ds(pl.multiple_of(n * 1024, 1024), 1024)
+        packed[:, columns] = product(ynorm[...], wqkv[:, columns]).astype(jnp.bfloat16)
+        return carry
+
+    lax.fori_loop(0, 3, project, 0)
+
+    low = lower_lanes()
+    scale = 1.0 / math.sqrt(DHS)
+
+    def seen(shape, queries):
+        at_query = lax.broadcasted_iota(jnp.int32, shape, queries) % GROUP
+        at_key = lax.broadcasted_iota(jnp.int32, shape, 1 - queries) % GROUP
+        return jnp.logical_and(at_query // STEPS == at_key // STEPS, at_key <= at_query)
+
+    def parts_of(rows, pair):
+        at = pair * 128
+        q = packed[rows, at : at + 128]
+        k = split_heads(packed[rows, 1024 + at : 1024 + at + 128], low)
+        v = split_heads(packed[rows, 2048 + at : 2048 + at + 128], low)
+        return q, k, v
+
+    def mix(n, carry):
+        rows = pl.ds(pl.multiple_of(n * GROUP, GROUP), GROUP)
+        allowed = seen((GROUP, 2 * GROUP), 0)
+        for first in (0, 4):
+            pairs = range(first, first + 4)
+            held = [parts_of(rows, pair) for pair in pairs]
+            scores = [rows_dot(q, k) for q, k, v in held]
+            scores = [jnp.exp(jnp.where(allowed, s * scale, -1e30)) for s in scores]
+            scores = [(s / head_sums(s, 1)).astype(jnp.bfloat16) for s in scores]
+            outs = [product(a, v) for a, (q, k, v) in zip(scores, held)]
+            for pair, a, out in zip(pairs, scores, outs):
+                weights[pair, rows, :] = a
+                mixed[rows, pair * 128 : pair * 128 + 128] = out.astype(jnp.bfloat16)
+        return carry
+
+    lax.fori_loop(0, 4, mix, 0)
+    wide_right.wait_recv()
+    before, beyond = step_of(z, -1), step_of(z, 1)
+    top_rows, end_rows = pl.ds(0, 32), pl.ds(32, 32)
+    wide_on_right = send(wide.at[before, top_rows], wide.at[before, top_rows], z_at(1))
+    wide_left.wait_recv()
+    wide_on_left = send(wide.at[beyond, end_rows], wide.at[beyond, end_rows], z_at(-1))
+    load_wo.wait()
+
+    def add_mixed(n, carry):
+        columns = pl.ds(pl.multiple_of(n * 512, 512), 512)
+        after[:, columns] = stream[:, columns] + product(mixed[...], wo[:, columns])
+        return carry
+
+    lax.fori_loop(0, 2, add_mixed, 0)
+
+    def norm2(n, carry):
+        rows = pl.ds(pl.multiple_of(n * 64, 64), 64)
+        s = after[rows, :]
+        r = lax.rsqrt(jnp.mean(s * s, axis=-1, keepdims=True) + eps)
+        ynorm2[rows, :] = (s * r).astype(jnp.bfloat16)
+        return carry
+
+    lax.fori_loop(0, 8, norm2, 0)
+    load_whead.wait()
+
+    def grow(n, total):
+        columns = pl.ds(pl.multiple_of(n * 512, 512), 512)
+        e = jnp.exp(product(ynorm2[...], whead[:, columns]))
+        grown[:, columns] = e.astype(jnp.bfloat16)
+        return total + jnp.sum(e, axis=-1, keepdims=True)
+
+    total = lax.fori_loop(0, 4, grow, jnp.zeros((512, 1), jnp.float32))
+    inverse = 1.0 / total
+    code = code_ref[...]
+
+    def from_loss(n, carry):
+        columns = pl.ds(pl.multiple_of(n * 256, 256), 256)
+        entry = lax.broadcasted_iota(jnp.int32, (512, 256), 1) + n * 256
+        grown[:, columns] = (
+            grown[:, columns].astype(jnp.float32) * inverse - (entry == code).astype(jnp.float32)
+        ).astype(jnp.bfloat16)
+        return carry
+
+    lax.fori_loop(0, 8, from_loss, 0)
+
+    def to_ynorm2(n, carry):
+        columns = pl.ds(pl.multiple_of(n * 512, 512), 512)
+        ynorm2[:, columns] = rows_dot(grown[...], whead[columns, :]).astype(jnp.bfloat16)
+        return carry
+
+    lax.fori_loop(0, 2, to_ynorm2, 0)
+    load_wout = [
+        load(
+            wout_in.at[up, :, pl.ds(part * 2048, 2048)],
+            whead.at[pl.ds((up * 2 + part) * 256, 256)],
+        )
+        for up in range(2)
+        for part in range(2)
+    ]
+
+    def to_after(n, carry):
+        rows = pl.ds(pl.multiple_of(n * 64, 64), 64)
+        s = after[rows, :]
+        d = ynorm2[rows, :].astype(jnp.float32)
+        r = lax.rsqrt(jnp.mean(s * s, axis=-1, keepdims=True) + eps)
+        dot = jnp.sum(d * s, axis=-1, keepdims=True)
+        da = r * d - s * (r * r * r * dot / 1024)
+        after[rows, :] = da
+        ynorm2[rows, :] = da.astype(jnp.bfloat16)
+        return carry
+
+    lax.fori_loop(0, 8, to_after, 0)
+
+    def to_mixed(n, carry):
+        columns = pl.ds(pl.multiple_of(n * 512, 512), 512)
+        mixed[:, columns] = rows_dot(ynorm2[...], wo[columns, :]).astype(jnp.bfloat16)
+        return carry
+
+    lax.fori_loop(0, 2, to_mixed, 0)
+
+    def unmix(n, carry):
+        rows = pl.ds(pl.multiple_of(n * GROUP, GROUP), GROUP)
+        allowed = seen((2 * GROUP, GROUP), 1)
+        for first in (0, 4):
+            pairs = range(first, first + 4)
+            held = [parts_of(rows, pair) for pair in pairs]
+            outs = [mixed[rows, pair * 128 : pair * 128 + 128] for pair in pairs]
+            kept = [weights[pair, rows, :].astype(jnp.float32) for pair in pairs]
+            turned = [rows_dot(k, q) for q, k, v in held]
+            d_kept = [rows_dot(d, v) for d, (q, k, v) in zip(outs, held)]
+            d_turned = [rows_dot(v, d) for d, (q, k, v) in zip(outs, held)]
+            turned = [jnp.exp(jnp.where(allowed, s * scale, -1e30)) for s in turned]
+            turned = [s / head_sums(s, 0) for s in turned]
+            d_kept = [a * d for a, d in zip(kept, d_kept)]
+            d_kept = [
+                ((d - a * head_sums(d, 1)) * scale).astype(jnp.bfloat16)
+                for a, d in zip(kept, d_kept)
+            ]
+            d_turned = [a * d for a, d in zip(turned, d_turned)]
+            d_turned = [
+                ((d - a * head_sums(d, 0)) * scale).astype(jnp.bfloat16)
+                for a, d in zip(turned, d_turned)
+            ]
+            d_q = [product(d, k) for d, (q, k, v) in zip(d_kept, held)]
+            d_k = [product(d, q) for d, (q, k, v) in zip(d_turned, held)]
+            d_v = [product(a.astype(jnp.bfloat16), d) for a, d in zip(turned, outs)]
+            for pair, dq, dk, dv in zip(pairs, d_q, d_k, d_v):
+                at = pair * 128
+                packed[rows, at : at + 128] = dq.astype(jnp.bfloat16)
+                packed[rows, 1024 + at : 1024 + at + 128] = join_heads(dk, low).astype(jnp.bfloat16)
+                packed[rows, 2048 + at : 2048 + at + 128] = join_heads(dv, low).astype(jnp.bfloat16)
+        return carry
+
+    lax.fori_loop(0, 4, unmix, 0)
+
+    for n in range(4):
+        ynorm_t[n * 256 : (n + 1) * 256, :] = ynorm[:, n * 256 : (n + 1) * 256].T
 
     core_sends = {}
     far = {}
@@ -764,67 +726,42 @@
     for i, cb in enumerate(ORDER):
 
         def block(xi, carry, cb=cb):
-            left = ynorm[:, pl.ds(pl.multiple_of(xi * 256, 256), 256)]
-            product = columns_dot(left, d_packed[:, cb * CB : (cb + 1) * CB])
-            product = product.astype(jnp.bfloat16)
+            rows = pl.ds(pl.multiple_of(xi * 256, 256), 256)
+            term = product(ynorm_t[rows, :], packed[:, cb * CB : (cb + 1) * CB])
+            term = term.astype(jnp.bfloat16)
             for ylo in range(2):
                 for c in range(2):
                     for yhi in range(2):
                         at = ylo * 128 + c * 64 + yhi * 32
-                        g_parts[c, cb, xi, yhi * 2 + ylo] = product[at : at + 32]
+                        g_parts[c, cb, xi, yhi * 2 + ylo] = term[at : at + 32]
             return carry
 
         lax.fori_loop(0, 4, block, 0)
         core_sends[cb] = send(g_parts.at[1 - core, cb], core_sum.at[cb], other_core)
         if i > 0:
             first_phase(ORDER[i - 1])
-    loads[2].wait()
-
-    def dy_block(n, carry):
-        columns = pl.ds(pl.multiple_of(n * 256, 256), 256)
-        dy[:, columns] = rows_dot(d_packed[...], wqkv[columns, :]).astype(jnp.bfloat16)
-        return carry
-
-    lax.fori_loop(0, 4, dy_block, 0)
-    first_phase(ORDER[3])
-    loads[3].wait()
-    loads[4].wait()
+
+    for n in range(2):
+        columns = pl.ds(n * 512, 512)
+        mixed[:, columns] = rows_dot(packed[...], wqkv[columns, :]).astype(jnp.bfloat16)
+        if n == 0:
+            first_phase(ORDER[3])
 
     def units_block(n, carry):
-        rows = pl.ds(pl.multiple_of(n * 64, 64), 64)
+        rows = pl.ds(pl.multiple_of(n * 128, 128), 128)
         s = stream[rows, :]
-        d = dy[rows, :].astype(jnp.float32)
+        d = mixed[rows, :].astype(jnp.float32)
         r = lax.rsqrt(jnp.mean(s * s, axis=-1, keepdims=True) + eps)
         dot = jnp.sum(d * s, axis=-1, keepdims=True)
-        ds = d_stream[rows, :] + r * d - s * (r * r * r * dot / 1024)
-        d_units[pl.ds(pl.multiple_of(n * 8, 8), 8), :] = jnp.sum(ds.reshape(8, 8, 1024), axis=1)
-        return carry
-
-    lax.fori_loop(0, 8, units_block, 0)
-    loads[5].wait()
-
-    def normed_block(n, carry):
-        columns = pl.ds(pl.multiple_of(n * 512, 512), 512)
-        d_normed[:, columns] = rows_dot(d_units[...].astype(jnp.bfloat16), win[columns, :]).astype(
-            jnp.bfloat16
-        )
-        return carry
-
-    lax.fori_loop(0, 8, normed_block, 0)
-    loads[6].wait()
-    loads[7].wait()
-    for n in range(2):
-        rows = pl.ds(n * 32, 32)
-        h = hidden[rows, :]
-        rscale = lax.rsqrt(jnp.mean(h * h, axis=-1, keepdims=True) + eps)
-        grad_gain = d_normed[rows, :].astype(jnp.float32) * gain[...]
-        dot_rows = jnp.sum(grad_gain * h, axis=-1, keepdims=True)
-        d_hidden[z, rows, :] = (
-            rscale * grad_gain - h * (rscale * rscale * rscale * dot_rows / D)
+        ds = after[rows, :] + r * d - s * (r * r * r * dot / 1024)
+        d_units[z, pl.ds(pl.multiple_of(n * 16, 16), 16), :] = jnp.sum(
+            ds.reshape(16, 8, 1024), axis=1
         ).astype(jnp.bfloat16)
-
-    to_right = send(d_hidden.at[z], d_hidden.at[z], z_at(1))
-    to_left = send(d_hidden.at[z], d_hidden.at[z], z_at(-1))
+        return carry
+
+    lax.fori_loop(0, 4, units_block, 0)
+    units_right = send(d_units.at[z], d_units.at[z], z_at(1))
+    units_left = send(d_units.at[z], d_units.at[z], z_at(-1))
 
     second = {}
     last = {}
@@ -838,7 +775,10 @@
         )
         last[cb] = send(mid, first_in.at[cb, 2], at(s))
 
-    loads[8].wait()
+    units_right.wait_recv()
+    units_on_right = send(d_units.at[before, top_rows], d_units.at[before, top_rows], z_at(1))
+    units_left.wait_recv()
+    units_on_left = send(d_units.at[beyond, end_rows], d_units.at[beyond, end_rows], z_at(-1))
 
     for cb in ORDER:
         p, at = axis_of(cb)
@@ -855,14 +795,17 @@
             for by in (1, 2, 3)
         ]
 
-    to_right.wait_recv()
-    on_right = send(
-        d_hidden.at[step_of(z, -1), pl.ds(0, 32)], d_hidden.at[step_of(z, -1), pl.ds(0, 32)], z_at(1)
-    )
-    to_left.wait_recv()
-    on_left = send(
-        d_hidden.at[step_of(z, 1), pl.ds(32, 32)], d_hidden.at[step_of(z, 1), pl.ds(32, 32)], z_at(-1)
-    )
+    units_on_right.wait_recv()
+    units_on_left.wait_recv()
+    load_win.wait()
+    every = d_units[...].reshape(256, 1024)
+
+    def normed_block(n, carry):
+        columns = pl.ds(pl.multiple_of(n * 512, 512), 512)
+        d_normed[:, columns] = rows_dot(every, win[columns, :]).astype(jnp.bfloat16)
+        return carry
+
+    lax.fori_loop(0, 8, normed_block, 0)
 
     for pair in range(2):
         sums = []
@@ -881,51 +824,88 @@
         send(third_out.at[step_of(z, by)], third_in.at[by - 1], z_at(by)) for by in (1, 2, 3)
     ]
 
-    on_right.wait_recv()
-    on_left.wait_recv()
+    wide_on_right.wait_recv()
+    wide_on_left.wait_recv()
+    wide_sends = (wide_right, wide_left, wide_on_right, wide_on_left)
+    for copy in wide_sends:
+        copy.wait_send()
+
+    def hidden_block(n, carry):
+        rows = pl.ds(pl.multiple_of((n % 2) * 32, 32), 32)
+        h = wide[n // 2, rows, :].astype(jnp.float32)
+        rscale = lax.rsqrt(jnp.mean(h * h, axis=-1, keepdims=True) + eps)
+        grad_gain = (
+            d_normed[pl.ds(pl.multiple_of(n * 32, 32), 32), :].astype(jnp.float32) * gain[...]
+        )
+        dot_rows = jnp.sum(grad_gain * h, axis=-1, keepdims=True)
+        wide[n // 2, rows, :] = (
+            rscale * grad_gain - h * (rscale * rscale * rscale * dot_rows / D)
+        ).astype(jnp.bfloat16)
+        return carry
+
+    lax.fori_loop(0, 8, hidden_block, 0)
+    for one in load_wout:
+        one.wait()
     yhi = y // 2
-    full = d_hidden[...].reshape(256, D)
-    d_other[0] = rows_dot(full, wout[1 - yhi]).astype(jnp.bfloat16)
+
+    def attn_of(up):
+        total = jnp.zeros((256, 256), jnp.float32)
+        for part in range(2):
+            rows = pl.ds(pl.multiple_of((up * 2 + part) * 256, 256), 256)
+            total += rows_dot(
+                wide[:, :, part * 2048 : (part + 1) * 2048].reshape(256, 2048), whead[rows, :]
+            )
+        return total.astype(jnp.bfloat16)
+
+    d_other[0] = attn_of(1 - yhi)
     to_other = send(d_other.at[0], d_other.at[1], y_at(2))
-    d_attn_ref[pl.ds(pl.multiple_of(yhi * 256, 256), 256), :] = rows_dot(full, wout[yhi]).astype(
-        jnp.bfloat16
-    )
-
+    d_attn_ref[pl.ds(pl.multiple_of(yhi * 256, 256), 256), :] = attn_of(yhi)
+
+    for one in third:
+        one.wait_recv()
     for pair in range(2):
         total = third_out[z, pair].astype(jnp.float32)
         for by in (1, 2, 3):
-            if pair == 0:
-                third[by - 1].wait_recv()
             total += third_in[by - 1, pair].astype(jnp.float32)
         d_wqkv_ref[:, pair * 2 * CB : (pair * 2 + 1) * CB] = total[:8]
         d_wqkv_ref[:, (pair * 2 + 1) * CB : (pair * 2 + 2) * CB] = total[8:]
 
     to_other.wait_recv()
     d_attn_ref[pl.ds(pl.multiple_of((1 - yhi) * 256, 256), 256), :] = d_other[1]
-    copies = list(core_sends.values()) + list(far.values()) + list(near.values())
-    copies += list(last.values()) + [one for group in second.values() for one in group]
-    copies += third + [to_right, to_left, on_right, on_left, to_other]
-    for copy in copies:
-        copy.wait_send()
-
-
-def tail(ynorm, d_packed, stream, d_stream, hidden, gain, w_qkv, full_in, out_pair):
+    for copy in sends:
+        if not any(copy is one for one in wide_sends):
+            copy.wait_send()
+
+
+def back(units, earlier, code, gain, hidden, w_qkv, w_o, w_head, w_in, w_out):
     bf16, f32 = jnp.bfloat16, jnp.float32
-    operands = (ynorm, d_packed, stream, d_stream, hidden, gain, w_qkv, full_in, out_pair)
+    vmem = pl.BlockSpec(memory_space=pltpu.VMEM)
+    anywhere = pl.BlockSpec(memory_space=pl.ANY)
     return pl.pallas_call(
-        tail_kernel,
+        back_kernel,
         out_shape=(
             jax.ShapeDtypeStruct((512, 256), bf16),
             jax.ShapeDtypeStruct((8, 3072), f32),
         ),
-        in_specs=[pl.BlockSpec(memory_space=pl.ANY)] * 9,
-        out_specs=(pl.BlockSpec(memory_space=pltpu.VMEM),) * 2,
-        scratch_shapes=[pltpu.VMEM(one.shape, one.dtype) for one in operands]
-        + [
+        in_specs=[vmem] * 4 + [anywhere] * 6,
+        out_specs=(vmem,) * 2,
+        scratch_shapes=[
+            pltpu.VMEM((1024, 3072), bf16),
+            pltpu.VMEM((1024, 1024), bf16),
+            pltpu.VMEM((1024, 2048), bf16),
+            pltpu.VMEM((D, 1024), bf16),
+            pltpu.VMEM((4, 64, D), bf16),
             pltpu.VMEM((512, 1024), bf16),
-            pltpu.VMEM((64, 1024), f32),
-            pltpu.VMEM((64, D), bf16),
-            pltpu.VMEM((4, 64, D), bf16),
+            pltpu.VMEM((1024, 512), bf16),
+            pltpu.VMEM((512, 1024), f32),
+            pltpu.VMEM((512, 3072), bf16),
+            pltpu.VMEM((8, 512, 256), bf16),
+            pltpu.VMEM((512, 1024), bf16),
+            pltpu.VMEM((512, 1024), f32),
+            pltpu.VMEM((512, 1024), bf16),
+            pltpu.VMEM((512, 2048), bf16),
+            pltpu.VMEM((4, 64, 1024), bf16),
+            pltpu.VMEM((256, D), bf16),
             pltpu.VMEM((2, 256, 256), bf16),
             pltpu.VMEM((2, 4, 4, 4, 32, CB), bf16),
             pltpu.VMEM((4, 4, 4, 32, CB), bf16),
@@ -935,16 +915,16 @@
             pltpu.VMEM((4, 2, 16, CB), bf16),
             pltpu.VMEM((3, 2, 16, CB), bf16),
             pltpu.SemaphoreType.DMA((9,)),
-            pltpu.SemaphoreType.DMA((40,)),
-            pltpu.SemaphoreType.DMA((40,)),
+            pltpu.SemaphoreType.DMA((48,)),
+            pltpu.SemaphoreType.DMA((48,)),
         ],
         compiler_params=pltpu.CompilerParams(
-            collective_id=1, has_side_effects=True, vmem_limit_bytes=60 * 1024 * 1024
+            collective_id=1, has_side_effects=True, vmem_limit_bytes=62 * 1024 * 1024
         ),
         cost_estimate=pl.CostEstimate(
-            flops=9_000_000_000, bytes_accessed=30_000_000, transcendentals=0
+            flops=22_000_000_000, bytes_accessed=40_000_000, transcendentals=2_000_000
         ),
-    )(*operands)
+    )(units, earlier, code, gain, hidden, w_qkv, w_o, w_head, w_in, w_out)
 
 
 def body(
@@ -968,11 +948,17 @@
     units, earlier, hidden, win, wout = front(
         block_of, q_heads, k_heads, v_heads, resid, gain, w_in, w_out_t, embed, earlier_code
     )
-    ynorm, d_packed, stream, d_stream = depth_step(
-        units, earlier, codes.reshape(-1, 1), w_qkv, w_o, w_head
-    )
-    return tail(
-        ynorm, d_packed, stream, d_stream, hidden, gain, w_qkv, win.reshape(D, -1), wout
+    return back(
+        units,
+        earlier,
+        codes.reshape(-1, 1),
+        gain,
+        hidden,
+        w_qkv,
+        w_o,
+        w_head,
+        win.reshape(D, -1),
+        wout,
     )
 
 

time: 181 us -> 166 us (0.917)
  Pallas kernels: 174 us -> 158 us
    pallas_call x2 -> x1, Pallas kernels: 90.4 us -> 75.3 us  [back(): pl.pallas_call(back_kernel, out_shape=(jax.ShapeDtypeStruct((512, 256), b...]
where the time goes in v3:
time: 166 us; the launch traced here: 165 us
  Pallas kernels  158 us (95%)
  local copies, waits for them, and re-layouts  6.5 us (4%)
    pallas_call x1, Pallas kernels, front(): pl.pallas_call(front_kernel, out_shape=tuple((jax.ShapeDtypeStruct(*one)...  83 us
    pallas_call x1, Pallas kernels, back(): pl.pallas_call(back_kernel, out_shape=(jax.ShapeDtypeStruct((512, 256), b...  75.3 us
    unnamed x4, local copies, waits for them, and re-layouts  4.76 us

profile of v3, /device:TPU:0, one launch (start us, length us, event | category | flops | bytes accessed | tf_op | source)
XLA Modules:
  0.0 165.5 jit_solution(615001461095701836)
XLA Ops:
  0.6 0.8 copy.21
  1.4 0.1 concatenate.3.clone
  1.5 0.8 copy.19
  2.3 0.8 reshape.21.code_ref
  3.1 0.8 reshape.20.earlier_code
  3.9 83.0 %shard_map.140 = (bf16[64,1024]{1,0:T(8,128)(2,1)}, bf16[512,1024]{1,0:T(8,128)(2,1)}, bf16[64,4096]{1,0:T(8,128)(2,1)}, bf16[8,2,256,1024]{3,2,1,0:T(8,128)(2,1)}, bf16[2,256,4096]{2,1,0:T(8,128)(2,1)}) custom-call(s32[32]{0:T(128)} %block_of.1, bf16[512,256]{1,0:T(8,128)(2,1)} %q_in.1, bf16[512,256]{1,0:T(8,128)(2,1)} %k_in.1, bf16[512,256]{1,0:T(8,128)(2,1)} %v_in.1, ...), custom_call_target="tpu_custom_call" | custom-call | flops 8999999488 | bytes 40000000 | tf_op jit(solution)/shard_map/pallas_call | solution.py:377
  86.9 75.3 %shard_map.141 = (bf16[512,256]{1,0:T(8,128)(2,1)}, f32[8,3072]{1,0:T(8,128)}) custom-call(bf16[64,1024]{1,0:T(8,128)(2,1)} %get-tuple-element.7.units_ref, bf16[512,1024]{1,0:T(8,128)(2,1)} %get-tuple-element.8.earlier_ref, s32[512,1]{1,0:T(8,128)} %reshape.21.code_ref, f32[1,4096]{1,0:T(1,128)} %bitcast.5, bf16[64,4096]{1,0:T(8,128)(2,1)} %get-tuple-element.9.hidden_in, ...), custom_call_target="tpu_custom_call" | custom-call | flops 22000001024 | bytes 40000000 | tf_op jit(solution)/shard_map/pallas_call | solution.py:884
  162.3 1.7 %copy.24 = bf16[512,256]{1,0:T(8,128)(2,1)} copy(bf16[512,256]{1,0:T(8,128)(2,1)} %get-tuple-element.14) | data formatting | bytes 524288
  163.9 1.5 copy.25

commit v4 on v3

--- a/solution.py
+++ b/solution.py
@@ -41,6 +41,18 @@
 
 def rows_dot(a, b):
     return lax.dot_general(a, b, (((1,), (1,)), ((), ())), preferred_element_type=jnp.float32)
+
+
+def code_column(codes_ref, back_by):
+    frame = lax.broadcasted_iota(jnp.int32, (512, 64), 0) // 8
+    spread = (frame == lax.broadcasted_iota(jnp.int32, (512, 64), 1)).astype(jnp.bfloat16)
+    codes = codes_ref[...]
+    high = rows_dot(spread, (codes // 128).astype(jnp.float32).astype(jnp.bfloat16))
+    low = rows_dot(spread, (codes % 128).astype(jnp.float32).astype(jnp.bfloat16))
+    step = lax.broadcasted_iota(jnp.int32, (512, 8), 0) % 8 - back_by
+    chosen = step == lax.broadcasted_iota(jnp.int32, (512, 8), 1)
+    column = jnp.sum(jnp.where(chosen, high * 128 + low, 0.0), axis=1, keepdims=True)
+    return jnp.where(step[:, :1] < 0, -1, column.astype(jnp.int32))
 
 
 def front_kernel(
@@ -53,13 +65,14 @@
     win_in,
     wout_in,
     embed_in,
-    earlier_code,
+    codes_ref,
     units_ref,
     earlier_ref,
     hidden_ref,
     win_out,
     wout_out,
     kv,
+    other_head,
     queries,
     top,
     total,
@@ -72,8 +85,8 @@
     resid,
     partial,
     partial_in,
-    hidden,
-    normed,
+    entered,
+    earlier_code,
     load_sem,
     send_sem,
     recv_sem,
@@ -127,11 +140,17 @@
     load_k = load(k_in.at[:, lanes(core)], kv.at[0, x, ylo, half(core)])
     load_v = load(v_in.at[:, lanes(core)], kv.at[1, x, ylo, half(core)])
     load_q = load(q_in.at[:, lanes(core)], queries.at[half(core)])
+    load_other = [
+        load(one.at[:, lanes(1 - core)], other_head.at[i]) for i, one in enumerate((k_in, v_in))
+    ]
     greet(
         [
             other_core,
             x_at(1),
             x_at(-1),
+            device_at(step_of(x, 1), y, 1 - core, z),
+            device_at(step_of(x, -1), y, 1 - core, z),
+            device_at(x, side, 1 - core, z),
             z_at(1),
             z_at(-1),
             device_at(x, side, core, z),
@@ -140,8 +159,20 @@
             device_at(x, step_of(y, 2), 1 - core, z),
         ]
     )
-    swap_k = send(k_in.at[:, lanes(1 - core)], kv.at[0, x, ylo, half(core)], other_core)
-    swap_v = send(v_in.at[:, lanes(1 - core)], kv.at[1, x, ylo, half(core)], other_core)
+    for one in [load_k, load_v] + load_other:
+        one.wait()
+    here = kv.at[:, x, ylo, half(core)]
+    swap_kv = send(other_head, here, other_core)
+
+    def spread(xi, yi):
+        return [
+            send(here, here, device_at(xi, yi, core, z)),
+            send(other_head, here, device_at(xi, yi, 1 - core, z)),
+        ]
+
+    kv_right = spread(step_of(x, 1), y)
+    kv_left = spread(step_of(x, -1), y)
+    kv_side = spread(x, side)
     swap_q = send(q_in.at[:, lanes(1 - core)], queries.at[half(core)], other_core)
 
     shard = win_in.at[pl.ds(pl.multiple_of(core * 256, 256), 256)]
@@ -151,17 +182,10 @@
     load_win = [
         load(win_in.at[pl.ds(i * 256, 256)], win.at[own, i]) for i in range(2)
     ]
+    stores = []
     load_embed = load(embed_in, embed)
     load_wout = load(wout_in, wout.at[yhi])
     load_resid = load(resid_in, resid)
-
-    load_k.wait()
-    load_v.wait()
-    swap_k.wait_recv()
-    swap_v.wait_recv()
-    kv_side = send(kv.at[:, x, ylo], kv.at[:, x, ylo], device_at(x, side, core, z))
-    kv_right = send(kv.at[:, x, ylo], kv.at[:, x, ylo], x_at(1))
-    kv_left = send(kv.at[:, x, ylo], kv.at[:, x, ylo], x_at(-1))
 
     top[...] = jnp.full_like(top, -1e29)
     total[...] = jnp.zeros_like(total)
@@ -178,29 +202,40 @@
         )
         key_pos = lane % 256 + block * 256
 
+        values = jnp.concatenate([kv[1, xi, yi], jnp.ones((1024, HS), jnp.bfloat16)], axis=1)
+
         def rows_of(n, carry):
-            rows = pl.ds(pl.multiple_of(n * 256, 256), 256)
-            pos = lax.broadcasted_iota(jnp.int32, (256, 1), 0) + block_of[x * 8 + ylo * 4 + n] * 256
-            scores = rows_dot(queries[rows, :], kv[0, xi, yi])
-            scores = jnp.where(pos >= key_pos, scores, -1e30)
-            before = top[rows, :]
-            now = jnp.maximum(before, jnp.max(scores, axis=-1, keepdims=True))
-            weights = jnp.exp2((scores - now[:, :1]) * factor)
-            fade = jnp.exp2((before - now) * factor)
-            top[rows, :] = now
-            total[rows, :] = total[rows, :] * fade + jnp.sum(weights, axis=-1, keepdims=True)
-            mixed[rows, :] = mixed[rows, :] * fade + jnp.dot(
-                weights.astype(jnp.bfloat16), kv[1, xi, yi], preferred_element_type=jnp.float32
-            )
+            parts = [pl.ds(pl.multiple_of(n * 512 + i * 256, 256), 256) for i in range(2)]
+            start = lax.broadcasted_iota(jnp.int32, (256, 1), 0)
+            pos = [start + block_of[x * 8 + ylo * 4 + 2 * n + i] * 256 for i in range(2)]
+            scores = [rows_dot(queries[rows, :], kv[0, xi, yi]) for rows in parts]
+            scores = [jnp.where(p >= key_pos, s, -1e30) for p, s in zip(pos, scores)]
+            before = [top[rows, :] for rows in parts]
+            now = [
+                jnp.maximum(b, jnp.max(s, axis=-1, keepdims=True)) for b, s in zip(before, scores)
+            ]
+            weights = [
+                jnp.exp2((s - m[:, :1]) * factor).astype(jnp.bfloat16) for s, m in zip(scores, now)
+            ]
+            sums = [
+                jnp.dot(w, values, preferred_element_type=jnp.float32) for w in weights
+            ]
+            for rows, b, m, s in zip(parts, before, now, sums):
+                fade = jnp.exp2((b - m) * factor)
+                top[rows, :] = m
+                total[rows, :] = total[rows, :] * fade + s[:, HS:]
+                mixed[rows, :] = mixed[rows, :] * fade + s[:, :HS]
             return carry
 
-        lax.fori_loop(0, 4, rows_of, 0)
+        lax.fori_loop(0, 2, rows_of, 0)
 
     load_q.wait()
     swap_q.wait_recv()
+    swap_kv.wait_recv()
     attend(x, ylo)
 
     load_embed.wait()
+    earlier_code[...] = code_column(codes_ref, 1)
 
     def look_up(n, carry):
         rows = pl.ds(pl.multiple_of(n * 128, 128), 128)
@@ -214,23 +249,37 @@
     lax.fori_loop(0, 4, look_up, 0)
 
     def pass_on(ref, left_arrived, right_arrived, at, before, after, first, second):
-        left_arrived.wait_recv()
+        for one in left_arrived:
+            one.wait_recv()
         on_right = send(ref(before, first), ref(before, first), at(1))
-        right_arrived.wait_recv()
+        for one in right_arrived:
+            one.wait_recv()
         on_left = send(ref(after, second), ref(after, second), at(-1))
         return on_right, on_left
 
+    def keep(d, c):
+        stores.append(load(win.at[d, c], win_out.at[d, c]))
+
     def kv_of(yi):
         return lambda xi, part: kv.at[:, xi, yi, part]
 
     def win_of(up):
         return lambda zi, part: win.at[up * 4 + zi, core, part]
 
-    kv_side.wait_recv()
+    for one in load_win:
+        one.wait()
+    keep(own, 0)
+    keep(own, 1)
+    load_wout.wait()
+    stores.append(load(wout.at[yhi], wout_out.at[yhi]))
+    for one in kv_side:
+        one.wait_recv()
     side_lo = 1 - ylo
-    side_right = send(kv.at[:, x, side_lo], kv.at[:, x, side_lo], x_at(1))
-    side_left = send(kv.at[:, x, side_lo], kv.at[:, x, side_lo], x_at(-1))
+    first_half, second_half = pl.ds(0, 512), pl.ds(512, 512)
+    side_right = send(kv.at[:, x, side_lo, first_half], kv.at[:, x, side_lo, first_half], x_at(1))
+    side_left = send(kv.at[:, x, side_lo, second_half], kv.at[:, x, side_lo, second_half], x_at(-1))
     win_cross.wait_recv()
+    keep(crossed, core)
     cross_right = send(win.at[crossed, core], win.at[crossed, core], z_at(1))
     cross_left = send(win.at[crossed, core], win.at[crossed, core], z_at(-1))
     wout_half = pl.ds(pl.multiple_of(core * 128, 128), 128)
@@ -243,28 +292,38 @@
     before_x, after_x = step_of(x, -1), step_of(x, 1)
     before_z, after_z = step_of(z, -1), step_of(z, 1)
     win_on = pass_on(
-        win_of(yhi), win_right, win_left, z_at, before_z, after_z, pl.ds(0, 128), pl.ds(128, 128)
+        win_of(yhi), [win_right], [win_left], z_at, before_z, after_z, pl.ds(0, 128), pl.ds(128, 128)
     )
     kv_on = pass_on(
-        kv_of(ylo), kv_right, kv_left, x_at, before_x, after_x, pl.ds(0, 512), pl.ds(512, 512)
+        kv_of(ylo), kv_right, kv_left, x_at, before_x, after_x, first_half, second_half
     )
+    beside = device_at(x, side, core, z)
+    kv_across = [
+        send(kv.at[:, xi, ylo, part], kv.at[:, xi, ylo, part], beside)
+        for xi, part in ((before_x, second_half), (after_x, first_half))
+    ]
     for zi in (before_z, after_z):
         to_core.append(send(win.at[yhi * 4 + zi, core], win.at[yhi * 4 + zi, core], other_core))
+        keep(yhi * 4 + zi, core)
     attend(before_x, ylo)
     attend(after_x, ylo)
     side_on = pass_on(
-        kv_of(side_lo), side_right, side_left, x_at, before_x, after_x, pl.ds(0, 512), pl.ds(512, 512)
+        kv_of(side_lo), [side_right], [side_left], x_at, before_x, after_x, first_half, second_half
     )
     cross_on = pass_on(
-        win_of(1 - yhi), cross_right, cross_left, z_at, before_z, after_z, pl.ds(0, 128), pl.ds(128, 128)
+        win_of(1 - yhi), [cross_right], [cross_left], z_at, before_z, after_z, pl.ds(0, 128), pl.ds(128, 128)
     )
     for zi in (before_z, after_z):
         at = (1 - yhi) * 4 + zi
         to_core.append(send(win.at[at, core], win.at[at, core], other_core))
+        keep(at, core)
+    for one in kv_across:
+        one.wait_recv()
     attend(before_x, side_lo)
     attend(after_x, side_lo)
     wout_cross.wait_recv()
     wout_core = send(wout.at[1 - yhi, wout_half], wout.at[1 - yhi, wout_half], other_core)
+    stores.append(load(wout.at[1 - yhi, wout_half], wout_out.at[1 - yhi, wout_half]))
     for one in kv_on:
         one.wait_recv()
     attend(step_of(x, 2), ylo)
@@ -272,6 +331,7 @@
         one.wait_recv()
     at = yhi * 4 + step_of(z, 2)
     to_core.append(send(win.at[at, core], win.at[at, core], other_core))
+    keep(at, core)
     for one in side_on:
         one.wait_recv()
     attend(step_of(x, 2), side_lo)
@@ -297,9 +357,10 @@
         one.wait_recv()
     at = (1 - yhi) * 4 + step_of(z, 2)
     to_core.append(send(win.at[at, core], win.at[at, core], other_core))
-    load_wout.wait()
+    keep(at, core)
     wout_core.wait_recv()
-    store_wout = load(wout, wout_out)
+    rest = pl.ds(pl.multiple_of((1 - core) * 128, 128), 128)
+    stores.append(load(wout.at[1 - yhi, rest], wout_out.at[1 - yhi, rest]))
     for one in swaps:
         one.wait_recv()
 
@@ -316,6 +377,12 @@
         partial[cb] = sums.astype(jnp.bfloat16).reshape(4, 64, 1024)
         far[cb] = send(partial.at[cb, step_of(z, 2)], partial_in.at[cb, 0], z_at(s))
         near[cb] = send(partial.at[cb, step_of(z, -s)], partial_in.at[cb, 1], z_at(-s))
+    arrived = [crossed]
+    arrived += [up * 4 + zi for up in (yhi, 1 - yhi) for zi in (before_z, after_z)]
+    arrived += [up * 4 + step_of(z, 2) for up in (yhi, 1 - yhi)]
+    for one, d in zip(to_core, arrived):
+        one.wait_recv()
+        keep(d, 1 - core)
     for cb in range(4):
         s = 1 if cb % 2 == 0 else -1
         far[cb].wait_recv()
@@ -332,38 +399,26 @@
         last[cb].wait_recv()
         h = partial[cb, z].astype(jnp.float32) + resid[:, columns].astype(jnp.float32)
         h = h + partial_in[cb, 1].astype(jnp.float32) + partial_in[cb, 2].astype(jnp.float32)
-        hidden[:, columns] = h
         hidden_ref[:, columns] = h.astype(jnp.bfloat16)
         squares += jnp.sum(h * h, axis=-1, keepdims=True)
+        gained = (h * gain_ref[:, columns]).astype(jnp.bfloat16)
+        for n in range(2):
+            some = pl.ds(n * 512, 512)
+            term = jnp.dot(
+                gained,
+                win[2 * cb : 2 * cb + 2, :, :, some].reshape(1024, 512),
+                preferred_element_type=jnp.float32,
+            )
+            entered[:, some] = term if cb == 0 else entered[:, some] + term
     rscale = lax.rsqrt(squares / D + eps)
-    for cb in range(4):
-        columns = pl.ds(cb * 1024, 1024)
-        normed[:, columns] = (hidden[:, columns] * rscale * gain_ref[:, columns]).astype(
-            jnp.bfloat16
-        )
-    for one in load_win:
+    units_ref[...] = (entered[...] * rscale).astype(jnp.bfloat16)
+    for one in stores:
         one.wait()
-    for one in to_core:
-        one.wait_recv()
-    store_win = load(win, win_out)
-
-    def enter(n, carry):
-        columns = pl.ds(pl.multiple_of(n * 256, 256), 256)
-        units_ref[:, columns] = jnp.dot(
-            normed[...],
-            win[:, :, :, columns].reshape(D, 256),
-            preferred_element_type=jnp.float32,
-        ).astype(jnp.bfloat16)
-        return carry
-
-    lax.fori_loop(0, 4, enter, 0)
-    store_wout.wait()
-    store_win.wait()
     for one in sends:
         one.wait_send()
 
 
-def front(block_of, q, k, v, resid, gain, w_in, w_out, embed, earlier_code):
+def front(block_of, q, k, v, resid, gain, w_in, w_out, embed, codes):
     bf16, f32 = jnp.bfloat16, jnp.float32
     shapes = (
         ((64, 1024), bf16),
@@ -385,6 +440,7 @@
         out_specs=(vmem, vmem, vmem, anywhere, anywhere),
         scratch_shapes=[
             pltpu.VMEM((2, 4, 2, 1024, HS), bf16),
+            pltpu.VMEM((2, 512, HS), bf16),
             pltpu.VMEM((1024, HS), bf16),
             pltpu.VMEM((1024, HS), f32),
             pltpu.VMEM((1024, HS), f32),
@@ -397,11 +453,11 @@
             pltpu.VMEM((64, D), bf16),
             pltpu.VMEM((4, 4, 64, 1024), bf16),
             pltpu.VMEM((4, 3, 64, 1024), bf16),
-            pltpu.VMEM((64, D), f32),
-            pltpu.VMEM((64, D), bf16),
-            pltpu.SemaphoreType.DMA((12,)),
-            pltpu.SemaphoreType.DMA((48,)),
-            pltpu.SemaphoreType.DMA((48,)),
+            pltpu.VMEM((64, 1024), f32),
+            pltpu.VMEM((512, 1), jnp.int32),
+            pltpu.SemaphoreType.DMA((32,)),
+            pltpu.SemaphoreType.DMA((56,)),
+            pltpu.SemaphoreType.DMA((56,)),
         ],
         compiler_params=pltpu.CompilerParams(
             collective_id=2, has_side_effects=True, vmem_limit_bytes=60 * 1024 * 1024
@@ -409,11 +465,10 @@
         cost_estimate=pl.CostEstimate(
             flops=9_000_000_000, bytes_accessed=40_000_000, transcendentals=8_000_000
         ),
-    )(block_of, q, k, v, resid, gain, w_in, w_out, embed, earlier_code)
+    )(block_of, q, k, v, resid, gain, w_in, w_out, embed, codes)
 
 
 CB = 768
-ORDER = (0, 2, 1, 3)
 STEPS = 8
 GROUP = 128
 
@@ -445,7 +500,7 @@
 def back_kernel(
     units_ref,
     earlier_ref,
-    code_ref,
+    codes_ref,
     gain,
     hidden_in,
     wqkv_in,
@@ -479,6 +534,8 @@
     second_in,
     third_out,
     third_in,
+    sums,
+    code_at,
     load_sem,
     send_sem,
     recv_sem,
@@ -519,11 +576,15 @@
         sends.append(copy)
         return copy
 
-    load_wqkv = load(wqkv_in, wqkv)
     load_hidden = load(hidden_in, wide.at[z])
-    load_wo = load(wo_in, wo)
-    load_whead = load(whead_in, whead)
-    load_win = load(win_in, win)
+    load_wqkv = [
+        load(
+            wqkv_in.at[pl.ds(n * 256, 256), pl.ds(part * 1024, 1024)],
+            wqkv.at[pl.ds(n * 256, 256), pl.ds(part * 1024, 1024)],
+        )
+        for part in range(3)
+        for n in range(4)
+    ]
 
     frame_of = lax.broadcasted_iota(jnp.int32, (GROUP, 16), 0) // STEPS
     spread = (frame_of == lax.broadcasted_iota(jnp.int32, (GROUP, 16), 1)).astype(jnp.bfloat16)
@@ -542,14 +603,17 @@
     load_hidden.wait()
     wide_right = send(wide.at[z], wide.at[z], z_at(1))
     wide_left = send(wide.at[z], wide.at[z], z_at(-1))
-    load_wqkv.wait()
-
-    def project(n, carry):
-        columns = pl.ds(pl.multiple_of(n * 1024, 1024), 1024)
+    code_at[...] = code_column(codes_ref, 0)
+    for n in range(4):
+        ynorm_t[n * 256 : (n + 1) * 256, :] = ynorm[:, n * 256 : (n + 1) * 256].T
+    load_wo = load(wo_in, wo)
+    load_whead = load(whead_in, whead)
+    for n in range(3):
+        columns = pl.ds(n * 1024, 1024)
+        for one in load_wqkv[n * 4 : n * 4 + 4]:
+            one.wait()
         packed[:, columns] = product(ynorm[...], wqkv[:, columns]).astype(jnp.bfloat16)
-        return carry
-
-    lax.fori_loop(0, 3, project, 0)
+    load_win = load(win_in, win)
 
     low = lower_lanes()
     scale = 1.0 / math.sqrt(DHS)
@@ -582,50 +646,55 @@
         return carry
 
     lax.fori_loop(0, 4, mix, 0)
+    load_wo.wait()
+
+    def add_mixed(n, carry):
+        columns = pl.ds(pl.multiple_of(n * 512, 512), 512)
+        after[:, columns] = stream[:, columns] + product(mixed[...], wo[:, columns])
+        return carry
+
+    lax.fori_loop(0, 2, add_mixed, 0)
+
+    def norm2(n, carry):
+        rows = pl.ds(pl.multiple_of(n * 64, 64), 64)
+        s = after[rows, :]
+        r = lax.rsqrt(jnp.mean(s * s, axis=-1, keepdims=True) + eps)
+        ynorm2[rows, :] = (s * r).astype(jnp.bfloat16)
+        return carry
+
+    lax.fori_loop(0, 8, norm2, 0)
+    load_whead.wait()
+
+    def grow(n, carry):
+        columns = pl.ds(pl.multiple_of(n * 512, 512), 512)
+        e = jnp.exp(product(ynorm2[...], whead[:, columns]))
+        grown[:, columns] = e.astype(jnp.bfloat16)
+        sums[...] += e[:, :128] + e[:, 128:256] + e[:, 256:384] + e[:, 384:]
+        return carry
+
+    sums[...] = jnp.zeros_like(sums)
+    lax.fori_loop(0, 4, grow, 0)
+
+    def from_loss(n, carry):
+        rows = pl.ds(pl.multiple_of(n * 64, 64), 64)
+        inverse = 1.0 / jnp.sum(sums[rows, :], axis=-1, keepdims=True)
+        code = code_at[rows, :]
+        for part in range(4):
+            columns = pl.ds(part * 512, 512)
+            entry = lax.broadcasted_iota(jnp.int32, (64, 512), 1) + part * 512
+            scaled = grown[rows, columns].astype(jnp.float32) * inverse
+            grown[rows, columns] = jnp.where(entry == code, scaled - 1.0, scaled).astype(
+                jnp.bfloat16
+            )
+        return carry
+
+    lax.fori_loop(0, 8, from_loss, 0)
     wide_right.wait_recv()
     before, beyond = step_of(z, -1), step_of(z, 1)
     top_rows, end_rows = pl.ds(0, 32), pl.ds(32, 32)
     wide_on_right = send(wide.at[before, top_rows], wide.at[before, top_rows], z_at(1))
     wide_left.wait_recv()
     wide_on_left = send(wide.at[beyond, end_rows], wide.at[beyond, end_rows], z_at(-1))
-    load_wo.wait()
-
-    def add_mixed(n, carry):
-        columns = pl.ds(pl.multiple_of(n * 512, 512), 512)
-        after[:, columns] = stream[:, columns] + product(mixed[...], wo[:, columns])
-        return carry
-
-    lax.fori_loop(0, 2, add_mixed, 0)
-
-    def norm2(n, carry):
-        rows = pl.ds(pl.multiple_of(n * 64, 64), 64)
-        s = after[rows, :]
-        r = lax.rsqrt(jnp.mean(s * s, axis=-1, keepdims=True) + eps)
-        ynorm2[rows, :] = (s * r).astype(jnp.bfloat16)
-        return carry
-
-    lax.fori_loop(0, 8, norm2, 0)
-    load_whead.wait()
-
-    def grow(n, total):
-        columns = pl.ds(pl.multiple_of(n * 512, 512), 512)
-        e = jnp.exp(product(ynorm2[...], whead[:, columns]))
-        grown[:, columns] = e.astype(jnp.bfloat16)
-        return total + jnp.sum(e, axis=-1, keepdims=True)
-
-    total = lax.fori_loop(0, 4, grow, jnp.zeros((512, 1), jnp.float32))
-    inverse = 1.0 / total
-    code = code_ref[...]
-
-    def from_loss(n, carry):
-        columns = pl.ds(pl.multiple_of(n * 256, 256), 256)
-        entry = lax.broadcasted_iota(jnp.int32, (512, 256), 1) + n * 256
-        grown[:, columns] = (
-            grown[:, columns].astype(jnp.float32) * inverse - (entry == code).astype(jnp.float32)
-        ).astype(jnp.bfloat16)
-        return carry
-
-    lax.fori_loop(0, 8, from_loss, 0)
 
     def to_ynorm2(n, carry):
         columns = pl.ds(pl.multiple_of(n * 512, 512), 512)
@@ -697,9 +766,6 @@
 
     lax.fori_loop(0, 4, unmix, 0)
 
-    for n in range(4):
-        ynorm_t[n * 256 : (n + 1) * 256, :] = ynorm[:, n * 256 : (n + 1) * 256].T
-
     core_sends = {}
     far = {}
     near = {}
@@ -723,9 +789,8 @@
         far[cb] = send(chunk(cb, step_of(p, 2)), first_in.at[cb, 0], at(s))
         near[cb] = send(chunk(cb, step_of(p, -s)), first_in.at[cb, 1], at(-s))
 
-    for i, cb in enumerate(ORDER):
-
-        def block(xi, carry, cb=cb):
+    def multiply(cb):
+        def block(xi, carry):
             rows = pl.ds(pl.multiple_of(xi * 256, 256), 256)
             term = product(ynorm_t[rows, :], packed[:, cb * CB : (cb + 1) * CB])
             term = term.astype(jnp.bfloat16)
@@ -738,34 +803,11 @@
 
         lax.fori_loop(0, 4, block, 0)
         core_sends[cb] = send(g_parts.at[1 - core, cb], core_sum.at[cb], other_core)
-        if i > 0:
-            first_phase(ORDER[i - 1])
-
-    for n in range(2):
-        columns = pl.ds(n * 512, 512)
-        mixed[:, columns] = rows_dot(packed[...], wqkv[columns, :]).astype(jnp.bfloat16)
-        if n == 0:
-            first_phase(ORDER[3])
-
-    def units_block(n, carry):
-        rows = pl.ds(pl.multiple_of(n * 128, 128), 128)
-        s = stream[rows, :]
-        d = mixed[rows, :].astype(jnp.float32)
-        r = lax.rsqrt(jnp.mean(s * s, axis=-1, keepdims=True) + eps)
-        dot = jnp.sum(d * s, axis=-1, keepdims=True)
-        ds = after[rows, :] + r * d - s * (r * r * r * dot / 1024)
-        d_units[z, pl.ds(pl.multiple_of(n * 16, 16), 16), :] = jnp.sum(
-            ds.reshape(16, 8, 1024), axis=1
-        ).astype(jnp.bfloat16)
-        return carry
-
-    lax.fori_loop(0, 4, units_block, 0)
-    units_right = send(d_units.at[z], d_units.at[z], z_at(1))
-    units_left = send(d_units.at[z], d_units.at[z], z_at(-1))
 
     second = {}
     last = {}
-    for cb in ORDER:
+
+    def second_phase(cb):
         p, at = axis_of(cb)
         s = sign_of(cb)
         far[cb].wait_recv()
@@ -775,12 +817,7 @@
         )
         last[cb] = send(mid, first_in.at[cb, 2], at(s))
 
-    units_right.wait_recv()
-    units_on_right = send(d_units.at[before, top_rows], d_units.at[before, top_rows], z_at(1))
-    units_left.wait_recv()
-    units_on_left = send(d_units.at[beyond, end_rows], d_units.at[beyond, end_rows], z_at(-1))
-
-    for cb in ORDER:
+    def other_axis(cb):
         p, at = axis_of(cb)
         near[cb].wait_recv()
         last[cb].wait_recv()
@@ -795,6 +832,41 @@
             for by in (1, 2, 3)
         ]
 
+    multiply(0)
+    multiply(2)
+    first_phase(0)
+    multiply(1)
+    first_phase(2)
+    multiply(3)
+    first_phase(1)
+    mixed[:, :512] = rows_dot(packed[...], wqkv[:512, :]).astype(jnp.bfloat16)
+    first_phase(3)
+    mixed[:, 512:] = rows_dot(packed[...], wqkv[512:, :]).astype(jnp.bfloat16)
+
+    def units_block(n, carry):
+        rows = pl.ds(pl.multiple_of(n * 128, 128), 128)
+        s = stream[rows, :]
+        d = mixed[rows, :].astype(jnp.float32)
+        r = lax.rsqrt(jnp.mean(s * s, axis=-1, keepdims=True) + eps)
+        dot = jnp.sum(d * s, axis=-1, keepdims=True)
+        ds = after[rows, :] + r * d - s * (r * r * r * dot / 1024)
+        d_units[z, pl.ds(pl.multiple_of(n * 16, 16), 16), :] = jnp.sum(
+            ds.reshape(16, 8, 1024), axis=1
+        ).astype(jnp.bfloat16)
+        return carry
+
+    lax.fori_loop(0, 4, units_block, 0)
+    units_right = send(d_units.at[z], d_units.at[z], z_at(1))
+    units_left = send(d_units.at[z], d_units.at[z], z_at(-1))
+    for cb in (0, 2, 1, 3):
+        second_phase(cb)
+    units_right.wait_recv()
+    units_on_right = send(d_units.at[before, top_rows], d_units.at[before, top_rows], z_at(1))
+    units_left.wait_recv()
+    units_on_left = send(d_units.at[beyond, end_rows], d_units.at[beyond, end_rows], z_at(-1))
+    other_axis(0)
+    other_axis(2)
+    other_axis(1)
     units_on_right.wait_recv()
     units_on_left.wait_recv()
     load_win.wait()
@@ -805,24 +877,9 @@
         d_normed[:, columns] = rows_dot(every, win[columns, :]).astype(jnp.bfloat16)
         return carry
 
-    lax.fori_loop(0, 8, normed_block, 0)
-
-    for pair in range(2):
-        sums = []
-        for cb in (2 * pair, 2 * pair + 1):
-            q = y if cb < 2 else x
-            total = first_out[cb, q].astype(jnp.float32)
-            for by in (1, 2, 3):
-                second[cb][by - 1].wait_recv()
-                total += second_in[cb, by - 1].astype(jnp.float32)
-            sums.append(total)
-        for zq in range(4):
-            third_out[zq, pair] = jnp.concatenate(
-                [one[zq * 8 : zq * 8 + 8] for one in sums], axis=0
-            ).astype(jnp.bfloat16)
-    third = [
-        send(third_out.at[step_of(z, by)], third_in.at[by - 1], z_at(by)) for by in (1, 2, 3)
-    ]
+    lax.fori_loop(0, 4, normed_block, 0)
+    other_axis(3)
+    lax.fori_loop(4, 8, normed_block, 0)
 
     wide_on_right.wait_recv()
     wide_on_left.wait_recv()
@@ -844,6 +901,22 @@
         return carry
 
     lax.fori_loop(0, 8, hidden_block, 0)
+    for pair in range(2):
+        totals = []
+        for cb in (2 * pair, 2 * pair + 1):
+            q = y if cb < 2 else x
+            total = first_out[cb, q].astype(jnp.float32)
+            for by in (1, 2, 3):
+                second[cb][by - 1].wait_recv()
+                total += second_in[cb, by - 1].astype(jnp.float32)
+            totals.append(total)
+        for zq in range(4):
+            third_out[zq, pair] = jnp.concatenate(
+                [one[zq * 8 : zq * 8 + 8] for one in totals], axis=0
+            ).astype(jnp.bfloat16)
+    third = [
+        send(third_out.at[step_of(z, by)], third_in.at[by - 1], z_at(by)) for by in (1, 2, 3)
+    ]
     for one in load_wout:
         one.wait()
     yhi = y // 2
@@ -861,6 +934,8 @@
     to_other = send(d_other.at[0], d_other.at[1], y_at(2))
     d_attn_ref[pl.ds(pl.multiple_of(yhi * 256, 256), 256), :] = attn_of(yhi)
 
+    to_other.wait_recv()
+    d_attn_ref[pl.ds(pl.multiple_of((1 - yhi) * 256, 256), 256), :] = d_other[1]
     for one in third:
         one.wait_recv()
     for pair in range(2):
@@ -870,14 +945,12 @@
         d_wqkv_ref[:, pair * 2 * CB : (pair * 2 + 1) * CB] = total[:8]
         d_wqkv_ref[:, (pair * 2 + 1) * CB : (pair * 2 + 2) * CB] = total[8:]
 
-    to_other.wait_recv()
-    d_attn_ref[pl.ds(pl.multiple_of((1 - yhi) * 256, 256), 256), :] = d_other[1]
     for copy in sends:
         if not any(copy is one for one in wide_sends):
             copy.wait_send()
 
 
-def back(units, earlier, code, gain, hidden, w_qkv, w_o, w_head, w_in, w_out):
+def back(units, earlier, codes, gain, hidden, w_qkv, w_o, w_head, w_in, w_out):
     bf16, f32 = jnp.bfloat16, jnp.float32
     vmem = pl.BlockSpec(memory_space=pltpu.VMEM)
     anywhere = pl.BlockSpec(memory_space=pl.ANY)
@@ -914,7 +987,9 @@
             pltpu.VMEM((4, 3, 32, CB), bf16),
             pltpu.VMEM((4, 2, 16, CB), bf16),
             pltpu.VMEM((3, 2, 16, CB), bf16),
-            pltpu.SemaphoreType.DMA((9,)),
+            pltpu.VMEM((512, 128), f32),
+            pltpu.VMEM((512, 1), jnp.int32),
+            pltpu.SemaphoreType.DMA((24,)),
             pltpu.SemaphoreType.DMA((48,)),
             pltpu.SemaphoreType.DMA((48,)),
         ],
@@ -924,7 +999,21 @@
         cost_estimate=pl.CostEstimate(
             flops=22_000_000_000, bytes_accessed=40_000_000, transcendentals=2_000_000
         ),
-    )(units, earlier, code, gain, hidden, w_qkv, w_o, w_head, w_in, w_out)
+    )(units, earlier, codes, gain, hidden, w_qkv, w_o, w_head, w_in, w_out)
+
+
+def finish_kernel(attn_in, wqkv_in, attn_out, wqkv_out):
+    attn_out[...] = attn_in[...]
+    wqkv_out[...] = wqkv_in[...]
+
+
+def finish(d_attn, d_wqkv):
+    return pl.pallas_call(
+        finish_kernel,
+        out_shape=tuple(jax.ShapeDtypeStruct(one.shape, one.dtype) for one in (d_attn, d_wqkv)),
+        in_specs=[pl.BlockSpec(memory_space=pltpu.VMEM)] * 2,
+        out_specs=(pl.BlockSpec(memory_space=pltpu.VMEM),) * 2,
+    )(d_attn, d_wqkv)
 
 
 def body(
@@ -943,15 +1032,14 @@
     codes,
 ):
     gain = norm_gain.reshape(1, D)
-    first = jnp.full((codes.shape[0], 1), -1, codes.dtype)
-    earlier_code = jnp.concatenate([first, codes[:, :-1]], axis=1).reshape(-1, 1)
+    codes = codes.T
     units, earlier, hidden, win, wout = front(
-        block_of, q_heads, k_heads, v_heads, resid, gain, w_in, w_out_t, embed, earlier_code
+        block_of, q_heads, k_heads, v_heads, resid, gain, w_in, w_out_t, embed, codes
     )
-    return back(
+    return finish(*back(
         units,
         earlier,
-        codes.reshape(-1, 1),
+        codes,
         gain,
         hidden,
         w_qkv,
@@ -959,7 +1047,7 @@
         w_head,
         win.reshape(D, -1),
         wout,
-    )
+    ))
 
 
 def solution(mesh):

time: 166 us -> 148 us (0.89)
  Pallas kernels: 158 us -> 147 us
  local copies, waits for them, and re-layouts: 6.5 us -> 0 us
    pallas_call x1, Pallas kernels: 75.3 us -> 67.8 us  [back(): pl.pallas_call(back_kernel, out_shape=(jax.ShapeDtypeStruct((512, 256), b...]
    pallas_call x1, Pallas kernels: 83 us -> 77.4 us  [front(): pl.pallas_call(front_kernel, out_shape=tuple((jax.ShapeDtypeStruct(*one)...]
    unnamed x4 -> x0, local copies, waits for them, and re-layouts: 4.76 us -> none
    pallas_call x0 -> x1, Pallas kernels: none -> 1.72 us  [finish(): pl.pallas_call(finish_kernel, out_shape=tuple((jax.ShapeDtypeStruct(one.s...]
    reshape x2 -> x0, local copies, waits for them, and re-layouts: 1.66 us -> none  [the longest x1 0.83 us: body(): codes.reshape(-1, 1)]
where the time goes in v4:
time: 148 us
  Pallas kernels  147 us (99%)
    pallas_call x1, Pallas kernels, front(): pl.pallas_call(front_kernel, out_shape=tuple((jax.ShapeDtypeStruct(*one)...  77.4 us
    pallas_call x1, Pallas kernels, back(): pl.pallas_call(back_kernel, out_shape=(jax.ShapeDtypeStruct((512, 256), b...  67.8 us

profile of v4, /device:TPU:0, one launch (start us, length us, event | category | flops | bytes accessed | tf_op | source)
XLA Modules:
  0.0 147.6 jit_solution(9599855228599095732)
XLA Ops:
  0.6 77.4 %shard_map.140 = (bf16[64,1024]{1,0:T(8,128)(2,1)}, bf16[512,1024]{1,0:T(8,128)(2,1)}, bf16[64,4096]{1,0:T(8,128)(2,1)}, bf16[8,2,256,1024]{3,2,1,0:T(8,128)(2,1)}, bf16[2,256,4096]{2,1,0:T(8,128)(2,1)}) custom-call(s32[32]{0:T(128)} %block_of.1, bf16[512,256]{1,0:T(8,128)(2,1)} %q_in.1, bf16[512,256]{1,0:T(8,128)(2,1)} %k_in.1, bf16[512,256]{1,0:T(8,128)(2,1)} %v_in.1, ...), custom_call_target="tpu_custom_call" | custom-call | flops 8999999488 | bytes 40000000 | tf_op jit(solution)/shard_map/pallas_call | solution.py:432
  78.1 67.8 %shard_map.141 = (bf16[512,256]{1,0:T(8,128)(2,1)}, f32[8,3072]{1,0:T(8,128)}) custom-call(bf16[64,1024]{1,0:T(8,128)(2,1)} %get-tuple-element.9.units_ref, bf16[512,1024]{1,0:T(8,128)(2,1)} %get-tuple-element.10.earlier_ref, s32[8,64]{1,0:T(8,128)} %bitcast.6, f32[1,4096]{1,0:T(1,128)} %bitcast.4, bf16[64,4096]{1,0:T(8,128)(2,1)} %get-tuple-element.11.hidden_in, ...), custom_call_target="tpu_custom_call" | custom-call | flops 22000001024 | bytes 40000000 | tf_op jit(solution)/shard_map/pallas_call | solution.py:957
  145.9 1.7 %shard_map.142 = (bf16[512,256]{1,0:T(8,128)(2,1)}, f32[8,3072]{1,0:T(8,128)}) custom-call(bf16[512,256]{1,0:T(8,128)(2,1)} %get-tuple-element.14.attn_in, f32[8,3072]{1,0:T(8,128)} %get-tuple-element.15.wqkv_in), custom_call_target="tpu_custom_call" | custom-call | tf_op jit(solution)/shard_map/pallas_call | solution.py:1011

commit v5 on v4

--- a/solution.py
+++ b/solution.py
@@ -272,28 +272,25 @@
     keep(own, 1)
     load_wout.wait()
     stores.append(load(wout.at[yhi], wout_out.at[yhi]))
-    for one in kv_side:
-        one.wait_recv()
-    side_lo = 1 - ylo
-    first_half, second_half = pl.ds(0, 512), pl.ds(512, 512)
-    side_right = send(kv.at[:, x, side_lo, first_half], kv.at[:, x, side_lo, first_half], x_at(1))
-    side_left = send(kv.at[:, x, side_lo, second_half], kv.at[:, x, side_lo, second_half], x_at(-1))
-    win_cross.wait_recv()
-    keep(crossed, core)
-    cross_right = send(win.at[crossed, core], win.at[crossed, core], z_at(1))
-    cross_left = send(win.at[crossed, core], win.at[crossed, core], z_at(-1))
     wout_half = pl.ds(pl.multiple_of(core * 128, 128), 128)
     wout_cross = send(
         wout_in.at[wout_half], wout.at[yhi, wout_half], device_at(x, cross, core, z)
     )
-    to_core = [send(win.at[crossed, core], win.at[crossed, core], other_core)]
-    attend(x, side_lo)
-
-    before_x, after_x = step_of(x, -1), step_of(x, 1)
-    before_z, after_z = step_of(z, -1), step_of(z, 1)
-    win_on = pass_on(
-        win_of(yhi), [win_right], [win_left], z_at, before_z, after_z, pl.ds(0, 128), pl.ds(128, 128)
-    )
+    before_x, after_x, far_x = step_of(x, -1), step_of(x, 1), step_of(x, 2)
+    before_z, after_z, far_z = step_of(z, -1), step_of(z, 1), step_of(z, 2)
+    first_half, second_half = pl.ds(0, 512), pl.ds(512, 512)
+    win_first, win_second = pl.ds(0, 128), pl.ds(128, 128)
+    side_lo = 1 - ylo
+    to_core = []
+
+    def share(d):
+        to_core.append(send(win.at[d, core], win.at[d, core], other_core))
+        keep(d, core)
+
+    for one in kv_side:
+        one.wait_recv()
+    side_right = send(kv.at[:, x, side_lo, first_half], kv.at[:, x, side_lo, first_half], x_at(1))
+    side_left = send(kv.at[:, x, side_lo, second_half], kv.at[:, x, side_lo, second_half], x_at(-1))
     kv_on = pass_on(
         kv_of(ylo), kv_right, kv_left, x_at, before_x, after_x, first_half, second_half
     )
@@ -302,39 +299,39 @@
         send(kv.at[:, xi, ylo, part], kv.at[:, xi, ylo, part], beside)
         for xi, part in ((before_x, second_half), (after_x, first_half))
     ]
-    for zi in (before_z, after_z):
-        to_core.append(send(win.at[yhi * 4 + zi, core], win.at[yhi * 4 + zi, core], other_core))
-        keep(yhi * 4 + zi, core)
+    win_on = pass_on(
+        win_of(yhi), [win_right], [win_left], z_at, before_z, after_z, win_first, win_second
+    )
+    attend(x, side_lo)
+    share(yhi * 4 + before_z)
+    share(yhi * 4 + after_z)
     attend(before_x, ylo)
+    win_cross.wait_recv()
+    cross_right = send(win.at[crossed, core], win.at[crossed, core], z_at(1))
+    cross_left = send(win.at[crossed, core], win.at[crossed, core], z_at(-1))
+    share(crossed)
     attend(after_x, ylo)
     side_on = pass_on(
         kv_of(side_lo), [side_right], [side_left], x_at, before_x, after_x, first_half, second_half
     )
-    cross_on = pass_on(
-        win_of(1 - yhi), [cross_right], [cross_left], z_at, before_z, after_z, pl.ds(0, 128), pl.ds(128, 128)
-    )
-    for zi in (before_z, after_z):
-        at = (1 - yhi) * 4 + zi
-        to_core.append(send(win.at[at, core], win.at[at, core], other_core))
-        keep(at, core)
+    for one in kv_on:
+        one.wait_recv()
+    attend(far_x, ylo)
+    for one in win_on:
+        one.wait_recv()
+    share(yhi * 4 + far_z)
     for one in kv_across:
         one.wait_recv()
     attend(before_x, side_lo)
     attend(after_x, side_lo)
-    wout_cross.wait_recv()
-    wout_core = send(wout.at[1 - yhi, wout_half], wout.at[1 - yhi, wout_half], other_core)
-    stores.append(load(wout.at[1 - yhi, wout_half], wout_out.at[1 - yhi, wout_half]))
-    for one in kv_on:
-        one.wait_recv()
-    attend(step_of(x, 2), ylo)
-    for one in win_on:
-        one.wait_recv()
-    at = yhi * 4 + step_of(z, 2)
-    to_core.append(send(win.at[at, core], win.at[at, core], other_core))
-    keep(at, core)
+    cross_on = pass_on(
+        win_of(1 - yhi), [cross_right], [cross_left], z_at, before_z, after_z, win_first, win_second
+    )
+    share((1 - yhi) * 4 + before_z)
+    share((1 - yhi) * 4 + after_z)
     for one in side_on:
         one.wait_recv()
-    attend(step_of(x, 2), side_lo)
+    attend(far_x, side_lo)
 
     for n in range(4):
         rows = pl.ds(n * 256, 256)
@@ -353,11 +350,9 @@
         ),
     ]
     heads_in[yhi, core] = attn[core, yhi]
-    for one in cross_on:
-        one.wait_recv()
-    at = (1 - yhi) * 4 + step_of(z, 2)
-    to_core.append(send(win.at[at, core], win.at[at, core], other_core))
-    keep(at, core)
+    wout_cross.wait_recv()
+    wout_core = send(wout.at[1 - yhi, wout_half], wout.at[1 - yhi, wout_half], other_core)
+    stores.append(load(wout.at[1 - yhi, wout_half], wout_out.at[1 - yhi, wout_half]))
     wout_core.wait_recv()
     rest = pl.ds(pl.multiple_of((1 - core) * 128, 128), 128)
     stores.append(load(wout.at[1 - yhi, rest], wout_out.at[1 - yhi, rest]))
@@ -377,9 +372,11 @@
         partial[cb] = sums.astype(jnp.bfloat16).reshape(4, 64, 1024)
         far[cb] = send(partial.at[cb, step_of(z, 2)], partial_in.at[cb, 0], z_at(s))
         near[cb] = send(partial.at[cb, step_of(z, -s)], partial_in.at[cb, 1], z_at(-s))
-    arrived = [crossed]
-    arrived += [up * 4 + zi for up in (yhi, 1 - yhi) for zi in (before_z, after_z)]
-    arrived += [up * 4 + step_of(z, 2) for up in (yhi, 1 - yhi)]
+    for one in cross_on:
+        one.wait_recv()
+    share((1 - yhi) * 4 + far_z)
+    arrived = [yhi * 4 + before_z, yhi * 4 + after_z, crossed, yhi * 4 + far_z]
+    arrived += [(1 - yhi) * 4 + zi for zi in (before_z, after_z, far_z)]
     for one, d in zip(to_core, arrived):
         one.wait_recv()
         keep(d, 1 - core)
@@ -901,6 +898,21 @@
         return carry
 
     lax.fori_loop(0, 8, hidden_block, 0)
+    for one in load_wout:
+        one.wait()
+    yhi = y // 2
+
+    def attn_of(up):
+        total = jnp.zeros((256, 256), jnp.float32)
+        for part in range(2):
+            rows = pl.ds(pl.multiple_of((up * 2 + part) * 256, 256), 256)
+            total += rows_dot(
+                wide[:, :, part * 2048 : (part + 1) * 2048].reshape(256, 2048), whead[rows, :]
+            )
+        return total.astype(jnp.bfloat16)
+
+    d_other[0] = attn_of(1 - yhi)
+    to_other = send(d_other.at[0], d_other.at[1], y_at(2))
     for pair in range(2):
         totals = []
         for cb in (2 * pair, 2 * pair + 1):
@@ -917,21 +929,6 @@
     third = [
         send(third_out.at[step_of(z, by)], third_in.at[by - 1], z_at(by)) for by in (1, 2, 3)
     ]
-    for one in load_wout:
-        one.wait()
-    yhi = y // 2
-
-    def attn_of(up):
-        total = jnp.zeros((256, 256), jnp.float32)
-        for part in range(2):
-            rows = pl.ds(pl.multiple_of((up * 2 + part) * 256, 256), 256)
-            total += rows_dot(
-                wide[:, :, part * 2048 : (part + 1) * 2048].reshape(256, 2048), whead[rows, :]
-            )
-        return total.astype(jnp.bfloat16)
-
-    d_other[0] = attn_of(1 - yhi)
-    to_other = send(d_other.at[0], d_other.at[1], y_at(2))
     d_attn_ref[pl.ds(pl.multiple_of(yhi * 256, 256), 256), :] = attn_of(yhi)
 
     to_other.wait_recv()

time: 148 us -> 140 us (0.946)
  Pallas kernels: 147 us -> 140 us
    pallas_call x1, Pallas kernels: 77.4 us -> 71.9 us  [front(): pl.pallas_call(front_kernel, out_shape=tuple((jax.ShapeDtypeStruct(*one)...]
    pallas_call x1, Pallas kernels: 67.8 us -> 66 us  [back(): pl.pallas_call(back_kernel, out_shape=(jax.ShapeDtypeStruct((512, 256), b...]
where the time goes in v5:
time: 140 us
  Pallas kernels  140 us (100%)
    pallas_call x1, Pallas kernels, front(): pl.pallas_call(front_kernel, out_shape=tuple((jax.ShapeDtypeStruct(*one)...  71.9 us
    pallas_call x1, Pallas kernels, back(): pl.pallas_call(back_kernel, out_shape=(jax.ShapeDtypeStruct((512, 256), b...  66 us

profile of v5, /device:TPU:0, one launch (start us, length us, event | category | flops | bytes accessed | tf_op | source)
XLA Modules:
  0.0 140.2 jit_solution(4177609748407227736)
XLA Ops:
  0.6 71.9 %shard_map.140 = (bf16[64,1024]{1,0:T(8,128)(2,1)}, bf16[512,1024]{1,0:T(8,128)(2,1)}, bf16[64,4096]{1,0:T(8,128)(2,1)}, bf16[8,2,256,1024]{3,2,1,0:T(8,128)(2,1)}, bf16[2,256,4096]{2,1,0:T(8,128)(2,1)}) custom-call(s32[32]{0:T(128)} %block_of.1, bf16[512,256]{1,0:T(8,128)(2,1)} %q_in.1, bf16[512,256]{1,0:T(8,128)(2,1)} %k_in.1, bf16[512,256]{1,0:T(8,128)(2,1)} %v_in.1, ...), custom_call_target="tpu_custom_call" | custom-call | flops 8999999488 | bytes 40000000 | tf_op jit(solution)/shard_map/pallas_call | solution.py:429
  72.5 66.0 %shard_map.141 = (bf16[512,256]{1,0:T(8,128)(2,1)}, f32[8,3072]{1,0:T(8,128)}) custom-call(bf16[64,1024]{1,0:T(8,128)(2,1)} %get-tuple-element.9.units_ref, bf16[512,1024]{1,0:T(8,128)(2,1)} %get-tuple-element.10.earlier_ref, s32[8,64]{1,0:T(8,128)} %bitcast.6, f32[1,4096]{1,0:T(1,128)} %bitcast.4, bf16[64,4096]{1,0:T(8,128)(2,1)} %get-tuple-element.11.hidden_in, ...), custom_call_target="tpu_custom_call" | custom-call | flops 22000001024 | bytes 40000000 | tf_op jit(solution)/shard_map/pallas_call | solution.py:954
  138.5 1.7 %shard_map.142 = (bf16[512,256]{1,0:T(8,128)(2,1)}, f32[8,3072]{1,0:T(8,128)}) custom-call(bf16[512,256]{1,0:T(8,128)(2,1)} %get-tuple-element.14.attn_in, f32[8,3072]{1,0:T(8,128)} %get-tuple-element.15.wqkv_in), custom_call_target="tpu_custom_call" | custom-call | tf_op jit(solution)/shard_map/pallas_call | solution.py:1008

commit v6 on v5

--- a/solution.py
+++ b/solution.py
@@ -1,3 +1,4 @@
+import functools
 import math
 
 import jax
@@ -182,7 +183,6 @@
     load_win = [
         load(win_in.at[pl.ds(i * 256, 256)], win.at[own, i]) for i in range(2)
     ]
-    stores = []
     load_embed = load(embed_in, embed)
     load_wout = load(wout_in, wout.at[yhi])
     load_resid = load(resid_in, resid)
@@ -247,6 +247,7 @@
         return carry
 
     lax.fori_loop(0, 4, look_up, 0)
+    stores = []
 
     def pass_on(ref, left_arrived, right_arrived, at, before, after, first, second):
         for one in left_arrived:
@@ -291,9 +292,8 @@
         one.wait_recv()
     side_right = send(kv.at[:, x, side_lo, first_half], kv.at[:, x, side_lo, first_half], x_at(1))
     side_left = send(kv.at[:, x, side_lo, second_half], kv.at[:, x, side_lo, second_half], x_at(-1))
-    kv_on = pass_on(
-        kv_of(ylo), kv_right, kv_left, x_at, before_x, after_x, first_half, second_half
-    )
+    for one in kv_right + kv_left:
+        one.wait_recv()
     beside = device_at(x, side, core, z)
     kv_across = [
         send(kv.at[:, xi, ylo, part], kv.at[:, xi, ylo, part], beside)
@@ -303,6 +303,7 @@
         win_of(yhi), [win_right], [win_left], z_at, before_z, after_z, win_first, win_second
     )
     attend(x, side_lo)
+    kv_on = pass_on(kv_of(ylo), [], [], x_at, before_x, after_x, first_half, second_half)
     share(yhi * 4 + before_z)
     share(yhi * 4 + after_z)
     attend(before_x, ylo)
@@ -524,7 +525,8 @@
     d_units,
     d_normed,
     d_other,
-    g_parts,
+    turned_other,
+    packed_other,
     core_sum,
     first_in,
     first_out,
@@ -602,7 +604,12 @@
     wide_left = send(wide.at[z], wide.at[z], z_at(-1))
     code_at[...] = code_column(codes_ref, 0)
     for n in range(4):
-        ynorm_t[n * 256 : (n + 1) * 256, :] = ynorm[:, n * 256 : (n + 1) * 256].T
+        turned = ynorm[:, n * 256 : (n + 1) * 256].T
+        for ylo in range(2):
+            for c in range(2):
+                at = ylo * 128 + c * 64
+                ynorm_t[c, n * 2 + ylo] = turned[at : at + 64]
+    swap_turned = send(ynorm_t.at[1 - core], turned_other, other_core)
     load_wo = load(wo_in, wo)
     load_whead = load(whead_in, whead)
     for n in range(3):
@@ -620,29 +627,28 @@
         at_key = lax.broadcasted_iota(jnp.int32, shape, 1 - queries) % GROUP
         return jnp.logical_and(at_query // STEPS == at_key // STEPS, at_key <= at_query)
 
+    def lanes_of(pair, which=0):
+        return pl.ds(pl.multiple_of(which * 1024 + pair * 128, 128), 128)
+
     def parts_of(rows, pair):
-        at = pair * 128
-        q = packed[rows, at : at + 128]
-        k = split_heads(packed[rows, 1024 + at : 1024 + at + 128], low)
-        v = split_heads(packed[rows, 2048 + at : 2048 + at + 128], low)
-        return q, k, v
+        q, k, v = (packed[rows, lanes_of(pair, which)] for which in range(3))
+        return q, split_heads(k, low), split_heads(v, low)
 
     def mix(n, carry):
-        rows = pl.ds(pl.multiple_of(n * GROUP, GROUP), GROUP)
+        rows = pl.ds(pl.multiple_of((n // 2) * GROUP, GROUP), GROUP)
         allowed = seen((GROUP, 2 * GROUP), 0)
-        for first in (0, 4):
-            pairs = range(first, first + 4)
-            held = [parts_of(rows, pair) for pair in pairs]
-            scores = [rows_dot(q, k) for q, k, v in held]
-            scores = [jnp.exp(jnp.where(allowed, s * scale, -1e30)) for s in scores]
-            scores = [(s / head_sums(s, 1)).astype(jnp.bfloat16) for s in scores]
-            outs = [product(a, v) for a, (q, k, v) in zip(scores, held)]
-            for pair, a, out in zip(pairs, scores, outs):
-                weights[pair, rows, :] = a
-                mixed[rows, pair * 128 : pair * 128 + 128] = out.astype(jnp.bfloat16)
-        return carry
-
-    lax.fori_loop(0, 4, mix, 0)
+        pairs = [(n % 2) * 4 + i for i in range(4)]
+        held = [parts_of(rows, pair) for pair in pairs]
+        scores = [rows_dot(q, k) for q, k, v in held]
+        scores = [jnp.exp(jnp.where(allowed, s * scale, -1e30)) for s in scores]
+        scores = [(s / head_sums(s, 1)).astype(jnp.bfloat16) for s in scores]
+        outs = [product(a, v) for a, (q, k, v) in zip(scores, held)]
+        for pair, a, out in zip(pairs, scores, outs):
+            weights[pair, rows, :] = a
+            mixed[rows, lanes_of(pair)] = out.astype(jnp.bfloat16)
+        return carry
+
+    lax.fori_loop(0, 8, mix, 0)
     load_wo.wait()
 
     def add_mixed(n, carry):
@@ -728,42 +734,49 @@
 
     lax.fori_loop(0, 2, to_mixed, 0)
 
-    def unmix(n, carry):
+    def unmix(cb, n, carry):
         rows = pl.ds(pl.multiple_of(n * GROUP, GROUP), GROUP)
         allowed = seen((2 * GROUP, GROUP), 1)
-        for first in (0, 4):
-            pairs = range(first, first + 4)
-            held = [parts_of(rows, pair) for pair in pairs]
-            outs = [mixed[rows, pair * 128 : pair * 128 + 128] for pair in pairs]
-            kept = [weights[pair, rows, :].astype(jnp.float32) for pair in pairs]
-            turned = [rows_dot(k, q) for q, k, v in held]
-            d_kept = [rows_dot(d, v) for d, (q, k, v) in zip(outs, held)]
-            d_turned = [rows_dot(v, d) for d, (q, k, v) in zip(outs, held)]
-            turned = [jnp.exp(jnp.where(allowed, s * scale, -1e30)) for s in turned]
-            turned = [s / head_sums(s, 0) for s in turned]
-            d_kept = [a * d for a, d in zip(kept, d_kept)]
-            d_kept = [
-                ((d - a * head_sums(d, 1)) * scale).astype(jnp.bfloat16)
-                for a, d in zip(kept, d_kept)
-            ]
-            d_turned = [a * d for a, d in zip(turned, d_turned)]
-            d_turned = [
-                ((d - a * head_sums(d, 0)) * scale).astype(jnp.bfloat16)
-                for a, d in zip(turned, d_turned)
-            ]
-            d_q = [product(d, k) for d, (q, k, v) in zip(d_kept, held)]
-            d_k = [product(d, q) for d, (q, k, v) in zip(d_turned, held)]
-            d_v = [product(a.astype(jnp.bfloat16), d) for a, d in zip(turned, outs)]
-            for pair, dq, dk, dv in zip(pairs, d_q, d_k, d_v):
-                at = pair * 128
-                packed[rows, at : at + 128] = dq.astype(jnp.bfloat16)
-                packed[rows, 1024 + at : 1024 + at + 128] = join_heads(dk, low).astype(jnp.bfloat16)
-                packed[rows, 2048 + at : 2048 + at + 128] = join_heads(dv, low).astype(jnp.bfloat16)
-        return carry
-
-    lax.fori_loop(0, 4, unmix, 0)
-
-    core_sends = {}
+        pairs = (2 * cb, 2 * cb + 1)
+        held = [parts_of(rows, pair) for pair in pairs]
+        outs = [mixed[rows, lanes_of(pair)] for pair in pairs]
+        kept = [weights[pair, rows, :].astype(jnp.float32) for pair in pairs]
+        turned = [rows_dot(k, q) for q, k, v in held]
+        d_kept = [rows_dot(d, v) for d, (q, k, v) in zip(outs, held)]
+        d_turned = [rows_dot(v, d) for d, (q, k, v) in zip(outs, held)]
+        turned = [jnp.exp(jnp.where(allowed, s * scale, -1e30)) for s in turned]
+        turned = [s / head_sums(s, 0) for s in turned]
+        d_kept = [a * d for a, d in zip(kept, d_kept)]
+        d_kept = [
+            ((d - a * head_sums(d, 1)) * scale).astype(jnp.bfloat16)
+            for a, d in zip(kept, d_kept)
+        ]
+        d_turned = [a * d for a, d in zip(turned, d_turned)]
+        d_turned = [
+            ((d - a * head_sums(d, 0)) * scale).astype(jnp.bfloat16)
+            for a, d in zip(turned, d_turned)
+        ]
+        d_q = [product(d, k) for d, (q, k, v) in zip(d_kept, held)]
+        d_k = [product(d, q) for d, (q, k, v) in zip(d_turned, held)]
+        d_v = [product(a.astype(jnp.bfloat16), d) for a, d in zip(turned, outs)]
+        for pair, dq, dk, dv in zip(pairs, d_q, d_k, d_v):
+            packed[rows, lanes_of(pair)] = dq.astype(jnp.bfloat16)
+            packed[rows, lanes_of(pair, 1)] = join_heads(dk, low).astype(jnp.bfloat16)
+            packed[rows, lanes_of(pair, 2)] = join_heads(dv, low).astype(jnp.bfloat16)
+        return carry
+
+    swap_packed = {}
+
+    def columns_of(cb):
+        return [pl.ds(which * 1024 + cb * 256, 256) for which in range(3)]
+
+    def unmix_block(cb):
+        lax.fori_loop(0, 4, functools.partial(unmix, cb), 0)
+        swap_packed[cb] = [
+            send(packed.at[:, columns], packed_other.at[:, columns], other_core)
+            for columns in columns_of(cb)
+        ]
+
     far = {}
     near = {}
 
@@ -777,29 +790,28 @@
         return core_sum.at[cb, q] if cb < 2 else core_sum.at[cb, :, q]
 
     def first_phase(cb):
-        core_sends[cb].wait_recv()
-        core_sum[cb] = (
-            core_sum[cb].astype(jnp.float32) + g_parts[core, cb].astype(jnp.float32)
-        ).astype(jnp.bfloat16)
         p, at = axis_of(cb)
         s = sign_of(cb)
         far[cb] = send(chunk(cb, step_of(p, 2)), first_in.at[cb, 0], at(s))
         near[cb] = send(chunk(cb, step_of(p, -s)), first_in.at[cb, 1], at(-s))
 
     def multiply(cb):
-        def block(xi, carry):
-            rows = pl.ds(pl.multiple_of(xi * 256, 256), 256)
-            term = product(ynorm_t[rows, :], packed[:, cb * CB : (cb + 1) * CB])
+        for one in swap_packed[cb]:
+            one.wait_recv()
+        for side in range(2):
+            own = ynorm_t[core, side * 4 : side * 4 + 4].reshape(256, 512)
+            term = product(own, jnp.concatenate([packed[:, c] for c in columns_of(cb)], axis=1))
+            term += product(
+                turned_other[side * 4 : side * 4 + 4].reshape(256, 512),
+                jnp.concatenate([packed_other[:, c] for c in columns_of(cb)], axis=1),
+            )
             term = term.astype(jnp.bfloat16)
-            for ylo in range(2):
-                for c in range(2):
+            for xi in range(2):
+                for ylo in range(2):
                     for yhi in range(2):
-                        at = ylo * 128 + c * 64 + yhi * 32
-                        g_parts[c, cb, xi, yhi * 2 + ylo] = term[at : at + 32]
-            return carry
-
-        lax.fori_loop(0, 4, block, 0)
-        core_sends[cb] = send(g_parts.at[1 - core, cb], core_sum.at[cb], other_core)
+                        at = xi * 128 + ylo * 64 + yhi * 32
+                        core_sum[cb, side * 2 + xi, yhi * 2 + ylo] = term[at : at + 32]
+        first_phase(cb)
 
     second = {}
     last = {}
@@ -829,16 +841,19 @@
             for by in (1, 2, 3)
         ]
 
+    unmix_block(0)
+    unmix_block(2)
+    swap_turned.wait_recv()
     multiply(0)
+    unmix_block(1)
     multiply(2)
-    first_phase(0)
+    unmix_block(3)
     multiply(1)
-    first_phase(2)
+    mixed[:, :512] = rows_dot(packed[...], wqkv[:512, :]).astype(jnp.bfloat16)
     multiply(3)
-    first_phase(1)
-    mixed[:, :512] = rows_dot(packed[...], wqkv[:512, :]).astype(jnp.bfloat16)
-    first_phase(3)
     mixed[:, 512:] = rows_dot(packed[...], wqkv[512:, :]).astype(jnp.bfloat16)
+    second_phase(0)
+    second_phase(2)
 
     def units_block(n, carry):
         rows = pl.ds(pl.multiple_of(n * 128, 128), 128)
@@ -855,15 +870,12 @@
     lax.fori_loop(0, 4, units_block, 0)
     units_right = send(d_units.at[z], d_units.at[z], z_at(1))
     units_left = send(d_units.at[z], d_units.at[z], z_at(-1))
-    for cb in (0, 2, 1, 3):
-        second_phase(cb)
     units_right.wait_recv()
     units_on_right = send(d_units.at[before, top_rows], d_units.at[before, top_rows], z_at(1))
     units_left.wait_recv()
     units_on_left = send(d_units.at[beyond, end_rows], d_units.at[beyond, end_rows], z_at(-1))
-    other_axis(0)
-    other_axis(2)
-    other_axis(1)
+    second_phase(1)
+    second_phase(3)
     units_on_right.wait_recv()
     units_on_left.wait_recv()
     load_win.wait()
@@ -875,7 +887,8 @@
         return carry
 
     lax.fori_loop(0, 4, normed_block, 0)
-    other_axis(3)
+    for cb in (0, 2, 1, 3):
+        other_axis(cb)
     lax.fori_loop(4, 8, normed_block, 0)
 
     wide_on_right.wait_recv()
@@ -898,21 +911,6 @@
         return carry
 
     lax.fori_loop(0, 8, hidden_block, 0)
-    for one in load_wout:
-        one.wait()
-    yhi = y // 2
-
-    def attn_of(up):
-        total = jnp.zeros((256, 256), jnp.float32)
-        for part in range(2):
-            rows = pl.ds(pl.multiple_of((up * 2 + part) * 256, 256), 256)
-            total += rows_dot(
-                wide[:, :, part * 2048 : (part + 1) * 2048].reshape(256, 2048), whead[rows, :]
-            )
-        return total.astype(jnp.bfloat16)
-
-    d_other[0] = attn_of(1 - yhi)
-    to_other = send(d_other.at[0], d_other.at[1], y_at(2))
     for pair in range(2):
         totals = []
         for cb in (2 * pair, 2 * pair + 1):
@@ -929,6 +927,21 @@
     third = [
         send(third_out.at[step_of(z, by)], third_in.at[by - 1], z_at(by)) for by in (1, 2, 3)
     ]
+    for one in load_wout:
+        one.wait()
+    yhi = y // 2
+
+    def attn_of(up):
+        total = jnp.zeros((256, 256), jnp.float32)
+        for part in range(2):
+            rows = pl.ds(pl.multiple_of((up * 2 + part) * 256, 256), 256)
+            total += rows_dot(
+                wide[:, :, part * 2048 : (part + 1) * 2048].reshape(256, 2048), whead[rows, :]
+            )
+        return total.astype(jnp.bfloat16)
+
+    d_other[0] = attn_of(1 - yhi)
+    to_other = send(d_other.at[0], d_other.at[1], y_at(2))
     d_attn_ref[pl.ds(pl.multiple_of(yhi * 256, 256), 256), :] = attn_of(yhi)
 
     to_other.wait_recv()
@@ -939,8 +952,12 @@
         total = third_out[z, pair].astype(jnp.float32)
         for by in (1, 2, 3):
             total += third_in[by - 1, pair].astype(jnp.float32)
-        d_wqkv_ref[:, pair * 2 * CB : (pair * 2 + 1) * CB] = total[:8]
-        d_wqkv_ref[:, (pair * 2 + 1) * CB : (pair * 2 + 2) * CB] = total[8:]
+        for i in range(2):
+            for which in range(3):
+                at = which * 1024 + (pair * 2 + i) * 256
+                d_wqkv_ref[:, at : at + 256] = total[
+                    i * 8 : i * 8 + 8, which * 256 : which * 256 + 256
+                ]
 
     for copy in sends:
         if not any(copy is one for one in wide_sends):
@@ -966,7 +983,7 @@
             pltpu.VMEM((D, 1024), bf16),
             pltpu.VMEM((4, 64, D), bf16),
             pltpu.VMEM((512, 1024), bf16),
-            pltpu.VMEM((1024, 512), bf16),
+            pltpu.VMEM((2, 8, 64, 512), bf16),
             pltpu.VMEM((512, 1024), f32),
             pltpu.VMEM((512, 3072), bf16),
             pltpu.VMEM((8, 512, 256), bf16),
@@ -977,7 +994,8 @@
             pltpu.VMEM((4, 64, 1024), bf16),
             pltpu.VMEM((256, D), bf16),
             pltpu.VMEM((2, 256, 256), bf16),
-            pltpu.VMEM((2, 4, 4, 4, 32, CB), bf16),
+            pltpu.VMEM((8, 64, 512), bf16),
+            pltpu.VMEM((512, 3072), bf16),
             pltpu.VMEM((4, 4, 4, 32, CB), bf16),
             pltpu.VMEM((4, 3, 4, 32, CB), bf16),
             pltpu.VMEM((4, 4, 32, CB), bf16),
@@ -987,8 +1005,8 @@
             pltpu.VMEM((512, 128), f32),
             pltpu.VMEM((512, 1), jnp.int32),
             pltpu.SemaphoreType.DMA((24,)),
-            pltpu.SemaphoreType.DMA((48,)),
-            pltpu.SemaphoreType.DMA((48,)),
+            pltpu.SemaphoreType.DMA((64,)),
+            pltpu.SemaphoreType.DMA((64,)),
         ],
         compiler_params=pltpu.CompilerParams(
             collective_id=1, has_side_effects=True, vmem_limit_bytes=62 * 1024 * 1024

time: 140 us -> 142 us (1.014)
    pallas_call x1, Pallas kernels: 66 us -> 67.8 us  [back(): pl.pallas_call(back_kernel, out_shape=(jax.ShapeDtypeStruct((512, 256), b...]
where the time goes in v6:
time: 142 us
  Pallas kernels  141 us (99%)
    pallas_call x1, Pallas kernels, front(): pl.pallas_call(front_kernel, out_shape=tuple((jax.ShapeDtypeStruct(*one)...  71.9 us
    pallas_call x1, Pallas kernels, back(): pl.pallas_call(back_kernel, out_shape=(jax.ShapeDtypeStruct((512, 256), b...  67.8 us

profile of v6, /device:TPU:0, one launch (start us, length us, event | category | flops | bytes accessed | tf_op | source)
XLA Modules:
  0.0 142.1 jit_solution(4866522093354435362)
XLA Ops:
  0.6 71.9 %shard_map.140 = (bf16[64,1024]{1,0:T(8,128)(2,1)}, bf16[512,1024]{1,0:T(8,128)(2,1)}, bf16[64,4096]{1,0:T(8,128)(2,1)}, bf16[8,2,256,1024]{3,2,1,0:T(8,128)(2,1)}, bf16[2,256,4096]{2,1,0:T(8,128)(2,1)}) custom-call(s32[32]{0:T(128)} %block_of.1, bf16[512,256]{1,0:T(8,128)(2,1)} %q_in.1, bf16[512,256]{1,0:T(8,128)(2,1)} %k_in.1, bf16[512,256]{1,0:T(8,128)(2,1)} %v_in.1, ...), custom_call_target="tpu_custom_call" | custom-call | flops 8999999488 | bytes 40000000 | tf_op jit(solution)/shard_map/pallas_call | solution.py:430
  72.5 67.8 %shard_map.141 = (bf16[512,256]{1,0:T(8,128)(2,1)}, f32[8,3072]{1,0:T(8,128)}) custom-call(bf16[64,1024]{1,0:T(8,128)(2,1)} %get-tuple-element.9.units_ref, bf16[512,1024]{1,0:T(8,128)(2,1)} %get-tuple-element.10.earlier_ref, s32[8,64]{1,0:T(8,128)} %bitcast.6, f32[1,4096]{1,0:T(1,128)} %bitcast.4, bf16[64,4096]{1,0:T(8,128)(2,1)} %get-tuple-element.11.hidden_in, ...), custom_call_target="tpu_custom_call" | custom-call | flops 22000001024 | bytes 40000000 | tf_op jit(solution)/shard_map/pallas_call | solution.py:971
  140.3 1.7 %shard_map.142 = (bf16[512,256]{1,0:T(8,128)(2,1)}, f32[8,3072]{1,0:T(8,128)}) custom-call(bf16[512,256]{1,0:T(8,128)(2,1)} %get-tuple-element.14.attn_in, f32[8,3072]{1,0:T(8,128)} %get-tuple-element.15.wqkv_in), custom_call_target="tpu_custom_call" | custom-call | tf_op jit(solution)/shard_map/pallas_call | solution.py:1026

commit v7 on v5

--- a/solution.py
+++ b/solution.py
@@ -182,7 +182,6 @@
     load_win = [
         load(win_in.at[pl.ds(i * 256, 256)], win.at[own, i]) for i in range(2)
     ]
-    stores = []
     load_embed = load(embed_in, embed)
     load_wout = load(wout_in, wout.at[yhi])
     load_resid = load(resid_in, resid)
@@ -247,6 +246,7 @@
         return carry
 
     lax.fori_loop(0, 4, look_up, 0)
+    stores = []
 
     def pass_on(ref, left_arrived, right_arrived, at, before, after, first, second):
         for one in left_arrived:
@@ -291,9 +291,8 @@
         one.wait_recv()
     side_right = send(kv.at[:, x, side_lo, first_half], kv.at[:, x, side_lo, first_half], x_at(1))
     side_left = send(kv.at[:, x, side_lo, second_half], kv.at[:, x, side_lo, second_half], x_at(-1))
-    kv_on = pass_on(
-        kv_of(ylo), kv_right, kv_left, x_at, before_x, after_x, first_half, second_half
-    )
+    for one in kv_right + kv_left:
+        one.wait_recv()
     beside = device_at(x, side, core, z)
     kv_across = [
         send(kv.at[:, xi, ylo, part], kv.at[:, xi, ylo, part], beside)
@@ -303,6 +302,7 @@
         win_of(yhi), [win_right], [win_left], z_at, before_z, after_z, win_first, win_second
     )
     attend(x, side_lo)
+    kv_on = pass_on(kv_of(ylo), [], [], x_at, before_x, after_x, first_half, second_half)
     share(yhi * 4 + before_z)
     share(yhi * 4 + after_z)
     attend(before_x, ylo)
@@ -839,6 +839,8 @@
     mixed[:, :512] = rows_dot(packed[...], wqkv[:512, :]).astype(jnp.bfloat16)
     first_phase(3)
     mixed[:, 512:] = rows_dot(packed[...], wqkv[512:, :]).astype(jnp.bfloat16)
+    second_phase(0)
+    second_phase(2)
 
     def units_block(n, carry):
         rows = pl.ds(pl.multiple_of(n * 128, 128), 128)
@@ -855,8 +857,8 @@
     lax.fori_loop(0, 4, units_block, 0)
     units_right = send(d_units.at[z], d_units.at[z], z_at(1))
     units_left = send(d_units.at[z], d_units.at[z], z_at(-1))
-    for cb in (0, 2, 1, 3):
-        second_phase(cb)
+    second_phase(1)
+    second_phase(3)
     units_right.wait_recv()
     units_on_right = send(d_units.at[before, top_rows], d_units.at[before, top_rows], z_at(1))
     units_left.wait_recv()
@@ -898,21 +900,6 @@
         return carry
 
     lax.fori_loop(0, 8, hidden_block, 0)
-    for one in load_wout:
-        one.wait()
-    yhi = y // 2
-
-    def attn_of(up):
-        total = jnp.zeros((256, 256), jnp.float32)
-        for part in range(2):
-            rows = pl.ds(pl.multiple_of((up * 2 + part) * 256, 256), 256)
-            total += rows_dot(
-                wide[:, :, part * 2048 : (part + 1) * 2048].reshape(256, 2048), whead[rows, :]
-            )
-        return total.astype(jnp.bfloat16)
-
-    d_other[0] = attn_of(1 - yhi)
-    to_other = send(d_other.at[0], d_other.at[1], y_at(2))
     for pair in range(2):
         totals = []
         for cb in (2 * pair, 2 * pair + 1):
@@ -929,6 +916,21 @@
     third = [
         send(third_out.at[step_of(z, by)], third_in.at[by - 1], z_at(by)) for by in (1, 2, 3)
     ]
+    for one in load_wout:
+        one.wait()
+    yhi = y // 2
+
+    def attn_of(up):
+        total = jnp.zeros((256, 256), jnp.float32)
+        for part in range(2):
+            rows = pl.ds(pl.multiple_of((up * 2 + part) * 256, 256), 256)
+            total += rows_dot(
+                wide[:, :, part * 2048 : (part + 1) * 2048].reshape(256, 2048), whead[rows, :]
+            )
+        return total.astype(jnp.bfloat16)
+
+    d_other[0] = attn_of(1 - yhi)
+    to_other = send(d_other.at[0], d_other.at[1], y_at(2))
     d_attn_ref[pl.ds(pl.multiple_of(yhi * 256, 256), 256), :] = attn_of(yhi)
 
     to_other.wait_recv()

time: 140 us -> 141 us (level)
  no operation moved by 1% of the time
where the time goes in v7:
time: 141 us
  Pallas kernels  140 us (99%)
    pallas_call x1, Pallas kernels, front(): pl.pallas_call(front_kernel, out_shape=tuple((jax.ShapeDtypeStruct(*one)...  71.9 us
    pallas_call x1, Pallas kernels, back(): pl.pallas_call(back_kernel, out_shape=(jax.ShapeDtypeStruct((512, 256), b...  66.3 us

profile of v7, /device:TPU:0, one launch (start us, length us, event | category | flops | bytes accessed | tf_op | source)
XLA Modules:
  0.0 140.6 jit_solution(12039611314805310259)
XLA Ops:
  0.6 71.9 %shard_map.140 = (bf16[64,1024]{1,0:T(8,128)(2,1)}, bf16[512,1024]{1,0:T(8,128)(2,1)}, bf16[64,4096]{1,0:T(8,128)(2,1)}, bf16[8,2,256,1024]{3,2,1,0:T(8,128)(2,1)}, bf16[2,256,4096]{2,1,0:T(8,128)(2,1)}) custom-call(s32[32]{0:T(128)} %block_of.1, bf16[512,256]{1,0:T(8,128)(2,1)} %q_in.1, bf16[512,256]{1,0:T(8,128)(2,1)} %k_in.1, bf16[512,256]{1,0:T(8,128)(2,1)} %v_in.1, ...), custom_call_target="tpu_custom_call" | custom-call | flops 8999999488 | bytes 40000000 | tf_op jit(solution)/shard_map/pallas_call | solution.py:429
  72.5 66.3 %shard_map.141 = (bf16[512,256]{1,0:T(8,128)(2,1)}, f32[8,3072]{1,0:T(8,128)}) custom-call(bf16[64,1024]{1,0:T(8,128)(2,1)} %get-tuple-element.9.units_ref, bf16[512,1024]{1,0:T(8,128)(2,1)} %get-tuple-element.10.earlier_ref, s32[8,64]{1,0:T(8,128)} %bitcast.6, f32[1,4096]{1,0:T(1,128)} %bitcast.4, bf16[64,4096]{1,0:T(8,128)(2,1)} %get-tuple-element.11.hidden_in, ...), custom_call_target="tpu_custom_call" | custom-call | flops 22000001024 | bytes 40000000 | tf_op jit(solution)/shard_map/pallas_call | solution.py:956
  138.9 1.7 %shard_map.142 = (bf16[512,256]{1,0:T(8,128)(2,1)}, f32[8,3072]{1,0:T(8,128)}) custom-call(bf16[512,256]{1,0:T(8,128)(2,1)} %get-tuple-element.14.attn_in, f32[8,3072]{1,0:T(8,128)} %get-tuple-element.15.wqkv_in), custom_call_target="tpu_custom_call" | custom-call | tf_op jit(solution)/shard_map/pallas_call | solution.py:1010
